TPU v7x, 128 devices: a whole 4x4x4 slice. The times are simulated.
128 devices in a mesh: blk: 32 (over x, z, y_lo), dp: 4 (over y_hi, core).
Axes of the slice: x: 4, y: 4 (y_hi: 2, y_lo: 2; y = y_hi * 2 + y_lo), z: 4, core: 2. Of those that a mesh axis runs over, the one named last changes fastest.
Arguments:
- embeddings: bfloat16 [32768, 512], P(('dp', 'blk')), may hold values from -16 to 16
- centers: bfloat16 [65536, 512], P(('blk', 'dp')), may hold values from -10 to 10
- labels: int32 [32768], P(('dp', 'blk')), may hold values from 0 to 65535
Outputs:
- loss: float32 [32768], P(('dp', 'blk'))
All inputs are finite; a program needn't handle non-finite values.
Results may differ from a plain program's by a relative error of at most 0.0017.
Values may be sent and summed in bfloat16 or wider, within the bound.
No kernel may reach another device: no remote copies, remote signals or barrier semaphores. Data moves between devices by JAX's collectives and lax.ppermute only.
A program may use at most 128 MiB of HBM per device.

v0:
```python
import math

import jax
import jax.numpy as jnp
from jax import lax
from jax.sharding import Mesh
from jax.sharding import PartitionSpec as P

BLK = ("blk_0", "blk_1", "blk_2")
DP_BLK = ("dp", "blk_0", "blk_1", "blk_2")
BLK_DP = ("blk_0", "blk_1", "blk_2", "dp")


EPSILON = 1e-06
LOGIT_SCALE = 30.0
MARGIN = 0.5


def laid_out(tiles, dim):
    lengths = list(tiles.shape[1:])
    lengths[dim] *= tiles.shape[0]
    return jnp.moveaxis(tiles, 0, dim).reshape(lengths)


def sent_to_all(x, axis):
    length = lax.axis_size(axis)
    return lax.all_to_all(jnp.broadcast_to(x[None], (length, *x.shape)), axis, 0, 0, tiled=True)


def collect(x, axis, dim):
    return laid_out(sent_to_all(x, axis), dim)


def gather_in_order(x, axes, order):
    tiles = x[None]
    for k in order:
        tiles = lax.all_gather(tiles, axes[k], axis=0, tiled=True)
    carried = [lax.axis_size(axes[k]) for k in reversed(order)]
    tiles = tiles.reshape(*carried, *x.shape)
    turned = sorted(range(len(order)), key=lambda place: order[len(order) - 1 - place])
    return tiles.transpose(*turned, *range(len(order), tiles.ndim)).reshape(-1, *x.shape)


def gather_axes(x, axes, order, dim):
    return laid_out(gather_in_order(x, axes, order), dim)


def split_up(x, dim, length):
    before, after = (x.shape[:dim], x.shape[dim + 1 :])
    return jnp.moveaxis(x.reshape(*before, length, -1, *after), dim, 0)


def sum_at_owner(x, axis, dim):
    length = lax.axis_size(axis)
    tiles = lax.all_to_all(split_up(x, dim, length), axis, 0, 0, tiled=True)
    return jnp.sum(tiles, axis=0)


def unit_rows(matrix):
    values = matrix.astype(jnp.float32)
    return (values * lax.rsqrt(jnp.sum(values * values, axis=1, keepdims=True) + EPSILON)).astype(
        jnp.bfloat16
    )


def margin_loss(other_sum, target_cos):
    sine = jnp.sqrt(jnp.maximum(1.0 - target_cos * target_cos, 0.0))
    shifted = target_cos * math.cos(MARGIN) - sine * math.sin(MARGIN)
    return (
        LOGIT_SCALE
        + jnp.log(other_sum + jnp.exp(LOGIT_SCALE * shifted - LOGIT_SCALE))
        - LOGIT_SCALE * shifted
    )


def block_terms(rows, row_labels, centers_block, class_start):
    cosine = jnp.einsum("nd,cd->nc", rows, centers_block, preferred_element_type=jnp.float32)
    columns = class_start + jnp.arange(centers_block.shape[0], dtype=jnp.int32)
    is_target = row_labels[:, None] == columns[None, :]
    other_sum = jnp.sum(
        jnp.where(is_target, 0.0, jnp.exp(LOGIT_SCALE * cosine - LOGIT_SCALE)), axis=1
    )
    target_cos = jnp.sum(jnp.where(is_target, cosine, 0.0), axis=1)
    return (other_sum, target_cos)


def body(embeddings, centers, labels):
    emb_unit = unit_rows(embeddings)
    center_unit = unit_rows(centers)
    shard_classes = center_unit.shape[0]
    group_count = lax.axis_size("dp")
    group_index = lax.axis_index("dp")
    group_rows, group_labels = (collect(emb_unit, "dp", 0), collect(labels, "dp", 0))
    group_total = group_rows.shape[0]
    zeros_sum = jnp.zeros((group_total,), jnp.float32)
    pieces = gather_axes(center_unit, BLK, (2, 0, 1), 0)
    span_rows = math.gcd(math.gcd(pieces.shape[0], shard_classes), 512)

    def one_span(accum, step_index):
        first = step_index * span_rows
        block_rows = lax.dynamic_slice_in_dim(pieces, step_index * span_rows, span_rows, 0)
        class_start = (
            first // shard_classes * group_count + group_index
        ) * shard_classes + first % shard_classes
        other_part, target_part = block_terms(group_rows, group_labels, block_rows, class_start)
        return ((accum[0] + other_part, accum[1] + target_part), None)

    result, ignored = lax.scan(
        one_span, (zeros_sum, zeros_sum), jnp.arange(pieces.shape[0] // span_rows, dtype=jnp.int32)
    )
    other_group, target_group = result
    other_sum, target_cos = (
        sum_at_owner(other_group, "dp", 0),
        sum_at_owner(target_group, "dp", 0),
    )
    return margin_loss(other_sum, target_cos)


def solution(mesh):
    finer = Mesh(mesh.devices.reshape(4, 4, 2, mesh.shape["dp"]), ("blk_0", "blk_1", "blk_2", "dp"))
    placed = (P(DP_BLK, None), P(BLK_DP, None), P(DP_BLK))
    return jax.shard_map(body, mesh=finer, in_specs=placed, out_specs=P(DP_BLK), check_vma=False)
```

profile of v0, /device:TPU:0, one launch (start us, length us, event | category | flops | bytes accessed | tf_op | source)
XLA Modules:
  0.0 432.0 jit_solution(17319401200410657807)
XLA Ops:
  7.8 2.0 fusion.8
  9.8 26.4 %all-gather.9.cloned.1.call-done = bf16[1024,512]{1,0:T(8,128)(2,1)} async-done(((bf16[512,512]{1,0:T(8,128)(2,1)}), bf16[1024,512]{1,0:T(8,128)(2,1)}) %all-gather.9.cloned.1.call-update) | async-done | bytes 1048592 | tf_op jit(solution)/shard_map/all_gather | solution.py:37
  36.3 50.8 %all-gather.5.cloned.1.call-done = bf16[8,512,512]{2,1,0:T(8,128)(2,1)} async-done(((bf16[2,512,512]{2,1,0:T(8,128)(2,1)}), bf16[8,512,512]{2,1,0:T(8,128)(2,1)}) %all-gather.5.cloned.1.call-update) | async-done | bytes 4194320 | tf_op jit(solution)/shard_map/all_gather | solution.py:37
  88.4 4.3 all-to-all-start
  93.0 5.0 %all-to-all-done = s32[4,1,256]{2,1,0:T(1,128)S(1)} async-done(((s32[4,1,256]{2,1,0:T(1,128)}), s32[4,1,256]{2,1,0:T(1,128)S(1)}, u32[]{:S(2)}, u32[]{:S(2)}) %all-to-all-start) | async-done | bytes 4128 | tf_op jit(solution)/shard_map/all_to_all | solution.py:27
  99.1 3.6 all-to-all-start.1
  102.7 140.7 %all-gather.7.cloned.1.call-done = bf16[32,512,512]{2,1,0:T(8,128)(2,1)} async-done(((bf16[8,512,512]{2,1,0:T(8,128)(2,1)}), bf16[32,512,512]{2,1,0:T(8,128)(2,1)}) %all-gather.7.cloned.1.call-update) | async-done | bytes 16777232 | tf_op jit(solution)/shard_map/all_gather | solution.py:37
  243.4 13.7 %copy.7 = bf16[4,4,2,512,512]{4,3,2,1,0:T(8,128)(2,1)} copy(bf16[4,4,2,512,512]{4,3,2,0,1:T(8,128)(2,1)} %bitcast.35) | data formatting | bytes 33554432 | tf_op jit(solution)/shard_map/transpose | solution.py:41
  257.1 150.0 %while.15 = (s32[]{:T(128)}, f32[1024]{0:T(1024)S(1)}, f32[1024]{0:T(1024)}, s32[4,256]{1,0:T(4,128)S(1)}, s32[32]{0:T(128)S(1)}, /*index=5*/s32[]{:T(128)}, bf1...) while((s32[]{:T(128)}, f32[1024]{0:T(1024)S(1)}, ...), condition=%wide.region_5.6_spmd.clone, body=%wide.region_2.5_spmd.clone.sunk | while | flops 540543488 | bytes 1622475 | solution.py:108
  258.4 2.1 fusion.15
  262.5 2.1 fusion.15
  264.6 1.3 select_add_fusion.3
  267.2 2.1 fusion.15
  269.3 1.3 select_add_fusion.3
  271.9 2.1 fusion.15
  274.0 1.3 select_add_fusion.3
  276.6 2.1 fusion.15
  278.7 1.3 select_add_fusion.3
  281.3 2.1 fusion.15
  283.4 1.3 select_add_fusion.3
  286.0 2.1 fusion.15
  288.1 1.3 select_add_fusion.3
  290.7 2.1 fusion.15
  295.4 2.1 fusion.15
  297.5 1.3 select_add_fusion.3
  300.1 2.1 fusion.15
  302.2 1.3 select_add_fusion.3
  304.8 2.1 fusion.15
  306.9 1.3 select_add_fusion.3
  309.5 2.1 fusion.15
  311.7 1.3 select_add_fusion.3
  314.2 2.1 fusion.15
  316.4 1.3 select_add_fusion.3
  319.0 2.1 fusion.15
  321.1 1.3 select_add_fusion.3
  323.7 2.1 fusion.15
  328.4 2.1 fusion.15
  330.5 1.3 select_add_fusion.3
  333.1 2.1 fusion.15
  335.2 1.3 select_add_fusion.3
  337.8 2.1 fusion.15
  339.9 1.3 select_add_fusion.3
  342.5 2.1 fusion.15
  344.6 1.3 select_add_fusion.3
  347.2 2.1 fusion.15
  351.9 2.1 fusion.15
  354.0 1.3 select_add_fusion.3
  356.6 2.1 fusion.15
  358.7 1.3 select_add_fusion.3
  361.3 2.1 fusion.15
  363.4 1.3 select_add_fusion.3
  366.0 2.1 fusion.15
  368.1 1.3 select_add_fusion.3
  370.7 2.1 fusion.15
  375.4 2.1 fusion.15
  380.1 2.1 fusion.15
  384.9 2.1 fusion.15
  389.6 2.1 fusion.15
  394.3 2.1 fusion.15
  399.0 2.1 fusion.15
  403.7 2.1 fusion.15
  407.1 9.4 %all_to_all.32 = f32[4,1,256]{2,1,0:T(1,128)S(1)} all-to-all(f32[4,1,256]{2,1,0:T(1,128)S(1)} %bitcast.38), channel_id=1, replica_groups=mesh['blk_0'=4,'blk_1'=4,'blk_2'=2,'dp'=4] {'dp'}, dimensions={0} | all-to-all | bytes 8192 | tf_op jit(solution)/shard_map/all_to_all | solution.py:55
  416.4 3.2 all-to-all-start.3
  419.7 5.2 %all-to-all-done.3 = f32[4,1,256]{2,1,0:T(1,128)S(1)} async-done(((f32[4,1,256]{2,1,0:T(1,128)}), f32[4,1,256]{2,1,0:T(1,128)S(1)}, u32[]{:S(2)}, u32[]{:S(2)}) %all-to-all-start.3) | async-done | bytes 4128 | tf_op jit(solution)/shard_map/all_to_all | solution.py:55
  (133 shorter events, 38.9 us)
Async XLA Ops:
  6.5 29.7 %all-gather.9.cloned.1.call-start = ((), (), s32[]{:S(2)}) async-start(), calls=%async_computation.6 | async-start | bytes 1572864 | tf_op jit(solution)/shard_map/all_gather | solution.py:37
  9.8 77.4 %all-gather.5.cloned.1.call-start = ((), (), s32[]{:S(2)}) async-start(), calls=%async_computation.4 | async-start | bytes 5242880 | tf_op jit(solution)/shard_map/all_gather | solution.py:37
  36.3 207.1 %all-gather.7.cloned.1.call-start = ((), (), s32[]{:S(2)}) async-start(), calls=%async_computation.5 | async-start | bytes 20971520 | tf_op jit(solution)/shard_map/all_gather | solution.py:37
  87.1 0.7 copy-start.1
  87.1 5.6 %copy-start = (bf16[256,512]{1,0:T(8,128)(2,1)S(1)}, bf16[256,512]{1,0:T(8,128)(2,1)}, u32[]{:S(2)}) copy-start(bf16[256,512]{1,0:T(8,128)(2,1)} %param.5) | copy-start | bytes 786436
  88.4 9.6 %all-to-all-start = ((s32[4,1,256]{2,1,0:T(1,128)}), s32[4,1,256]{2,1,0:T(1,128)S(1)}, u32[]{:S(2)}, u32[]{:S(2)}) async-start(s32[4,1,256]{2,1,0:T(1,128)} %broadcast_in_dim.31), calls=%async_computation | async-start | bytes 8192 | tf_op jit(solution)/shard_map/all_to_all | solution.py:27
  99.1 158.0 %all-to-all-start.1 = ((bf16[4,256,512]{2,1,0:T(8,128)(2,1)}), bf16[4,256,512]{2,1,0:T(8,128)(2,1)S(1)}, u32[]{:S(2)}, u32[]{:S(2)}) async-start(bf16[4,256,512]{2,1,0:T(8,128)(2,1)} %broadcast_in_dim.33), calls=%async_computation.1 | async-start | bytes 2097152 | tf_op jit(solution)/shard_map/all_to_all | solution.py:27
  416.4 8.4 %all-to-all-start.3 = ((f32[4,1,256]{2,1,0:T(1,128)}), f32[4,1,256]{2,1,0:T(1,128)S(1)}, u32[]{:S(2)}, u32[]{:S(2)}) async-start(f32[4,1,256]{2,1,0:T(1,128)} %bitcast.6), calls=%async_computation.3 | async-start | bytes 8192 | tf_op jit(solution)/shard_map/all_to_all | solution.py:55
Sparse Core Ops, SparseCore 0:
  9.9 26.2 all-gather.8
  37.9 49.1 all-gather.4
  88.8 154.4 all-gather.6
where the time goes:
time: 436 us; the launch traced here: 432 us
  waiting for transfers between devices  228 us (52%)
  matrix products  67.3 us (15%)
  other arithmetic  44.4 us (10%)
  local copies, waits for them, and re-layouts  35.7 us (8%)
  loops' own time  22.9 us (5%)
  between operations  13.2 us (3%)
  starting transfers between devices  11.1 us (3%)
  blocking collectives  9.37 us (2%)
    all_gather x3, waiting for transfers between devices, gather_in_order(): tiles = lax.all_gather(tiles, axes[k], axis=0, tiled=True)  218 us
    dot_general x32, matrix products, block_terms(): jnp.einsum('nd,cd->nc', rows, centers_block, preferred_element_type=jnp.f...  67.3 us
    add x32, other arithmetic, one_span(): return ((accum[0] + other_part, accum[1] + target_part), None)  40.1 us
    another operation x1, loops' own time, body(): lax.scan(one_span, (zeros_sum, zeros_sum), jnp.arange(pieces.shape[0] //...  22.9 us
    dynamic_slice x32, local copies, waits for them, and re-layouts, body(): lax.scan(one_span, (zeros_sum, zeros_sum), jnp.arange(pieces.shape[0] //...  19.5 us
    transpose x1, local copies, waits for them, and re-layouts, gather_in_order(): tiles.transpose(*turned, *range(len(order), tiles.ndim))  13.7 us
    all_to_all x1, blocking collectives, sum_at_owner(): tiles = lax.all_to_all(split_up(x, dim, length), axis, 0, 0, tiled=True)  9.37 us
  transfers between devices with their start and end apart: 6, of which 5 were waited for; matrix products, arithmetic and copies ran while one was open for 4% of the time, Pallas kernels for 0%

commit v1 on v0

v1 whole, which is shorter than its diff:
```python
import functools
import math

import jax
import jax.numpy as jnp
from jax import lax
from jax.experimental import pallas as pl
from jax.experimental.pallas import tpu as pltpu
from jax.sharding import Mesh
from jax.sharding import PartitionSpec as P

AXES = ("x", "z", "yl", "yh", "c")
GROUP = ("x", "yl", "yh")
X, Y, Z, CORE = ("x",), ("yl", "yh"), ("z",), ("c",)
EPSILON = 1e-06
LOGIT_SCALE = 30.0
MARGIN = 0.5
SCALE2 = LOGIT_SCALE / math.log(2.0)
TILE = 512
NT = (((1,), (1,)), ((), ()))
MIB = 1024 * 1024


def unit_block(ref):
    values = ref[...].astype(jnp.float32)
    total = jnp.sum(values * values, axis=1, keepdims=True)
    return (values * lax.rsqrt(total + EPSILON)).astype(jnp.bfloat16)


def unit_kernel(e_ref, c_ref, a_ref, b_ref, u_ref):
    half = a_ref.shape[0]
    u_ref[...] = unit_block(c_ref)
    e = unit_block(e_ref)
    a_ref[...] = e[:half]
    b_ref[...] = e[half:]


def normalized(embeddings, centers):
    half = (embeddings.shape[0] // 2, embeddings.shape[1])
    shapes = [half, half, centers.shape]
    return pl.pallas_call(
        unit_kernel,
        out_shape=[jax.ShapeDtypeStruct(s, jnp.bfloat16) for s in shapes],
    )(embeddings, centers)


def add_terms(x_ref, first, rel, s, t):
    for j in range(TILE // 8):
        x = x_ref[first + 8 * j : first + 8 * j + 8, :]
        at_label = rel == 8 * j
        s = s + jnp.where(at_label, 0.0, jnp.exp2(x * SCALE2))
        t = jnp.where(at_label, x, t)
    return s, t


def terms_kernel(
    n_a, n_e, n_c, plan, owner_ref, base_ref, lab_ref, acc_ref, *refs
):
    e_refs, c_refs = refs[:n_e], refs[n_e : n_e + n_c]
    out_ref, e_buf, c_buf, even, odd, sems = refs[n_e + n_c :]
    copies = [
        pltpu.make_async_copy(ref, e_buf.at[pl.ds(i * TILE, TILE)], sems.at[i])
        for i, ref in enumerate(e_refs)
    ] + [
        pltpu.make_async_copy(ref, c_buf.at[pl.ds(i * TILE, TILE)], sems.at[n_e + i])
        for i, ref in enumerate(c_refs)
    ]
    for copy in copies:
        copy.start()
    if acc_ref is None:
        out_ref[...] = jnp.zeros_like(out_ref)
    else:
        out_ref[...] = acc_ref[...]
    for copy in copies:
        copy.wait()
    sub = lax.broadcasted_iota(jnp.int32, (8, TILE), 0)

    def product(r, k):
        rows = e_buf[pl.ds(pl.multiple_of(r * TILE, TILE), TILE), :]
        block = c_buf[pl.ds(pl.multiple_of(k * 2 * TILE, 2 * TILE), 2 * TILE), :]
        return lax.dot_general(block, rows, NT, preferred_element_type=jnp.float32)

    for e_lo, e_hi, k_lo, k_hi in plan:

        def one_tile(r, _, e_hi=e_hi, k_lo=k_lo, k_hi=k_hi):
            lanes = pl.ds(pl.multiple_of((r >= n_a).astype(jnp.int32) * 128, 128), 128)
            owners = [owner_ref[r * 4 + i] for i in range(4)]
            lab = jnp.concatenate([lab_ref[owners[i], :, lanes] for i in range(4)], axis=1)
            lab = lab - sub

            def add(x_ref, k, s, t):
                s, t = add_terms(x_ref, 0, lab - base_ref[2 * k], s, t)
                return add_terms(x_ref, TILE, lab - base_ref[2 * k + 1], s, t)

            def step(i, carry):
                s, t = carry
                k = k_lo + 2 * i
                odd[...] = product(r, k + 1)
                s, t = add(even, k, s, t)
                last = k + 2 >= k_hi
                even[...] = product(
                    jnp.where(last, jnp.minimum(r + 1, e_hi - 1), r),
                    jnp.where(last, k_lo, k + 2),
                )
                return add(odd, k + 1, s, t)

            zeros = jnp.zeros((8, TILE), jnp.float32)
            n = k_hi - k_lo
            if n == 1:
                s, t = add(even, k_lo, zeros, zeros)
                even[...] = product(jnp.minimum(r + 1, e_hi - 1), k_lo)
            else:
                s, t = lax.fori_loop(0, n // 2, step, (zeros, zeros))
            s = jnp.sum(s, axis=0, keepdims=True)
            t = jnp.sum(t, axis=0, keepdims=True)
            for i in range(4):
                part = slice(128 * i, 128 * i + 128)
                out_ref[owners[i], 0:1, lanes] += s[:, part]
                out_ref[owners[i], 1:2, lanes] += t[:, part]
            return 0

        even[...] = product(e_lo, k_lo)
        lax.fori_loop(e_lo, e_hi, one_tile, 0)


def terms(acc, pieces_a, pieces_b, classes, plan, labels):
    rows = [p for p, _ in pieces_a + pieces_b]
    owners = jnp.stack([o for _, own in pieces_a + pieces_b for o in own])
    bases = jnp.stack([b for _, b in classes])
    n_e, n_c = len(rows), len(classes)
    kernel = functools.partial(terms_kernel, len(pieces_a), n_e, n_c, plan)
    first = acc is None
    if first:
        kernel = functools.partial(lambda k, o, b, l, *refs: k(o, b, l, None, *refs), kernel)
    smem = pl.BlockSpec(memory_space=pltpu.SMEM)
    vmem = pl.BlockSpec(memory_space=pltpu.VMEM)
    blocks = sum((e1 - e0) * (k1 - k0) * 2 for e0, e1, k0, k1 in plan)
    return pl.pallas_call(
        kernel,
        out_shape=jax.ShapeDtypeStruct((16, 2, 256), jnp.float32),
        in_specs=[smem, smem, vmem]
        + [vmem] * (not first)
        + [pl.BlockSpec(memory_space=pl.ANY)] * (n_e + n_c),
        out_specs=vmem,
        scratch_shapes=[
            pltpu.VMEM((n_e * TILE, 512), jnp.bfloat16),
            pltpu.VMEM((n_c * TILE, 512), jnp.bfloat16),
            pltpu.VMEM((2 * TILE, TILE), jnp.float32),
            pltpu.VMEM((2 * TILE, TILE), jnp.float32),
            pltpu.SemaphoreType.DMA((n_e + n_c,)),
        ],
        compiler_params=pltpu.CompilerParams(vmem_limit_bytes=32 * MIB),
        cost_estimate=pl.CostEstimate(
            flops=blocks * 2 * TILE**3,
            bytes_accessed=(n_e + n_c) * TILE * 1024,
            transcendentals=blocks * TILE * TILE,
        ),
    )(owners, bases, labels, *([] if first else [acc]), *rows, *[p for p, _ in classes])


def shift(x, axes, by):
    def place(i):
        return (i % 2) * 2 + i // 2 if axes == Y else i

    n = lax.axis_size(axes)
    return lax.ppermute(x, axes, [(place(i), place((i + by) % n)) for i in range(n)])


def ring(x, axes):
    up, down = shift(x, axes, 1), shift(x, axes, -1)
    return up, down, shift(up, axes, 1)


def body(embeddings, centers, labels):
    a, b, c = normalized(embeddings, centers)
    x, z, c_i = lax.axis_index("x"), lax.axis_index("z"), lax.axis_index("c")
    yl, yh = lax.axis_index("yl"), lax.axis_index("yh")
    y = yh * 2 + yl

    def owner(dx, dy):
        ys = (y - dy) % 4
        return (x - dx) % 4 * 4 + ys % 2 * 2 + ys // 2

    def base(dz, other):
        core = 1 - c_i if other else c_i
        return ((((x * 4 + (z - dz) % 4) * 2 + yl) * 2 + yh) * 2 + core) * 512

    order = (0, 1, -1, 2)
    a_ring = ring(a, Y)
    b_ring = ring(b, X)
    c_ring = ring(c, Z)
    lab = lax.all_to_all(
        jnp.broadcast_to(labels[None, None], (16, 1, 256)), GROUP, 0, 0, tiled=True
    )
    a_all = jnp.concatenate([a, *a_ring])
    b_all = jnp.concatenate([b, *b_ring])
    classes = []
    for dz, piece in zip(order, (c, *c_ring)):
        classes.append((piece, base(dz, False)))
        classes.append((shift(piece, CORE, 1), base(dz, True)))
    a_rings = [(p, [owner(dx, dy) for dy in order]) for dx, p in zip(order, (a_all, *ring(a_all, X)))]
    b_rings = [(p, [owner(dx, dy) for dx in order]) for dy, p in zip(order, (b_all, *ring(b_all, Y)))]
    acc = terms(None, a_rings[:1], b_rings[:1], classes, ((0, 2, 0, 4),), lab)
    acc = terms(acc, a_rings[1:3], b_rings[1:3], classes, ((0, 4, 0, 4),), lab)
    acc = terms(acc, a_rings[3:], b_rings[3:], classes, ((0, 2, 0, 4),), lab)
    parts = lax.all_to_all(acc, GROUP, 0, 0, tiled=True)
    sums = jnp.sum(parts, axis=0)
    return margin_loss(sums[0], sums[1])


def margin_loss(other_sum, target_cos):
    sine = jnp.sqrt(jnp.maximum(1.0 - target_cos * target_cos, 0.0))
    shifted = target_cos * math.cos(MARGIN) - sine * math.sin(MARGIN)
    return jnp.log(other_sum + jnp.exp(LOGIT_SCALE * shifted)) - LOGIT_SCALE * shifted


def solution(mesh):
    finer = Mesh(mesh.devices.reshape(4, 4, 2, 2, 2), AXES)
    rows = ("yh", "c", "x", "z", "yl")
    placed = (P(rows, None), P(AXES, None), P(rows))
    return jax.shard_map(body, mesh=finer, in_specs=placed, out_specs=P(rows), check_vma=False)
```

time: 436 us -> 99.9 us (0.23)
  waiting for transfers between devices: 228 us -> 20.3 us
  matrix products: 67.3 us -> 0 us
  other arithmetic: 44.4 us -> 0.63 us
  Pallas kernels: 0 us -> 36.3 us
  local copies, waits for them, and re-layouts: 35.7 us -> 2.82 us
  loops' own time: 22.9 us -> 0 us
  starting transfers between devices: 11.1 us -> 27.1 us
  between operations: 13.2 us -> 0.58 us
    all_gather x3 -> x0, waiting for transfers between devices: 218 us -> none  [gather_in_order(): tiles = lax.all_gather(tiles, axes[k], axis=0, tiled=True)]
    dot_general x32 -> x0, matrix products: 67.3 us -> none  [block_terms(): jnp.einsum('nd,cd->nc', rows, centers_block, preferred_element_type=jnp.f...]
    add x64 -> x0, other arithmetic: 40.2 us -> none  [the longest x32 40.1 us: one_span(): return ((accum[0] + other_part, accum[1] + target_part), None)]
    pallas_call x0 -> x4, Pallas kernels: none -> 36.3 us  [the longest x3 34.1 us: terms(): pl.pallas_call(kernel, out_shape=jax.ShapeDtypeStruct((16, 2, 256), jnp.f...]
    ppermute x0 -> x19, starting transfers between devices: none -> 23.6 us  [shift(): lax.ppermute(x, axes, [(place(i), place((i + by) % n)) for i in range(n)])]
    another operation x1 -> x0, loops' own time: 22.9 us -> none  [body(): lax.scan(one_span, (zeros_sum, zeros_sum), jnp.arange(pieces.shape[0] //...]
    dynamic_slice x32 -> x0, local copies, waits for them, and re-layouts: 19.5 us -> none  [body(): lax.scan(one_span, (zeros_sum, zeros_sum), jnp.arange(pieces.shape[0] //...]
    ppermute x0 -> x19, waiting for transfers between devices: none -> 16.3 us  [shift(): lax.ppermute(x, axes, [(place(i), place((i + by) % n)) for i in range(n)])]
  transfers between devices with their start and end apart: 6 -> 20, of which waited for: 5 -> 7; matrix products, arithmetic and copies ran while one was open for 4% -> 2% of each run, Pallas kernels for 0% -> 25%
where the time goes in v1:
time: 99.9 us; the launch traced here: 99.6 us
  Pallas kernels  36.3 us (36%)
  starting transfers between devices  27.1 us (27%)
  waiting for transfers between devices  20.3 us (20%)
  blocking collectives  11.8 us (12%)
  local copies, waits for them, and re-layouts  2.82 us (3%)
    pallas_call x3, Pallas kernels, terms(): pl.pallas_call(kernel, out_shape=jax.ShapeDtypeStruct((16, 2, 256), jnp.f...  34.1 us
    ppermute x19, starting transfers between devices, shift(): lax.ppermute(x, axes, [(place(i), place((i + by) % n)) for i in range(n)])  23.6 us
    ppermute x19, waiting for transfers between devices, shift(): lax.ppermute(x, axes, [(place(i), place((i + by) % n)) for i in range(n)])  16.3 us
    all_to_all x1, blocking collectives, body(): parts = lax.all_to_all(acc, GROUP, 0, 0, tiled=True)  11.8 us
    all_to_all x1, waiting for transfers between devices, body(): lax.all_to_all(jnp.broadcast_to(labels[None, None], (16, 1, 256)), GROUP,...  3.96 us
    all_to_all x1, starting transfers between devices, body(): lax.all_to_all(jnp.broadcast_to(labels[None, None], (16, 1, 256)), GROUP,...  3.49 us
    pallas_call x1, Pallas kernels, normalized(): pl.pallas_call(unit_kernel, out_shape=[jax.ShapeDtypeStruct(s, jnp.bfloat...  2.24 us
  transfers between devices with their start and end apart: 20, of which 7 were waited for; matrix products, arithmetic and copies ran while one was open for 2% of the time, Pallas kernels for 25%

profile of v1, /device:TPU:0, one launch (start us, length us, event | category | flops | bytes accessed | tf_op | source)
XLA Modules:
  0.0 99.6 jit_solution(15408057269435377600)
XLA Ops:
  0.0 2.2 %shard_map.37 = (bf16[128,512]{1,0:T(8,128)(2,1)}, bf16[128,512]{1,0:T(8,128)(2,1)}, bf16[512,512]{1,0:T(8,128)(2,1)}) custom-call(bf16[256,512]{1,0:T(8,128)(2,1)} %e_ref.1, bf16[512,512]{1,0:T(8,128)(2,1)} %c_ref.1), custom_call_target="tpu_custom_call" | custom-call | tf_op jit(solution)/shard_map/pallas_call | solution.py:41
  2.2 0.0 copy-start
  2.2 2.0 %collective-permute-start.7 = (bf16[512,512]{1,0:T(8,128)(2,1)}, bf16[512,512]{1,0:T(8,128)(2,1)S(1)}, u32[]{:S(2)}, u32[]{:S(2)}) collective-permute-start(bf16[512,512]{1,0:T(8,128)(2,1)} %get-tuple-element.10.refs_2_.refs_4_), channel_id=1, source_target_pairs={{0,8},{8,16},{16,24},{24,0},{1,9},{9,17},{17,25},{25,1},{2,10},{10... | collective-permute-start | bytes 1572872 | tf_op jit(solution)/shard_map/ppermute | solution.py:166
  4.2 1.6 %collective-permute-start = (bf16[128,512]{1,0:T(8,128)(2,1)}, bf16[128,512]{1,0:T(8,128)(2,1)S(1)}, u32[]{:S(2)}, u32[]{:S(2)}) collective-permute-start(bf16[128,512]{1,0:T(8,128)(2,1)} %get-tuple-element.8), channel_id=1, source_target_pairs={{0,4},{4,2},{2,6},{6,0},{1,5},{5,3},{3,7},{7,1},{8,12},{12,10},{10... | collective-permute-start | bytes 393224 | tf_op jit(solution)/shard_map/ppermute | solution.py:166
  5.8 1.7 %collective-permute-start.1 = (bf16[128,512]{1,0:T(8,128)(2,1)}, bf16[128,512]{1,0:T(8,128)(2,1)S(1)}, u32[]{:S(2)}, u32[]{:S(2)}) collective-permute-start(bf16[128,512]{1,0:T(8,128)(2,1)} %get-tuple-element.8), channel_id=1, source_target_pairs={{0,6},{4,0},{2,4},{6,2},{1,7},{5,1},{3,5},{7,3},{8,14},{12,8},{10,... | collective-permute-start | bytes 393224 | tf_op jit(solution)/shard_map/ppermute | solution.py:166
  7.5 1.5 %collective-permute-start.3 = (bf16[128,512]{1,0:T(8,128)(2,1)}, bf16[128,512]{1,0:T(8,128)(2,1)S(1)}, u32[]{:S(2)}, u32[]{:S(2)}) collective-permute-start(bf16[128,512]{1,0:T(8,128)(2,1)} %get-tuple-element.9), channel_id=1, source_target_pairs={{0,32},{32,64},{64,96},{96,0},{1,33},{33,65},{65,97},{97,1},{2,34}... | collective-permute-start | bytes 393224 | tf_op jit(solution)/shard_map/ppermute | solution.py:166
  9.0 1.7 %collective-permute-start.4 = (bf16[128,512]{1,0:T(8,128)(2,1)}, bf16[128,512]{1,0:T(8,128)(2,1)S(1)}, u32[]{:S(2)}, u32[]{:S(2)}) collective-permute-start(bf16[128,512]{1,0:T(8,128)(2,1)} %get-tuple-element.9), channel_id=1, source_target_pairs={{0,96},{32,0},{64,32},{96,64},{1,97},{33,1},{65,33},{97,65},{2,98}... | collective-permute-start | bytes 393224 | tf_op jit(solution)/shard_map/ppermute | solution.py:166
  10.7 1.0 constant_dynamic-update-slice_fusion.3
  11.7 0.0 collective-permute-done
  11.7 0.0 copy-done
  11.7 0.1 collective-permute-start.6
  11.8 0.0 collective-permute-done.1
  11.9 2.3 %collective-permute-start.9 = (bf16[512,512]{1,0:T(8,128)(2,1)S(1)}, bf16[512,512]{1,0:T(8,128)(2,1)S(1)}, u32[]{:S(2)}, u32[]{:S(2)}) collective-permute-start(bf16[512,512]{1,0:T(8,128)(2,1)S(1)} %copy-done), channel_id=1, source_target_pairs={{0,24},{8,0},{16,8},{24,16},{1,25},{9,1},{17,9},{25,17},{2,26},{10... | collective-permute-start | bytes 1572872 | tf_op jit(solution)/shard_map/ppermute | solution.py:166
  14.1 0.0 collective-permute-done.3
  14.1 0.7 collective-permute-start.2
  14.9 3.7 %collective-permute-done.7.refs_4_.refs_6_ = bf16[512,512]{1,0:T(8,128)(2,1)S(1)} collective-permute-done((bf16[512,512]{1,0:T(8,128)(2,1)}, bf16[512,512]{1,0:T(8,128)(2,1)S(1)}, u32[]{:S(2)}, u32[]{:S(2)}) %collective-permute-start.7) | collective-permute-done | bytes 524320 | tf_op jit(solution)/shard_map/ppermute | solution.py:166
  18.6 0.0 collective-permute-start.11
  18.6 0.0 collective-permute-done.4
  18.6 1.6 %collective-permute-start.5 = (bf16[128,512]{1,0:T(8,128)(2,1)S(1)}, bf16[128,512]{1,0:T(8,128)(2,1)S(1)}, u32[]{:S(2)}, u32[]{:S(2)}) collective-permute-start(bf16[128,512]{1,0:T(8,128)(2,1)S(1)} %collective-permute-done.3), channel_id=1, source_target_pairs={{0,32},{32,64},{64,96},{96,0},{1,33},{33,65},{65,97},{97,1},{2,34}... | collective-permute-start | bytes 393224 | tf_op jit(solution)/shard_map/ppermute | solution.py:166
  20.2 0.9 collective-permute-done.2
  21.0 0.0 copy-start.5
  21.1 0.7 collective-permute-start.13
  21.8 3.6 %collective-permute-done.5 = bf16[128,512]{1,0:T(8,128)(2,1)S(1)} collective-permute-done((bf16[128,512]{1,0:T(8,128)(2,1)S(1)}, bf16[128,512]{1,0:T(8,128)(2,1)S(1)}, u32[]{:S(2)}, u32[]{:S(2)}) %collective-permute-start.5) | collective-permute-done | bytes 131104 | tf_op jit(solution)/shard_map/ppermute | solution.py:166
  25.4 2.6 %collective-permute-start.15 = (bf16[512,512]{1,0:T(8,128)(2,1)S(1)}, bf16[512,512]{1,0:T(8,128)(2,1)S(1)}, u32[]{:S(2)}, u32[]{:S(2)}) collective-permute-start(bf16[512,512]{1,0:T(8,128)(2,1)S(1)} %constant_dynamic-update-slice_fusion.4.refs_1_), channel_id=1, source_target_pairs={{0,4},{4,2},{2,6},{6,0},{1,5},{5,3},{3,7},{7,1},{8,12},{12,10},{10... | collective-permute-start | bytes 1572872 | tf_op jit(solution)/shard_map/ppermute | solution.py:166
  28.0 0.0 collective-permute-done.6.refs_3_.refs_5_
  28.0 0.0 collective-permute-start.8
  28.0 0.0 collective-permute-done.9.refs_6_.refs_8_
  28.0 0.5 collective-permute-start.10
  28.5 4.5 %collective-permute-done.11.refs_8_.refs_10_ = bf16[512,512]{1,0:T(8,128)(2,1)} collective-permute-done((bf16[512,512]{1,0:T(8,128)(2,1)S(1)}, bf16[512,512]{1,0:T(8,128)(2,1)}, u32[]{:S(2)}, u32[]{:S(2)}) %collective-permute-start.11) | collective-permute-done | bytes 524320 | tf_op jit(solution)/shard_map/ppermute | solution.py:166
  33.0 0.0 collective-permute-start.12
  33.0 3.1 %collective-permute-done.13.refs_0_ = bf16[512,512]{1,0:T(8,128)(2,1)S(1)} collective-permute-done((bf16[512,512]{1,0:T(8,128)(2,1)S(1)}, bf16[512,512]{1,0:T(8,128)(2,1)S(1)}, u32[]{:S(2)}, u32[]{:S(2)}) %collective-permute-start.13) | collective-permute-done | bytes 524320 | tf_op jit(solution)/shard_map/ppermute | solution.py:166
  36.1 0.0 copy-start.1
  36.1 1.5 %collective-permute-start.14 = (bf16[512,512]{1,0:T(8,128)(2,1)S(1)}, bf16[512,512]{1,0:T(8,128)(2,1)}, u32[]{:S(2)}, u32[]{:S(2)}) collective-permute-start(bf16[512,512]{1,0:T(8,128)(2,1)S(1)} %constant_dynamic-update-slice_fusion.refs_0_), channel_id=1, source_target_pairs={{0,96},{32,0},{64,32},{96,64},{1,97},{33,1},{65,33},{97,65},{2,98}... | collective-permute-start | bytes 1572872 | tf_op jit(solution)/shard_map/ppermute | solution.py:166
  37.6 0.5 collective-permute-done.15.refs_2_
  38.2 0.0 copy-done.1
  38.2 0.0 copy-start.3
  38.2 0.8 copy-done.3
  39.0 2.2 %collective-permute-start.16 = (bf16[512,512]{1,0:T(8,128)(2,1)S(1)}, bf16[512,512]{1,0:T(8,128)(2,1)}, u32[]{:S(2)}, u32[]{:S(2)}) collective-permute-start(bf16[512,512]{1,0:T(8,128)(2,1)S(1)} %constant_dynamic-update-slice_fusion.4.refs_1_), channel_id=1, source_target_pairs={{0,6},{4,0},{2,4},{6,2},{1,7},{5,1},{3,5},{7,3},{8,14},{12,8},{10,... | collective-permute-start | bytes 1572872 | tf_op jit(solution)/shard_map/ppermute | solution.py:166
  41.2 0.0 copy-done.5
  41.2 0.6 broadcast_in_dim.2
  41.8 3.5 %all-to-all-start = ((s32[16,1,256]{2,1,0:T(1,128)}), s32[16,1,256]{2,1,0:T(1,128)S(1)}, u32[]{:S(2)}, u32[]{:S(2)}) async-start(s32[16,1,256]{2,1,0:T(1,128)} %broadcast_in_dim.2), calls=%async_computation | async-start | bytes 32768 | tf_op jit(solution)/shard_map/all_to_all | solution.py:192
  45.6 0.1 stack.125.owner_ref
  45.7 0.1 stack.145.o
  45.8 0.1 stack.143.owner_ref
  45.9 0.1 stack.134.b.base_ref
  46.0 0.0 collective-permute-done.8.refs_5_.refs_7_
  46.0 1.5 %collective-permute-start.17 = (bf16[512,512]{1,0:T(8,128)(2,1)}, bf16[512,512]{1,0:T(8,128)(2,1)}, u32[]{:S(2)}, u32[]{:S(2)}) collective-permute-start(bf16[512,512]{1,0:T(8,128)(2,1)} %copy-done.1), channel_id=1, source_target_pairs={{0,32},{32,64},{64,96},{96,0},{1,33},{33,65},{65,97},{97,1},{2,34}... | collective-permute-start | bytes 1572872 | tf_op jit(solution)/shard_map/ppermute | solution.py:166
  47.5 0.0 collective-permute-done.10.refs_7_.refs_9_
  47.5 1.5 %collective-permute-start.18 = (bf16[512,512]{1,0:T(8,128)(2,1)}, bf16[512,512]{1,0:T(8,128)(2,1)}, u32[]{:S(2)}, u32[]{:S(2)}) collective-permute-start(bf16[512,512]{1,0:T(8,128)(2,1)} %copy-done.3), channel_id=1, source_target_pairs={{0,4},{4,2},{2,6},{6,0},{1,5},{5,3},{3,7},{7,1},{8,12},{12,10},{10... | collective-permute-start | bytes 1572872 | tf_op jit(solution)/shard_map/ppermute | solution.py:166
  49.0 4.0 %all-to-all-done.l.lab_ref = s32[16,1,256]{2,1,0:T(1,128)S(1)} async-done(((s32[16,1,256]{2,1,0:T(1,128)}), s32[16,1,256]{2,1,0:T(1,128)S(1)}, u32[]{:S(2)}, u32[]{:S(2)}) %all-to-all-start) | async-done | bytes 16416 | tf_op jit(solution)/shard_map/all_to_all | solution.py:192
  53.0 0.0 copy-start.2
  53.0 0.0 copy-start.4
  53.0 0.0 collective-permute-done.12.refs_9_.refs_11_
  53.0 9.2 %shard_map.38.acc_ref = f32[16,2,256]{2,1,0:T(2,128)S(1)} custom-call(s32[8]{0:T(128)S(1)} %stack.145.o, s32[8]{0:T(128)S(1)} %stack.134.b.base_ref, s32[16,1,256]{2,1,0:T(1,128)S(1)} %all-to-all-done.l.lab_ref, bf16[512,512]{1,0:T(8,128)(2,1)S(1)} %constant_dynamic-update-slice_fusion.refs_0_, ...), custom_call_target="tpu_custom_call" | custom-call | flops 4294967296 | bytes 5242880 | tf_op jit(solution)/shard_map/pallas_call | solution.py:138
  62.2 0.0 collective-permute-done.14.refs_1_
  62.2 0.0 collective-permute-done.16.refs_3_
  62.2 0.0 copy-done.2
  62.2 0.0 copy-done.4
  62.2 15.5 %shard_map.39.acc_ref = f32[16,2,256]{2,1,0:T(2,128)S(1)} custom-call(s32[16]{0:T(128)S(1)} %stack.143.owner_ref, s32[8]{0:T(128)S(1)} %stack.134.b.base_ref, s32[16,1,256]{2,1,0:T(1,128)S(1)} %all-to-all-done.l.lab_ref, f32[16,2,256]{2,1,0:T(2,128)S(1)} %shard_map.38.acc_ref, bf16[512,512]{1,0:T(8,128)(2,1)S(1)} %copy-done.2, ...), custom_call_target="tpu_custom_call" | custom-call | flops 8589934592 | bytes 6291456 | tf_op jit(solution)/shard_map/pallas_call | solution.py:138
  77.7 0.0 collective-permute-done.17.refs_0_
  77.7 0.0 collective-permute-done.18.refs_1_
  77.8 9.4 %shard_map.40 = f32[16,2,256]{2,1,0:T(2,128)S(1)} custom-call(s32[8]{0:T(128)S(1)} %stack.125.owner_ref, s32[8]{0:T(128)S(1)} %stack.134.b.base_ref, s32[16,1,256]{2,1,0:T(1,128)S(1)} %all-to-all-done.l.lab_ref, f32[16,2,256]{2,1,0:T(2,128)S(1)} %shard_map.39.acc_ref, bf16[512,512]{1,0:T(8,128)(2,1)} %collective-permute-done.17.refs_0_, ...), custom_call_target="tpu_custom_call" | custom-call | flops 4294967296 | bytes 5242880 | tf_op jit(solution)/shard_map/pallas_call | solution.py:138
  87.1 11.8 %all_to_all.10 = f32[16,2,256]{2,1,0:T(2,128)S(1)} all-to-all(f32[16,2,256]{2,1,0:T(2,128)S(1)} %shard_map.40), channel_id=1, replica_groups=mesh['x'=4,'z'=4,'yl'=2,'yh'=2,'c'=2] {'x','yl','yh'}, dimensions={0} | all-to-all | bytes 65536 | tf_op jit(solution)/shard_map/all_to_all | solution.py:206
  99.0 0.6 log_subtract_fusion
  (8 shorter events, 0.1 us)
Async XLA Ops:
  2.2 9.5 %copy-start = (bf16[512,512]{1,0:T(8,128)(2,1)S(1)}, bf16[512,512]{1,0:T(8,128)(2,1)}, u32[]{:S(2)}) copy-start(bf16[512,512]{1,0:T(8,128)(2,1)} %get-tuple-element.10.refs_2_.refs_4_) | copy-start | bytes 1572868
  2.2 16.3 %collective-permute-start.7 = (bf16[512,512]{1,0:T(8,128)(2,1)}, bf16[512,512]{1,0:T(8,128)(2,1)S(1)}, u32[]{:S(2)}, u32[]{:S(2)}) collective-permute-start(bf16[512,512]{1,0:T(8,128)(2,1)} %get-tuple-element.10.refs_2_.refs_4_), channel_id=1, source_target_pairs={{0,8},{8,16},{16,24},{24,0},{1,9},{9,17},{17,25},{25,1},{2,10},{10... | collective-permute-start | bytes 1572872 | tf_op jit(solution)/shard_map/ppermute | solution.py:166
  4.2 7.5 %collective-permute-start = (bf16[128,512]{1,0:T(8,128)(2,1)}, bf16[128,512]{1,0:T(8,128)(2,1)S(1)}, u32[]{:S(2)}, u32[]{:S(2)}) collective-permute-start(bf16[128,512]{1,0:T(8,128)(2,1)} %get-tuple-element.8), channel_id=1, source_target_pairs={{0,4},{4,2},{2,6},{6,0},{1,5},{5,3},{3,7},{7,1},{8,12},{12,10},{10... | collective-permute-start | bytes 393224 | tf_op jit(solution)/shard_map/ppermute | solution.py:166
  5.8 6.0 %collective-permute-start.1 = (bf16[128,512]{1,0:T(8,128)(2,1)}, bf16[128,512]{1,0:T(8,128)(2,1)S(1)}, u32[]{:S(2)}, u32[]{:S(2)}) collective-permute-start(bf16[128,512]{1,0:T(8,128)(2,1)} %get-tuple-element.8), channel_id=1, source_target_pairs={{0,6},{4,0},{2,4},{6,2},{1,7},{5,1},{3,5},{7,3},{8,14},{12,8},{10,... | collective-permute-start | bytes 393224 | tf_op jit(solution)/shard_map/ppermute | solution.py:166
  7.5 6.6 %collective-permute-start.3 = (bf16[128,512]{1,0:T(8,128)(2,1)}, bf16[128,512]{1,0:T(8,128)(2,1)S(1)}, u32[]{:S(2)}, u32[]{:S(2)}) collective-permute-start(bf16[128,512]{1,0:T(8,128)(2,1)} %get-tuple-element.9), channel_id=1, source_target_pairs={{0,32},{32,64},{64,96},{96,0},{1,33},{33,65},{65,97},{97,1},{2,34}... | collective-permute-start | bytes 393224 | tf_op jit(solution)/shard_map/ppermute | solution.py:166
  9.0 9.6 %collective-permute-start.4 = (bf16[128,512]{1,0:T(8,128)(2,1)}, bf16[128,512]{1,0:T(8,128)(2,1)S(1)}, u32[]{:S(2)}, u32[]{:S(2)}) collective-permute-start(bf16[128,512]{1,0:T(8,128)(2,1)} %get-tuple-element.9), channel_id=1, source_target_pairs={{0,96},{32,0},{64,32},{96,64},{1,97},{33,1},{65,33},{97,65},{2,98}... | collective-permute-start | bytes 393224 | tf_op jit(solution)/shard_map/ppermute | solution.py:166
  11.7 16.2 %collective-permute-start.6 = (bf16[512,512]{1,0:T(8,128)(2,1)S(1)}, bf16[512,512]{1,0:T(8,128)(2,1)S(1)}, u32[]{:S(2)}, u32[]{:S(2)}) collective-permute-start(bf16[512,512]{1,0:T(8,128)(2,1)S(1)} %copy-done), channel_id=1, source_target_pairs={{0,1},{1,0},{2,3},{3,2},{4,5},{5,4},{6,7},{7,6},{8,9},{9,8},{10,11... | collective-permute-start | bytes 1572872 | tf_op jit(solution)/shard_map/ppermute | solution.py:166
  11.9 16.1 %collective-permute-start.9 = (bf16[512,512]{1,0:T(8,128)(2,1)S(1)}, bf16[512,512]{1,0:T(8,128)(2,1)S(1)}, u32[]{:S(2)}, u32[]{:S(2)}) collective-permute-start(bf16[512,512]{1,0:T(8,128)(2,1)S(1)} %copy-done), channel_id=1, source_target_pairs={{0,24},{8,0},{16,8},{24,16},{1,25},{9,1},{17,9},{25,17},{2,26},{10... | collective-permute-start | bytes 1572872 | tf_op jit(solution)/shard_map/ppermute | solution.py:166
  14.1 6.9 %collective-permute-start.2 = (bf16[128,512]{1,0:T(8,128)(2,1)S(1)}, bf16[128,512]{1,0:T(8,128)(2,1)S(1)}, u32[]{:S(2)}, u32[]{:S(2)}) collective-permute-start(bf16[128,512]{1,0:T(8,128)(2,1)S(1)} %collective-permute-done), channel_id=1, source_target_pairs={{0,4},{4,2},{2,6},{6,0},{1,5},{5,3},{3,7},{7,1},{8,12},{12,10},{10... | collective-permute-start | bytes 393224 | tf_op jit(solution)/shard_map/ppermute | solution.py:166
  18.6 14.4 %collective-permute-start.11 = (bf16[512,512]{1,0:T(8,128)(2,1)S(1)}, bf16[512,512]{1,0:T(8,128)(2,1)}, u32[]{:S(2)}, u32[]{:S(2)}) collective-permute-start(bf16[512,512]{1,0:T(8,128)(2,1)S(1)} %collective-permute-done.7.refs_4_.refs_6_), channel_id=1, source_target_pairs={{0,8},{8,16},{16,24},{24,0},{1,9},{9,17},{17,25},{25,1},{2,10},{10... | collective-permute-start | bytes 1572872 | tf_op jit(solution)/shard_map/ppermute | solution.py:166
  18.6 6.8 %collective-permute-start.5 = (bf16[128,512]{1,0:T(8,128)(2,1)S(1)}, bf16[128,512]{1,0:T(8,128)(2,1)S(1)}, u32[]{:S(2)}, u32[]{:S(2)}) collective-permute-start(bf16[128,512]{1,0:T(8,128)(2,1)S(1)} %collective-permute-done.3), channel_id=1, source_target_pairs={{0,32},{32,64},{64,96},{96,0},{1,33},{33,65},{65,97},{97,1},{2,34}... | collective-permute-start | bytes 393224 | tf_op jit(solution)/shard_map/ppermute | solution.py:166
  21.0 20.1 %copy-start.5 = (s32[256]{0:T(256)S(1)}, s32[256]{0:T(256)}, u32[]{:S(2)}) copy-start(s32[256]{0:T(256)} %param.5) | copy-start | bytes 3076
  21.1 15.0 %collective-permute-start.13 = (bf16[512,512]{1,0:T(8,128)(2,1)S(1)}, bf16[512,512]{1,0:T(8,128)(2,1)S(1)}, u32[]{:S(2)}, u32[]{:S(2)}) collective-permute-start(bf16[512,512]{1,0:T(8,128)(2,1)S(1)} %constant_dynamic-update-slice_fusion.refs_0_), channel_id=1, source_target_pairs={{0,32},{32,64},{64,96},{96,0},{1,33},{33,65},{65,97},{97,1},{2,34}... | collective-permute-start | bytes 1572872 | tf_op jit(solution)/shard_map/ppermute | solution.py:166
  25.4 12.8 %collective-permute-start.15 = (bf16[512,512]{1,0:T(8,128)(2,1)S(1)}, bf16[512,512]{1,0:T(8,128)(2,1)S(1)}, u32[]{:S(2)}, u32[]{:S(2)}) collective-permute-start(bf16[512,512]{1,0:T(8,128)(2,1)S(1)} %constant_dynamic-update-slice_fusion.4.refs_1_), channel_id=1, source_target_pairs={{0,4},{4,2},{2,6},{6,0},{1,5},{5,3},{3,7},{7,1},{8,12},{12,10},{10... | collective-permute-start | bytes 1572872 | tf_op jit(solution)/shard_map/ppermute | solution.py:166
  28.0 18.0 %collective-permute-start.8 = (bf16[512,512]{1,0:T(8,128)(2,1)S(1)}, bf16[512,512]{1,0:T(8,128)(2,1)}, u32[]{:S(2)}, u32[]{:S(2)}) collective-permute-start(bf16[512,512]{1,0:T(8,128)(2,1)S(1)} %collective-permute-done.7.refs_4_.refs_6_), channel_id=1, source_target_pairs={{0,1},{1,0},{2,3},{3,2},{4,5},{5,4},{6,7},{7,6},{8,9},{9,8},{10,11... | collective-permute-start | bytes 1572872 | tf_op jit(solution)/shard_map/ppermute | solution.py:166
  28.0 19.5 %collective-permute-start.10 = (bf16[512,512]{1,0:T(8,128)(2,1)S(1)}, bf16[512,512]{1,0:T(8,128)(2,1)}, u32[]{:S(2)}, u32[]{:S(2)}) collective-permute-start(bf16[512,512]{1,0:T(8,128)(2,1)S(1)} %collective-permute-done.9.refs_6_.refs_8_), channel_id=1, source_target_pairs={{0,1},{1,0},{2,3},{3,2},{4,5},{5,4},{6,7},{7,6},{8,9},{9,8},{10,11... | collective-permute-start | bytes 1572872 | tf_op jit(solution)/shard_map/ppermute | solution.py:166
  33.0 20.0 %collective-permute-start.12 = (bf16[512,512]{1,0:T(8,128)(2,1)}, bf16[512,512]{1,0:T(8,128)(2,1)}, u32[]{:S(2)}, u32[]{:S(2)}) collective-permute-start(bf16[512,512]{1,0:T(8,128)(2,1)} %collective-permute-done.11.refs_8_.refs_10_), channel_id=1, source_target_pairs={{0,1},{1,0},{2,3},{3,2},{4,5},{5,4},{6,7},{7,6},{8,9},{9,8},{10,11... | collective-permute-start | bytes 1572872 | tf_op jit(solution)/shard_map/ppermute | solution.py:166
  36.1 2.1 %copy-start.1 = (bf16[512,512]{1,0:T(8,128)(2,1)}, bf16[512,512]{1,0:T(8,128)(2,1)S(1)}, u32[]{:S(2)}) copy-start(bf16[512,512]{1,0:T(8,128)(2,1)S(1)} %collective-permute-done.13.refs_0_) | copy-start | bytes 1572868
  36.1 26.1 %collective-permute-start.14 = (bf16[512,512]{1,0:T(8,128)(2,1)S(1)}, bf16[512,512]{1,0:T(8,128)(2,1)}, u32[]{:S(2)}, u32[]{:S(2)}) collective-permute-start(bf16[512,512]{1,0:T(8,128)(2,1)S(1)} %constant_dynamic-update-slice_fusion.refs_0_), channel_id=1, source_target_pairs={{0,96},{32,0},{64,32},{96,64},{1,97},{33,1},{65,33},{97,65},{2,98}... | collective-permute-start | bytes 1572872 | tf_op jit(solution)/shard_map/ppermute | solution.py:166
  38.2 0.8 copy-start.3
  39.0 23.2 %collective-permute-start.16 = (bf16[512,512]{1,0:T(8,128)(2,1)S(1)}, bf16[512,512]{1,0:T(8,128)(2,1)}, u32[]{:S(2)}, u32[]{:S(2)}) collective-permute-start(bf16[512,512]{1,0:T(8,128)(2,1)S(1)} %constant_dynamic-update-slice_fusion.4.refs_1_), channel_id=1, source_target_pairs={{0,6},{4,0},{2,4},{6,2},{1,7},{5,1},{3,5},{7,3},{8,14},{12,8},{10,... | collective-permute-start | bytes 1572872 | tf_op jit(solution)/shard_map/ppermute | solution.py:166
  41.8 11.2 %all-to-all-start = ((s32[16,1,256]{2,1,0:T(1,128)}), s32[16,1,256]{2,1,0:T(1,128)S(1)}, u32[]{:S(2)}, u32[]{:S(2)}) async-start(s32[16,1,256]{2,1,0:T(1,128)} %broadcast_in_dim.2), calls=%async_computation | async-start | bytes 32768 | tf_op jit(solution)/shard_map/all_to_all | solution.py:192
  46.0 31.7 %collective-permute-start.17 = (bf16[512,512]{1,0:T(8,128)(2,1)}, bf16[512,512]{1,0:T(8,128)(2,1)}, u32[]{:S(2)}, u32[]{:S(2)}) collective-permute-start(bf16[512,512]{1,0:T(8,128)(2,1)} %copy-done.1), channel_id=1, source_target_pairs={{0,32},{32,64},{64,96},{96,0},{1,33},{33,65},{65,97},{97,1},{2,34}... | collective-permute-start | bytes 1572872 | tf_op jit(solution)/shard_map/ppermute | solution.py:166
  47.5 30.2 %collective-permute-start.18 = (bf16[512,512]{1,0:T(8,128)(2,1)}, bf16[512,512]{1,0:T(8,128)(2,1)}, u32[]{:S(2)}, u32[]{:S(2)}) collective-permute-start(bf16[512,512]{1,0:T(8,128)(2,1)} %copy-done.3), channel_id=1, source_target_pairs={{0,4},{4,2},{2,6},{6,0},{1,5},{5,3},{3,7},{7,1},{8,12},{12,10},{10... | collective-permute-start | bytes 1572872 | tf_op jit(solution)/shard_map/ppermute | solution.py:166
  53.0 9.2 %copy-start.2 = (bf16[512,512]{1,0:T(8,128)(2,1)S(1)}, bf16[512,512]{1,0:T(8,128)(2,1)}, u32[]{:S(2)}) copy-start(bf16[512,512]{1,0:T(8,128)(2,1)} %copy-done.1) | copy-start | bytes 1572868
  53.0 9.2 %copy-start.4 = (bf16[512,512]{1,0:T(8,128)(2,1)S(1)}, bf16[512,512]{1,0:T(8,128)(2,1)}, u32[]{:S(2)}) copy-start(bf16[512,512]{1,0:T(8,128)(2,1)} %copy-done.3) | copy-start | bytes 1572868

commit v2 on v1

v2 whole, which is shorter than its diff:
```python
import functools
import math

import jax
import jax.numpy as jnp
from jax import lax
from jax.experimental import pallas as pl
from jax.experimental.pallas import tpu as pltpu
from jax.sharding import Mesh
from jax.sharding import PartitionSpec as P

AXES = ("x", "z", "yl", "yh", "c")
CHIPS = ("x", "yl", "yh")
DEVICES = ("x", "yl", "yh", "c")
EPSILON = 1e-06
LOGIT_SCALE = 30.0
MARGIN = 0.5
SCALE2 = LOGIT_SCALE / math.log(2.0)
TILE = 512
ROWS = 256
PITCH = 272
NT = (((1,), (1,)), ((), ()))
MIB = 1024 * 1024
OFFSETS = (0, 1, -1, 2)


def unit_block(ref):
    values = ref[...].astype(jnp.float32)
    total = jnp.sum(values * values, axis=1, keepdims=True)
    return (values * lax.rsqrt(total + EPSILON)).astype(jnp.bfloat16)


def unit_kernel(e_ref, c_ref, l_ref, a_ref, u_ref):
    u_ref[...] = unit_block(c_ref)
    a_ref[:ROWS, :] = unit_block(e_ref)
    label = jnp.concatenate([l_ref[...] // 256, l_ref[...] % 256], axis=1)
    label = jnp.broadcast_to(label.astype(jnp.float32), (PITCH - ROWS, 2 * ROWS))
    a_ref[ROWS:, :] = label.astype(jnp.bfloat16)


def normalized(embeddings, centers, labels):
    shapes = [(PITCH, embeddings.shape[1]), centers.shape]
    return pl.pallas_call(
        unit_kernel,
        out_shape=[jax.ShapeDtypeStruct(s, jnp.bfloat16) for s in shapes],
    )(embeddings, centers, labels.reshape(1, ROWS))


def add_terms(x_ref, first, rel, s, t):
    ss, tt = [s, None], [t, None]
    for j in range(TILE // 8):
        x = x_ref[first + 8 * j : first + 8 * j + 8, :]
        at_label = rel == 8 * j
        e = jnp.where(at_label, 0.0, jnp.exp2(x * SCALE2))
        i = j % 2
        ss[i] = e if ss[i] is None else ss[i] + e
        tt[i] = jnp.where(at_label, x, 0.0 if tt[i] is None else tt[i])
    return ss[0] + ss[1], tt[0] + tt[1]


def terms_kernel(tiles, n_c, plan, first, last, owner_ref, base_ref, *refs):
    refs = list(refs)
    if not first:
        refs.pop(0)
    n_e = len(tiles)
    e_refs, c_refs = refs[: n_e // 2], refs[n_e // 2 : n_e // 2 + n_c]
    refs = refs[n_e // 2 + n_c :]
    acc_ref = refs.pop(0)
    outs = [refs.pop(0) for _ in range(2 * last)]
    e_buf, l_buf, c_buf, even, odd, sems = refs

    def rows_copies(tile, ref, base):
        copies = []
        for i in range(2):
            n = tile * 2 + i
            rows = e_buf.at[pl.ds(pl.multiple_of(n * ROWS, ROWS), ROWS)]
            copies.append((ref.at[pl.ds(base + i * PITCH, ROWS)], rows, sems.at[n]))
            labels = ref.at[pl.ds(base + i * PITCH + ROWS, PITCH - ROWS)]
            copies.append((labels, l_buf.at[n], sems.at[2 * n_e + n]))
        return [pltpu.make_async_copy(*c) for c in copies]

    classes = [
        pltpu.make_async_copy(ref, c_buf.at[pl.ds(i * TILE, TILE)], sems.at[4 * n_e + i])
        for i, ref in enumerate(c_refs)
    ]
    start = plan[0][2]
    order = classes[2 * start : 2 * start + 2], classes[: 2 * start] + classes[2 * start + 2 :]
    for copy in order[0] + rows_copies(0, e_refs[0], 0) + order[1]:
        copy.start()
    for i in range(1, n_e):
        for copy in rows_copies(i, e_refs[i // 2], i % 2 * 2 * PITCH):
            copy.start()
    if first:
        acc_ref[...] = jnp.zeros_like(acc_ref)
    sub = lax.broadcasted_iota(jnp.int32, (8, TILE), 0)

    def arrived(tile):
        for copy in rows_copies(tile, e_refs[0], 0):
            copy.wait()

    def product(r, k):
        rows = e_buf[pl.ds(pl.multiple_of(r * TILE, TILE), TILE), :]
        block = c_buf[pl.ds(pl.multiple_of(k * 2 * TILE, 2 * TILE), 2 * TILE), :]
        return lax.dot_general(block, rows, NT, preferred_element_type=jnp.float32)

    def add(x_ref, r, k):
        owners = [owner_ref[(tiles[0] + r) * 2 + i] for i in range(2)]
        halves = [l_buf[2 * r + i].astype(jnp.float32)[:1].astype(jnp.int32) for i in range(2)]
        lab = jnp.concatenate([h[:, :ROWS] * 256 + h[:, ROWS:] for h in halves], axis=1) - sub
        zeros = jnp.zeros((8, TILE), jnp.float32)
        s, t = add_terms(x_ref, 0, lab - base_ref[2 * k], zeros, zeros)
        s, t = add_terms(x_ref, TILE, lab - base_ref[2 * k + 1], s, t)
        for i, o in enumerate(owners):
            acc_ref[o, 0:8, :] += s[:, 256 * i : 256 * i + 256]
            acc_ref[o, 8:16, :] += t[:, 256 * i : 256 * i + 256]

    for segment, (e_lo, e_hi, k_lo, k_hi) in enumerate(plan):
        n_k = k_hi - k_lo

        def step(i, more, e_lo=e_lo, k_lo=k_lo, n_k=n_k):
            if n_k == 1:
                now, then, new = e_lo + 2 * i, e_lo + 2 * i + 1, e_lo + 2 * i + 2
                arrived(then)
                ks = (k_lo, k_lo)
            else:
                now = then = e_lo + i
                new = now + 1
                ks = (k_lo, k_lo + 1)
            if more:
                arrived(new)
            odd[...] = product(then, ks[1])
            add(even, now, ks[0])
            if more:
                even[...] = product(new, k_lo)
            add(odd, then, ks[1])

        arrived(e_lo)
        if segment == 0:
            for copy in order[0]:
                copy.wait()
        even[...] = product(e_lo, k_lo)
        if segment == 0:
            for copy in order[1]:
                copy.wait()
        n = (e_hi - e_lo) * n_k // 2
        lax.fori_loop(0, n - 1, lambda i, _, step=step: step(i, True) or 0, 0)
        step(n - 1, False)

    for which, out in enumerate(outs):
        for g in range(16):
            for i in range(2):
                part = acc_ref[2 * g + which, 8 * i : 8 * i + 8, :]
                out[g, i : i + 1, :] = jnp.sum(part, axis=0, keepdims=True)


def terms(acc, tiles, rows, classes, plan, owners, bases, last=False):
    n_e, n_c, first = len(tiles), len(classes), acc is None
    smem = pl.BlockSpec(memory_space=pltpu.SMEM)
    vmem = pl.BlockSpec(memory_space=pltpu.VMEM)
    blocks = sum((e1 - e0) * (k1 - k0) * 2 for e0, e1, k0, k1 in plan)
    sums = jax.ShapeDtypeStruct((16, 2, 256), jnp.float32)
    out = pl.pallas_call(
        functools.partial(terms_kernel, tiles, n_c, plan, first, last),
        out_shape=[jax.ShapeDtypeStruct((32, 16, 256), jnp.float32)] + [sums] * (2 * last),
        in_specs=[smem, smem]
        + [vmem] * (not first)
        + [pl.BlockSpec(memory_space=pl.ANY)] * (len(rows) + n_c),
        out_specs=[vmem] * (1 + 2 * last),
        scratch_shapes=[
            pltpu.VMEM((n_e * TILE, 512), jnp.bfloat16),
            pltpu.VMEM((n_e * 2, PITCH - ROWS, 512), jnp.bfloat16),
            pltpu.VMEM((n_c * TILE, 512), jnp.bfloat16),
            pltpu.VMEM((2 * TILE, TILE), jnp.float32),
            pltpu.VMEM((2 * TILE, TILE), jnp.float32),
            pltpu.SemaphoreType.DMA((4 * n_e + n_c,)),
        ],
        input_output_aliases={} if first else {2: 0},
        compiler_params=pltpu.CompilerParams(vmem_limit_bytes=24 * MIB),
        cost_estimate=pl.CostEstimate(
            flops=blocks * 2 * TILE**3,
            bytes_accessed=(n_e + n_c) * TILE * 1024,
            transcendentals=blocks * TILE * TILE,
        ),
    )(owners, bases, *([] if first else [acc]), *rows, *classes)
    return out[1:] if last else out[0]


def cross(x, way, by):
    pairs = []
    for i in range(4):
        for y in range(4):
            for core in range(2):
                j, v = (i, (y + by) % 4) if core == way else ((i + by) % 4, y)
                pairs.append((place(i, y) * 2 + core, place(j, v) * 2 + core))
    return lax.ppermute(x, DEVICES, pairs)


def place(x, y):
    return x * 4 + y % 2 * 2 + y // 2


def swap(x):
    return lax.ppermute(x, "c", [(0, 1), (1, 0)])


def up_z(x, by):
    return lax.ppermute(x, "z", [(i, (i + by) % 4) for i in range(4)])


def body(embeddings, centers, labels):
    x, z, core = lax.axis_index("x"), lax.axis_index("z"), lax.axis_index("c")
    yl, yh = lax.axis_index("yl"), lax.axis_index("yh")
    y = yh * 2 + yl

    e, c = normalized(embeddings, centers, labels)
    c_up = up_z(c, 1)
    e_up, e_down, e_far = cross(e, 0, 1), cross(e, 0, -1), cross(e, 0, 2)
    e_up, e_down, e_far, c_up = lax.optimization_barrier((e_up, e_down, e_far, c_up))
    own = jnp.concatenate([e, e_up, e_down, e_far])
    up, down = cross(own, 1, 1), cross(own, 1, -1)
    c_far, c_down = up_z(c_up, 1), up_z(c, -1)
    classes = (c, c_up, c_down, c_far)

    kinds = ((0, 0), (0, 1), (1, 0), (-1, 0), (1, 1), (-1, 1), (2, 1), (2, 0))
    second = jnp.array([d for d, _ in kinds for _ in OFFSETS], jnp.int32)
    first = jnp.array([o for _ in kinds for o in OFFSETS], jnp.int32)
    other = jnp.array([w for _, w in kinds for _ in OFFSETS], jnp.int32)
    along_y = (core + other) % 2 == 0
    gx = (x - jnp.where(along_y, second, first) + 4) % 4
    gy = (y - jnp.where(along_y, first, second) + 4) % 4
    owners = (gx * 4 + gy % 2 * 2 + gy // 2) * 2 + other
    at_z = (z - jnp.array((0, 1, -1, 2), jnp.int32) + 4) % 4
    bases = ((((x * 4 + at_z) * 2 + yl) * 2 + yh) * 2 + core) * TILE

    def run(acc, tiles, rows, n_c, plan, last=False):
        return terms(acc, tiles, rows, classes[:n_c], plan, owners, bases, last)

    own_swapped = swap(own)
    acc = run(None, range(0, 4), (own, own_swapped), 2, ((0, 4, 0, 1),))
    acc, up = lax.optimization_barrier((acc, up))
    far = cross(up, 1, 1)
    rows = (own, own_swapped, up, down)
    acc = run(acc, range(0, 8), rows, 4, ((0, 4, 1, 2), (4, 8, 0, 2)))
    acc, far = lax.optimization_barrier((acc, far))
    up_swapped, down_swapped = swap(up), swap(down)
    acc = run(acc, range(8, 12), (up_swapped, down_swapped), 4, ((0, 4, 0, 2),))
    mine, others = run(acc, range(12, 16), (swap(far), far), 4, ((0, 4, 0, 2),), True)
    mine = mine + swap(others)
    parts = lax.all_to_all(mine, CHIPS, 0, 0, tiled=True)
    sums = jnp.sum(parts, axis=0)
    return margin_loss(sums[0], sums[1])


def margin_loss(other_sum, target_cos):
    sine = jnp.sqrt(jnp.maximum(1.0 - target_cos * target_cos, 0.0))
    shifted = target_cos * math.cos(MARGIN) - sine * math.sin(MARGIN)
    return jnp.log(other_sum + jnp.exp(LOGIT_SCALE * shifted)) - LOGIT_SCALE * shifted


def solution(mesh):
    finer = Mesh(mesh.devices.reshape(4, 4, 2, 2, 2), AXES)
    rows = ("yh", "c", "x", "z", "yl")
    placed = (P(rows, None), P(AXES, None), P(rows))
    return jax.shard_map(body, mesh=finer, in_specs=placed, out_specs=P(rows), check_vma=False)
```

time: 99.9 us -> 83.2 us (0.83)
  starting transfers between devices: 27.1 us -> 13.5 us
  waiting for transfers between devices: 20.3 us -> 18.4 us
  Pallas kernels: 36.3 us -> 35.2 us
    ppermute x19 -> x14, starting transfers between devices: 23.6 us -> 13.5 us  [the longest x6 8.81 us: cross(): return lax.ppermute(x, DEVICES, pairs)]
    all_to_all x1 -> x0, waiting for transfers between devices: 3.96 us -> none  [body(): lax.all_to_all(jnp.broadcast_to(labels[None, None], (16, 1, 256)), GROUP,...]
    all_to_all x1 -> x0, starting transfers between devices: 3.49 us -> none  [body(): lax.all_to_all(jnp.broadcast_to(labels[None, None], (16, 1, 256)), GROUP,...]
    ppermute x19 -> x14, waiting for transfers between devices: 16.3 us -> 18.4 us  [the longest x6 14.1 us: cross(): return lax.ppermute(x, DEVICES, pairs)]
    pallas_call x3 -> x4, Pallas kernels: 34.1 us -> 33 us  [terms(): pl.pallas_call(functools.partial(terms_kernel, tiles, n_c, plan, first, l...]
    unnamed x17, local copies, waits for them, and re-layouts: 1.85 us -> 2.86 us
  transfers between devices with their start and end apart: 20 -> 14, of which waited for: 7 -> 9; matrix products, arithmetic and copies ran while one was open for 2% -> 1% of each run, Pallas kernels for 25% -> 30%
where the time goes in v2:
time: 83.2 us; the launch traced here: 82.9 us
  Pallas kernels  35.2 us (42%)
  waiting for transfers between devices  18.4 us (22%)
  starting transfers between devices  13.5 us (16%)
  blocking collectives  12.2 us (15%)
  local copies, waits for them, and re-layouts  2.88 us (3%)
    pallas_call x4, Pallas kernels, terms(): pl.pallas_call(functools.partial(terms_kernel, tiles, n_c, plan, first, l...  33 us
    ppermute x6, waiting for transfers between devices, cross(): return lax.ppermute(x, DEVICES, pairs)  14.1 us
    all_to_all x1, blocking collectives, body(): parts = lax.all_to_all(mine, CHIPS, 0, 0, tiled=True)  12.2 us
    ppermute x6, starting transfers between devices, cross(): return lax.ppermute(x, DEVICES, pairs)  8.81 us
    ppermute x3, starting transfers between devices, up_z(): return lax.ppermute(x, 'z', [(i, (i + by) % 4) for i in range(4)])  4.09 us
    ppermute x3, waiting for transfers between devices, up_z(): return lax.ppermute(x, 'z', [(i, (i + by) % 4) for i in range(4)])  3.35 us
    unnamed x17, local copies, waits for them, and re-layouts  2.86 us
    pallas_call x1, Pallas kernels, normalized(): pl.pallas_call(unit_kernel, out_shape=[jax.ShapeDtypeStruct(s, jnp.bfloat...  2.23 us
  transfers between devices with their start and end apart: 14, of which 9 were waited for; matrix products, arithmetic and copies ran while one was open for 1% of the time, Pallas kernels for 30%

profile of v2, /device:TPU:0, one launch (start us, length us, event | category | flops | bytes accessed | tf_op | source)
XLA Modules:
  0.0 82.9 jit_solution(2832101296479570986)
XLA Ops:
  0.0 2.2 %shard_map.73 = (bf16[272,512]{1,0:T(8,128)(2,1)}, bf16[512,512]{1,0:T(8,128)(2,1)}) custom-call(bf16[256,512]{1,0:T(8,128)(2,1)} %e_ref.1, bf16[512,512]{1,0:T(8,128)(2,1)} %c_ref.1, s32[1,256]{1,0:T(1,128)} %bitcast.5), custom_call_target="tpu_custom_call" | custom-call | tf_op jit(solution)/shard_map/pallas_call | solution.py:43
  2.2 2.0 %collective-permute-start.3 = (bf16[512,512]{1,0:T(8,128)(2,1)}, bf16[512,512]{1,0:T(8,128)(2,1)S(1)}, u32[]{:S(2)}, u32[]{:S(2)}) collective-permute-start(bf16[512,512]{1,0:T(8,128)(2,1)} %get-tuple-element.18.refs_2_.refs_5_.refs_3_), channel_id=1, source_target_pairs={{0,8},{8,16},{16,24},{24,0},{1,9},{9,17},{17,25},{25,1},{2,10},{10... | collective-permute-start | bytes 1572872 | tf_op jit(solution)/shard_map/ppermute | solution.py:207
  4.2 0.0 copy-start.6
  4.2 0.0 copy-start.3
  4.2 0.0 copy-start.4
  4.2 0.0 copy-start.5
  4.2 1.6 %collective-permute-start = (bf16[272,512]{1,0:T(8,128)(2,1)}, bf16[272,512]{1,0:T(8,128)(2,1)S(1)}, u32[]{:S(2)}, u32[]{:S(2)}) collective-permute-start(bf16[272,512]{1,0:T(8,128)(2,1)} %get-tuple-element.17), channel_id=1, source_target_pairs={{0,4},{1,33},{4,2},{5,37},{2,6},{3,35},{6,0},{7,39},{32,36},{33,65... | collective-permute-start | bytes 835592 | tf_op jit(solution)/shard_map/ppermute | solution.py:195
  5.9 1.7 %collective-permute-start.1 = (bf16[272,512]{1,0:T(8,128)(2,1)}, bf16[272,512]{1,0:T(8,128)(2,1)S(1)}, u32[]{:S(2)}, u32[]{:S(2)}) collective-permute-start(bf16[272,512]{1,0:T(8,128)(2,1)} %get-tuple-element.17), channel_id=1, source_target_pairs={{0,6},{1,97},{4,0},{5,101},{2,4},{3,99},{6,2},{7,103},{32,38},{33,... | collective-permute-start | bytes 835592 | tf_op jit(solution)/shard_map/ppermute | solution.py:195
  7.5 2.0 %collective-permute-start.2 = (bf16[272,512]{1,0:T(8,128)(2,1)}, bf16[272,512]{1,0:T(8,128)(2,1)S(1)}, u32[]{:S(2)}, u32[]{:S(2)}) collective-permute-start(bf16[272,512]{1,0:T(8,128)(2,1)} %get-tuple-element.17), channel_id=1, source_target_pairs={{0,2},{1,65},{4,6},{5,69},{2,0},{3,67},{6,4},{7,71},{32,34},{33,97... | collective-permute-start | bytes 835592 | tf_op jit(solution)/shard_map/ppermute | solution.py:195
  9.5 1.0 %constant_dynamic-update-slice_fusion.3 = bf16[1088,512]{1,0:T(8,128)(2,1)S(1)} fusion(bf16[272,512]{1,0:T(8,128)(2,1)} %get-tuple-element.17), kind=kLoop, calls=%fused_computation.3 | loop fusion | bytes 557056
  10.5 1.7 %collective-permute-done = bf16[272,512]{1,0:T(8,128)(2,1)S(1)} collective-permute-done((bf16[272,512]{1,0:T(8,128)(2,1)}, bf16[272,512]{1,0:T(8,128)(2,1)S(1)}, u32[]{:S(2)}, u32[]{:S(2)}) %collective-permute-start) | collective-permute-done | bytes 278560 | tf_op jit(solution)/shard_map/ppermute | solution.py:195
  12.3 0.4 collective-permute-done.1
  12.6 3.9 %collective-permute-done.2 = bf16[272,512]{1,0:T(8,128)(2,1)S(1)} collective-permute-done((bf16[272,512]{1,0:T(8,128)(2,1)}, bf16[272,512]{1,0:T(8,128)(2,1)S(1)}, u32[]{:S(2)}, u32[]{:S(2)}) %collective-permute-start.2) | collective-permute-done | bytes 278560 | tf_op jit(solution)/shard_map/ppermute | solution.py:195
  16.5 2.0 %collective-permute-done.3.refs_3_.refs_6_.refs_4_ = bf16[512,512]{1,0:T(8,128)(2,1)S(1)} collective-permute-done((bf16[512,512]{1,0:T(8,128)(2,1)}, bf16[512,512]{1,0:T(8,128)(2,1)S(1)}, u32[]{:S(2)}, u32[]{:S(2)}) %collective-permute-start.3) | collective-permute-done | bytes 524320 | tf_op jit(solution)/shard_map/ppermute | solution.py:207
  18.5 0.0 copy-start
  18.6 0.7 copy-done
  19.3 0.0 collective-permute-start.4
  19.3 1.5 %collective-permute-start.5 = (bf16[1088,512]{1,0:T(8,128)(2,1)S(1)}, bf16[1088,512]{1,0:T(8,128)(2,1)S(1)}, u32[]{:S(2)}, u32[]{:S(2)}) collective-permute-start(bf16[1088,512]{1,0:T(8,128)(2,1)S(1)} %constant_dynamic-update-slice_fusion.refs_0_.refs_1_), channel_id=1, source_target_pairs={{0,32},{1,5},{4,36},{5,3},{2,34},{3,7},{6,38},{7,1},{32,64},{33,37... | collective-permute-start | bytes 3342344 | tf_op jit(solution)/shard_map/ppermute | solution.py:195
  20.8 1.7 %collective-permute-start.7 = (bf16[512,512]{1,0:T(8,128)(2,1)}, bf16[512,512]{1,0:T(8,128)(2,1)}, u32[]{:S(2)}, u32[]{:S(2)}) collective-permute-start(bf16[512,512]{1,0:T(8,128)(2,1)} %get-tuple-element.18.refs_2_.refs_5_.refs_3_), channel_id=1, source_target_pairs={{0,24},{8,0},{16,8},{24,16},{1,25},{9,1},{17,9},{25,17},{2,26},{10... | collective-permute-start | bytes 1572872 | tf_op jit(solution)/shard_map/ppermute | solution.py:207
  22.5 1.7 %collective-permute-start.6 = (bf16[1088,512]{1,0:T(8,128)(2,1)S(1)}, bf16[1088,512]{1,0:T(8,128)(2,1)S(1)}, u32[]{:S(2)}, u32[]{:S(2)}) collective-permute-start(bf16[1088,512]{1,0:T(8,128)(2,1)S(1)} %constant_dynamic-update-slice_fusion.refs_0_.refs_1_), channel_id=1, source_target_pairs={{0,96},{1,7},{4,100},{5,1},{2,98},{3,5},{6,102},{7,3},{32,0},{33,3... | collective-permute-start | bytes 3342344 | tf_op jit(solution)/shard_map/ppermute | solution.py:195
  24.3 0.0 copy-done.6
  24.3 0.0 copy-done.3
  24.3 0.0 copy-done.4
  24.3 0.0 copy-done.5
  24.4 0.4 collective-permute-start.8
  24.7 0.0 collective-permute-done.4.refs_1_.refs_2_
  24.7 0.0 copy-start.1
  24.7 1.1 %copy-done.1 = bf16[512,512]{1,0:T(8,128)(2,1)S(1)} copy-done((bf16[512,512]{1,0:T(8,128)(2,1)S(1)}, bf16[512,512]{1,0:T(8,128)(2,1)}, u32[]{:S(2)}) %copy-start.1) | copy-done | bytes 524312
  25.8 0.0 copy-start.2
  25.8 5.6 %shard_map.74.refs_0_ = f32[32,16,256]{2,1,0:T(8,128)S(1)} custom-call(s32[32]{0:T(128)S(1)} %multiply_add_fusion.owner_ref, s32[4]{0:T(128)S(1)} %fusion.16.base_ref, bf16[1088,512]{1,0:T(8,128)(2,1)S(1)} %constant_dynamic-update-slice_fusion.refs_0_.refs_1_, bf16[1088,512]{1,0:T(8,128)(2,1)S(1)} %collective-permute-done.4.refs_1_.refs_2_, ...), custom_call_target="tpu_custom_call" | custom-call | flops 2147483648 | bytes 3145728 | tf_op jit(solution)/shard_map/pallas_call | solution.py:162
  31.4 4.6 %collective-permute-done.5.refs_3_ = bf16[1088,512]{1,0:T(8,128)(2,1)S(1)} collective-permute-done((bf16[1088,512]{1,0:T(8,128)(2,1)S(1)}, bf16[1088,512]{1,0:T(8,128)(2,1)S(1)}, u32[]{:S(2)}, u32[]{:S(2)}) %collective-permute-start.5) | collective-permute-done | bytes 1114144 | tf_op jit(solution)/shard_map/ppermute | solution.py:195
  36.0 0.3 collective-permute-start.9
  36.3 0.0 collective-permute-start.10
  36.3 1.7 %collective-permute-done.6.refs_4_ = bf16[1088,512]{1,0:T(8,128)(2,1)S(1)} collective-permute-done((bf16[1088,512]{1,0:T(8,128)(2,1)S(1)}, bf16[1088,512]{1,0:T(8,128)(2,1)S(1)}, u32[]{:S(2)}, u32[]{:S(2)}) %collective-permute-start.6) | collective-permute-done | bytes 1114144 | tf_op jit(solution)/shard_map/ppermute | solution.py:195
  38.0 0.0 collective-permute-start.11
  38.0 0.0 collective-permute-done.7.refs_7_.refs_5_
  38.0 1.4 %collective-permute-done.8.refs_8_.refs_6_ = bf16[512,512]{1,0:T(8,128)(2,1)S(1)} collective-permute-done((bf16[512,512]{1,0:T(8,128)(2,1)}, bf16[512,512]{1,0:T(8,128)(2,1)S(1)}, u32[]{:S(2)}, u32[]{:S(2)}) %collective-permute-start.8) | collective-permute-done | bytes 524320 | tf_op jit(solution)/shard_map/ppermute | solution.py:207
  39.4 0.0 copy-done.2
  39.4 11.5 %shard_map.75.refs_0_ = f32[32,16,256]{2,1,0:T(8,128)S(1)} custom-call(s32[32]{0:T(128)S(1)} %multiply_add_fusion.owner_ref, s32[4]{0:T(128)S(1)} %fusion.16.base_ref, f32[32,16,256]{2,1,0:T(8,128)S(1)} %shard_map.74.refs_0_, bf16[1088,512]{1,0:T(8,128)(2,1)S(1)} %constant_dynamic-update-slice_fusion.refs_0_.refs_1_, ...), custom_call_target="tpu_custom_call", output_to_operand_aliasing={{}: (2, {})} | custom-call | flops 6442450944 | bytes 6291456 | tf_op jit(solution)/shard_map/pallas_call | solution.py:162
  50.9 1.8 %collective-permute-done.9.refs_2_ = bf16[1088,512]{1,0:T(8,128)(2,1)S(1)} collective-permute-done((bf16[1088,512]{1,0:T(8,128)(2,1)S(1)}, bf16[1088,512]{1,0:T(8,128)(2,1)S(1)}, u32[]{:S(2)}, u32[]{:S(2)}) %collective-permute-start.9) | collective-permute-done | bytes 1114144 | tf_op jit(solution)/shard_map/ppermute | solution.py:195
  52.7 0.0 collective-permute-start.12
  52.7 0.0 collective-permute-done.10.refs_1_
  52.7 0.0 collective-permute-done.11.refs_2_
  52.7 7.9 %shard_map.76.refs_0_ = f32[32,16,256]{2,1,0:T(8,128)S(1)} custom-call(s32[32]{0:T(128)S(1)} %multiply_add_fusion.owner_ref, s32[4]{0:T(128)S(1)} %fusion.16.base_ref, f32[32,16,256]{2,1,0:T(8,128)S(1)} %shard_map.75.refs_0_, bf16[1088,512]{1,0:T(8,128)(2,1)S(1)} %collective-permute-done.10.refs_1_, ...), custom_call_target="tpu_custom_call", output_to_operand_aliasing={{}: (2, {})} | custom-call | flops 4294967296 | bytes 4194304 | tf_op jit(solution)/shard_map/pallas_call | solution.py:162
  60.6 0.0 collective-permute-done.12.refs_1_
  60.6 8.0 %shard_map.77 = (f32[32,16,256]{2,1,0:T(8,128)S(1)}, f32[16,2,256]{2,1,0:T(2,128)S(1)}, f32[16,2,256]{2,1,0:T(2,128)S(1)}) custom-call(s32[32]{0:T(128)S(1)} %multiply_add_fusion.owner_ref, s32[4]{0:T(128)S(1)} %fusion.16.base_ref, f32[32,16,256]{2,1,0:T(8,128)S(1)} %shard_map.76.refs_0_, ...), custom_call_target="tpu_custom_call", output_to_operand_aliasing={{0}: (2, {})} | custom-call | flops 4294967296 | bytes 4194304 | tf_op jit(solution)/shard_map/pallas_call | solution.py:162
  68.7 0.6 collective-permute-start.13
  69.3 0.9 %collective-permute-done.13 = f32[16,2,256]{2,1,0:T(2,128)S(1)} collective-permute-done((f32[16,2,256]{2,1,0:T(2,128)S(1)}, f32[16,2,256]{2,1,0:T(2,128)S(1)}, u32[]{:S(2)}, u32[]{:S(2)}) %collective-permute-start.13) | collective-permute-done | bytes 32800 | tf_op jit(solution)/shard_map/ppermute | solution.py:203
  70.1 12.2 %all_to_all.5 = f32[16,2,256]{2,1,0:T(2,128)S(1)} all-to-all(f32[16,2,256]{2,1,0:T(2,128)S(1)} %add.104), channel_id=1, replica_groups=mesh['x'=4,'z'=4,'yl'=2,'yh'=2,'c'=2] {'x','yl','yh'}, dimensions={0} | all-to-all | bytes 65536 | tf_op jit(solution)/shard_map/all_to_all | solution.py:249
  82.3 0.6 log_subtract_fusion
  (8 shorter events, 0.2 us)
Async XLA Ops:
  2.2 16.3 %collective-permute-start.3 = (bf16[512,512]{1,0:T(8,128)(2,1)}, bf16[512,512]{1,0:T(8,128)(2,1)S(1)}, u32[]{:S(2)}, u32[]{:S(2)}) collective-permute-start(bf16[512,512]{1,0:T(8,128)(2,1)} %get-tuple-element.18.refs_2_.refs_5_.refs_3_), channel_id=1, source_target_pairs={{0,8},{8,16},{16,24},{24,0},{1,9},{9,17},{17,25},{25,1},{2,10},{10... | collective-permute-start | bytes 1572872 | tf_op jit(solution)/shard_map/ppermute | solution.py:207
  4.2 20.0 %copy-start.6 = (s32[4]{0:T(128)S(1)}, s32[4]{0:T(128)}, u32[]{:S(2)}) copy-start(s32[4]{0:T(128)} %constant.103) | copy-start | bytes 52
  4.2 20.1 %copy-start.3 = (s32[32]{0:T(128)S(1)}, s32[32]{0:T(128)}, u32[]{:S(2)}) copy-start(s32[32]{0:T(128)} %constant.100.clone) | copy-start | bytes 388
  4.2 20.1 %copy-start.4 = (s32[32]{0:T(128)S(1)}, s32[32]{0:T(128)}, u32[]{:S(2)}) copy-start(s32[32]{0:T(128)} %constant.101.clone) | copy-start | bytes 388
  4.2 20.1 %copy-start.5 = (s32[32]{0:T(128)S(1)}, s32[32]{0:T(128)}, u32[]{:S(2)}) copy-start(s32[32]{0:T(128)} %constant.99.clone) | copy-start | bytes 388
  4.2 8.0 %collective-permute-start = (bf16[272,512]{1,0:T(8,128)(2,1)}, bf16[272,512]{1,0:T(8,128)(2,1)S(1)}, u32[]{:S(2)}, u32[]{:S(2)}) collective-permute-start(bf16[272,512]{1,0:T(8,128)(2,1)} %get-tuple-element.17), channel_id=1, source_target_pairs={{0,4},{1,33},{4,2},{5,37},{2,6},{3,35},{6,0},{7,39},{32,36},{33,65... | collective-permute-start | bytes 835592 | tf_op jit(solution)/shard_map/ppermute | solution.py:195
  5.9 6.8 %collective-permute-start.1 = (bf16[272,512]{1,0:T(8,128)(2,1)}, bf16[272,512]{1,0:T(8,128)(2,1)S(1)}, u32[]{:S(2)}, u32[]{:S(2)}) collective-permute-start(bf16[272,512]{1,0:T(8,128)(2,1)} %get-tuple-element.17), channel_id=1, source_target_pairs={{0,6},{1,97},{4,0},{5,101},{2,4},{3,99},{6,2},{7,103},{32,38},{33,... | collective-permute-start | bytes 835592 | tf_op jit(solution)/shard_map/ppermute | solution.py:195
  7.5 9.0 %collective-permute-start.2 = (bf16[272,512]{1,0:T(8,128)(2,1)}, bf16[272,512]{1,0:T(8,128)(2,1)S(1)}, u32[]{:S(2)}, u32[]{:S(2)}) collective-permute-start(bf16[272,512]{1,0:T(8,128)(2,1)} %get-tuple-element.17), channel_id=1, source_target_pairs={{0,2},{1,65},{4,6},{5,69},{2,0},{3,67},{6,4},{7,71},{32,34},{33,97... | collective-permute-start | bytes 835592 | tf_op jit(solution)/shard_map/ppermute | solution.py:195
  18.5 0.8 copy-start
  19.3 5.4 %collective-permute-start.4 = (bf16[1088,512]{1,0:T(8,128)(2,1)S(1)}, bf16[1088,512]{1,0:T(8,128)(2,1)S(1)}, u32[]{:S(2)}, u32[]{:S(2)}) collective-permute-start(bf16[1088,512]{1,0:T(8,128)(2,1)S(1)} %constant_dynamic-update-slice_fusion.refs_0_.refs_1_), channel_id=1, source_target_pairs={{0,1},{1,0},{2,3},{3,2},{4,5},{5,4},{6,7},{7,6},{8,9},{9,8},{10,11... | collective-permute-start | bytes 3342344 | tf_op jit(solution)/shard_map/ppermute | solution.py:203
  19.3 16.7 %collective-permute-start.5 = (bf16[1088,512]{1,0:T(8,128)(2,1)S(1)}, bf16[1088,512]{1,0:T(8,128)(2,1)S(1)}, u32[]{:S(2)}, u32[]{:S(2)}) collective-permute-start(bf16[1088,512]{1,0:T(8,128)(2,1)S(1)} %constant_dynamic-update-slice_fusion.refs_0_.refs_1_), channel_id=1, source_target_pairs={{0,32},{1,5},{4,36},{5,3},{2,34},{3,7},{6,38},{7,1},{32,64},{33,37... | collective-permute-start | bytes 3342344 | tf_op jit(solution)/shard_map/ppermute | solution.py:195
  20.8 17.3 %collective-permute-start.7 = (bf16[512,512]{1,0:T(8,128)(2,1)}, bf16[512,512]{1,0:T(8,128)(2,1)}, u32[]{:S(2)}, u32[]{:S(2)}) collective-permute-start(bf16[512,512]{1,0:T(8,128)(2,1)} %get-tuple-element.18.refs_2_.refs_5_.refs_3_), channel_id=1, source_target_pairs={{0,24},{8,0},{16,8},{24,16},{1,25},{9,1},{17,9},{25,17},{2,26},{10... | collective-permute-start | bytes 1572872 | tf_op jit(solution)/shard_map/ppermute | solution.py:207
  22.5 15.5 %collective-permute-start.6 = (bf16[1088,512]{1,0:T(8,128)(2,1)S(1)}, bf16[1088,512]{1,0:T(8,128)(2,1)S(1)}, u32[]{:S(2)}, u32[]{:S(2)}) collective-permute-start(bf16[1088,512]{1,0:T(8,128)(2,1)S(1)} %constant_dynamic-update-slice_fusion.refs_0_.refs_1_), channel_id=1, source_target_pairs={{0,96},{1,7},{4,100},{5,1},{2,98},{3,5},{6,102},{7,3},{32,0},{33,3... | collective-permute-start | bytes 3342344 | tf_op jit(solution)/shard_map/ppermute | solution.py:195
  24.4 15.0 %collective-permute-start.8 = (bf16[512,512]{1,0:T(8,128)(2,1)}, bf16[512,512]{1,0:T(8,128)(2,1)S(1)}, u32[]{:S(2)}, u32[]{:S(2)}) collective-permute-start(bf16[512,512]{1,0:T(8,128)(2,1)} %copy-done), channel_id=1, source_target_pairs={{0,8},{8,16},{16,24},{24,0},{1,9},{9,17},{17,25},{25,1},{2,10},{10... | collective-permute-start | bytes 1572872 | tf_op jit(solution)/shard_map/ppermute | solution.py:207
  24.7 1.1 %copy-start.1 = (bf16[512,512]{1,0:T(8,128)(2,1)S(1)}, bf16[512,512]{1,0:T(8,128)(2,1)}, u32[]{:S(2)}) copy-start(bf16[512,512]{1,0:T(8,128)(2,1)} %copy-done) | copy-start | bytes 1572868
  25.8 13.6 %copy-start.2 = (bf16[512,512]{1,0:T(8,128)(2,1)S(1)}, bf16[512,512]{1,0:T(8,128)(2,1)}, u32[]{:S(2)}) copy-start(bf16[512,512]{1,0:T(8,128)(2,1)} %copy-done) | copy-start | bytes 1572868
  36.0 16.7 %collective-permute-start.9 = (bf16[1088,512]{1,0:T(8,128)(2,1)S(1)}, bf16[1088,512]{1,0:T(8,128)(2,1)S(1)}, u32[]{:S(2)}, u32[]{:S(2)}) collective-permute-start(bf16[1088,512]{1,0:T(8,128)(2,1)S(1)} %collective-permute-done.5.refs_3_), channel_id=1, source_target_pairs={{0,32},{1,5},{4,36},{5,3},{2,34},{3,7},{6,38},{7,1},{32,64},{33,37... | collective-permute-start | bytes 3342344 | tf_op jit(solution)/shard_map/ppermute | solution.py:195
  36.3 16.4 %collective-permute-start.10 = (bf16[1088,512]{1,0:T(8,128)(2,1)S(1)}, bf16[1088,512]{1,0:T(8,128)(2,1)S(1)}, u32[]{:S(2)}, u32[]{:S(2)}) collective-permute-start(bf16[1088,512]{1,0:T(8,128)(2,1)S(1)} %collective-permute-done.5.refs_3_), channel_id=1, source_target_pairs={{0,1},{1,0},{2,3},{3,2},{4,5},{5,4},{6,7},{7,6},{8,9},{9,8},{10,11... | collective-permute-start | bytes 3342344 | tf_op jit(solution)/shard_map/ppermute | solution.py:203
  38.0 14.7 %collective-permute-start.11 = (bf16[1088,512]{1,0:T(8,128)(2,1)S(1)}, bf16[1088,512]{1,0:T(8,128)(2,1)S(1)}, u32[]{:S(2)}, u32[]{:S(2)}) collective-permute-start(bf16[1088,512]{1,0:T(8,128)(2,1)S(1)} %collective-permute-done.6.refs_4_), channel_id=1, source_target_pairs={{0,1},{1,0},{2,3},{3,2},{4,5},{5,4},{6,7},{7,6},{8,9},{9,8},{10,11... | collective-permute-start | bytes 3342344 | tf_op jit(solution)/shard_map/ppermute | solution.py:203
  52.7 7.9 %collective-permute-start.12 = (bf16[1088,512]{1,0:T(8,128)(2,1)S(1)}, bf16[1088,512]{1,0:T(8,128)(2,1)S(1)}, u32[]{:S(2)}, u32[]{:S(2)}) collective-permute-start(bf16[1088,512]{1,0:T(8,128)(2,1)S(1)} %collective-permute-done.9.refs_2_), channel_id=1, source_target_pairs={{0,1},{1,0},{2,3},{3,2},{4,5},{5,4},{6,7},{7,6},{8,9},{9,8},{10,11... | collective-permute-start | bytes 3342344 | tf_op jit(solution)/shard_map/ppermute | solution.py:203
  68.7 1.4 %collective-permute-start.13 = (f32[16,2,256]{2,1,0:T(2,128)S(1)}, f32[16,2,256]{2,1,0:T(2,128)S(1)}, u32[]{:S(2)}, u32[]{:S(2)}) collective-permute-start(f32[16,2,256]{2,1,0:T(2,128)S(1)} %get-tuple-element.28), channel_id=1, source_target_pairs={{0,1},{1,0},{2,3},{3,2},{4,5},{5,4},{6,7},{7,6},{8,9},{9,8},{10,11... | collective-permute-start | bytes 98312 | tf_op jit(solution)/shard_map/ppermute | solution.py:203

commit v3 on v2

v3 whole, which is shorter than its diff:
```python
import functools
import math

import jax
import jax.numpy as jnp
from jax import lax
from jax.experimental import pallas as pl
from jax.experimental.pallas import tpu as pltpu
from jax.sharding import Mesh
from jax.sharding import PartitionSpec as P

AXES = ("x", "z", "yl", "yh", "c")
CHIPS = ("x", "yl", "yh")
DEVICES = ("x", "yl", "yh", "c")
EPSILON = 1e-06
LOGIT_SCALE = 30.0
MARGIN = 0.5
SCALE2 = LOGIT_SCALE / math.log(2.0)
TILE = 512
WIDE = 1024
PARTS = 4
ROWS = 256
PITCH = 272
NT = (((1,), (1,)), ((), ()))
MIB = 1024 * 1024
OFFSETS = (0, 1, -1, 2)


def unit_block(ref):
    values = ref[...].astype(jnp.float32)
    total = jnp.sum(values * values, axis=1, keepdims=True)
    return (values * lax.rsqrt(total + EPSILON)).astype(jnp.bfloat16)


def unit_kernel(e_ref, c_ref, l_ref, a_ref, u_ref):
    u_ref[...] = unit_block(c_ref)
    a_ref[:ROWS, :] = unit_block(e_ref)
    label = jnp.concatenate([l_ref[...] // 256, l_ref[...] % 256], axis=1)
    label = jnp.broadcast_to(label.astype(jnp.float32), (PITCH - ROWS, 2 * ROWS))
    a_ref[ROWS:, :] = label.astype(jnp.bfloat16)


def normalized(embeddings, centers, labels):
    shapes = [(PITCH, embeddings.shape[1]), centers.shape]
    return pl.pallas_call(
        unit_kernel,
        out_shape=[jax.ShapeDtypeStruct(s, jnp.bfloat16) for s in shapes],
    )(embeddings, centers, labels.reshape(1, ROWS))


def add_terms(x_ref, rel):
    ss, tt = [0.0, 0.0], [0.0, 0.0]
    for j in range(TILE // 8):
        x = x_ref[8 * j : 8 * j + 8, :]
        at_label = rel == 8 * j
        e = jnp.where(at_label, 0.0, jnp.exp2(x * SCALE2))
        i = j % 2
        ss[i] = ss[i] + e
        tt[i] = jnp.where(at_label, x, tt[i])
    return ss[0] + ss[1], tt[0] + tt[1]


def steps_of(plan):
    rows, seen_r, seen_k = [], set(), set()
    for tiles, pieces in plan:
        for r in tiles:
            for k in pieces:
                rows.append((r, k, int(r not in seen_r), int(k not in seen_k)))
                seen_r.add(r)
                seen_k.add(k)
    return rows


def terms_kernel(shares, n_c, n_steps, at_owner, at_step, first, last, info_ref, *refs):
    refs = list(refs)
    if not first:
        refs.pop(0)
    n_e = len(shares)
    e_refs = [[refs.pop(0) for _ in range(n)] for n in shares]
    c_refs = [refs.pop(0) for _ in range(n_c)]
    acc_ref = refs.pop(0)
    outs = [refs.pop(0) for _ in range(2 * last)]
    e_buf, l_buf, c_buf, even, odd, sems = refs

    def part_copies(n, ref, first_row):
        rows = e_buf.at[pl.ds(pl.multiple_of(n * ROWS, ROWS), ROWS)]
        labels = ref.at[pl.ds(first_row + ROWS, PITCH - ROWS)]
        return [
            pltpu.make_async_copy(ref.at[pl.ds(first_row, ROWS)], rows, sems.at[n]),
            pltpu.make_async_copy(labels, l_buf.at[n], sems.at[PARTS * n_e + n]),
        ]

    def rows_copies(tile):
        copies = []
        for i in range(PARTS):
            each = PARTS // shares[tile]
            ref = e_refs[tile][i // each]
            copies += part_copies(tile * PARTS + i, ref, i % each * PITCH)
        return copies

    def class_copy(k, ref):
        here = c_buf.at[pl.ds(pl.multiple_of(k * TILE, TILE), TILE)]
        return pltpu.make_async_copy(ref, here, sems.at[2 * PARTS * n_e + k])

    def entry(step, which):
        return info_ref[at_step + 4 * step + which]

    starts = [[class_copy(k, ref)] for k, ref in enumerate(c_refs)]
    starts[1:1] = [rows_copies(0)]
    starts += [rows_copies(r) for r in range(1, n_e)]
    for copies in starts:
        for copy in copies:
            copy.start()
    if first:
        acc_ref[...] = jnp.zeros_like(acc_ref)
    sub = lax.broadcasted_iota(jnp.int32, (8, WIDE), 0)

    def arrived(step):
        @pl.when(entry(step, 2) == 1)
        def _():
            for i in range(PARTS):
                for copy in part_copies(entry(step, 0) * PARTS + i, e_refs[0][0], 0):
                    copy.wait()

        @pl.when(entry(step, 3) == 1)
        def _():
            class_copy(entry(step, 1), c_refs[0]).wait()

    def product(step):
        rows = e_buf[pl.ds(pl.multiple_of(entry(step, 0) * WIDE, WIDE), WIDE), :]
        block = c_buf[pl.ds(pl.multiple_of(entry(step, 1) * TILE, TILE), TILE), :]
        return lax.dot_general(block, rows, NT, preferred_element_type=jnp.float32)

    def add(x_ref, step):
        n = entry(step, 0) * PARTS
        parts = [l_buf[n + i].astype(jnp.float32)[:1].astype(jnp.int32) for i in range(PARTS)]
        lab = jnp.concatenate([h[:, :ROWS] * 256 + h[:, ROWS:] for h in parts], axis=1)
        s, t = add_terms(x_ref, lab - sub - info_ref[entry(step, 1)])
        for i in range(PARTS):
            o = info_ref[at_owner + n + i]
            acc_ref[o, 0:8, :] += s[:, ROWS * i : ROWS * i + ROWS]
            acc_ref[o, 8:16, :] += t[:, ROWS * i : ROWS * i + ROWS]

    arrived(0)
    even[...] = product(0)

    def two_steps(i, _):
        step = 2 * i
        more = step + 2 < n_steps
        arrived(step + 1)
        pl.when(more)(lambda: arrived(step + 2))
        odd[...] = product(step + 1)
        add(even, step)

        even[...] = product(jnp.minimum(step + 2, n_steps - 1))
        add(odd, step + 1)
        return 0

    lax.fori_loop(0, n_steps // 2, two_steps, 0)

    for which, out in enumerate(outs):
        for g in range(16):
            for i in range(2):
                part = acc_ref[2 * g + which, 8 * i : 8 * i + 8, :]
                out[g, i : i + 1, :] = jnp.sum(part, axis=0, keepdims=True)


def terms(acc, tiles, classes, plan, info, at_owner, at_step, last=False):
    n_e, n_c, first = len(tiles), len(classes), acc is None
    rows = [piece for tile in tiles for piece in tile]
    smem = pl.BlockSpec(memory_space=pltpu.SMEM)
    vmem = pl.BlockSpec(memory_space=pltpu.VMEM)
    n_steps = len(steps_of(plan))
    sums = jax.ShapeDtypeStruct((16, 2, 256), jnp.float32)
    out = pl.pallas_call(
        functools.partial(terms_kernel, [len(t) for t in tiles], n_c, n_steps, at_owner, at_step, first, last),
        out_shape=[jax.ShapeDtypeStruct((32, 16, 256), jnp.float32)] + [sums] * (2 * last),
        in_specs=[smem] + [vmem] * (not first) + [pl.BlockSpec(memory_space=pl.ANY)] * (len(rows) + n_c),
        out_specs=[vmem] * (1 + 2 * last),
        scratch_shapes=[
            pltpu.VMEM((n_e * WIDE, 512), jnp.bfloat16),
            pltpu.VMEM((n_e * PARTS, PITCH - ROWS, 512), jnp.bfloat16),
            pltpu.VMEM((n_c * TILE, 512), jnp.bfloat16),
            pltpu.VMEM((TILE, WIDE), jnp.float32),
            pltpu.VMEM((TILE, WIDE), jnp.float32),
            pltpu.SemaphoreType.DMA((2 * PARTS * n_e + n_c,)),
        ],
        input_output_aliases={} if first else {1: 0},
        compiler_params=pltpu.CompilerParams(vmem_limit_bytes=(52 if first else 24) * MIB),
        cost_estimate=pl.CostEstimate(
            flops=n_steps * 2 * TILE * WIDE * 512,
            bytes_accessed=(2 * n_e + n_c) * TILE * 1024,
            transcendentals=n_steps * TILE * WIDE,
        ),
    )(info, *([] if first else [acc]), *rows, *classes)
    return out[1:] if last else out[0]


def cross(x, way, by):
    pairs = []
    for i in range(4):
        for y in range(4):
            for core in range(2):
                j, v = (i, (y + by) % 4) if core == way else ((i + by) % 4, y)
                pairs.append((place(i, y) * 2 + core, place(j, v) * 2 + core))
    return lax.ppermute(x, DEVICES, pairs)


def place(x, y):
    return x * 4 + y % 2 * 2 + y // 2


def swap(x):
    return lax.ppermute(x, "c", [(0, 1), (1, 0)])


def up_z(x, by):
    return lax.ppermute(x, "z", [(i, (i + by) % 4) for i in range(4)])


def body(embeddings, centers, labels):
    x, z, core = lax.axis_index("x"), lax.axis_index("z"), lax.axis_index("c")
    yl, yh = lax.axis_index("yl"), lax.axis_index("yh")
    y = yh * 2 + yl

    e, c = normalized(embeddings, centers, labels)
    c_up, c_down = up_z(c, 1), up_z(c, -1)
    e_up, e_down, e_far = cross(e, 0, 1), cross(e, 0, -1), cross(e, 0, 2)
    e_far, c_up, c_down, e_up, e_down = lax.optimization_barrier(
        (e_far, c_up, c_down, e_up, e_down)
    )
    own = jnp.concatenate([e, e_up, e_down, e_far])
    up, down = cross(own, 1, 1), cross(own, 1, -1)
    c_far = up_z(c_up, 1)
    classes = (c, c_up, c_down, c_far)

    kinds = ((0, 0), (0, 1), (1, 0), (-1, 0), (1, 1), (-1, 1), (2, 1), (2, 0))
    plans = (
        (((0, 1), (0, 1, 2)),),
        (((2, 3), (0, 1, 2, 3)), ((0, 1), (3,))),
        (((0, 1), (0, 1, 2, 3)),),
        (((0, 1), (0, 1, 2, 3)),),
    )
    firsts = (0, 0, 4, 6)
    second = jnp.array([d for d, _ in kinds for _ in OFFSETS], jnp.int32)
    first = jnp.array([o for _ in kinds for o in OFFSETS], jnp.int32)
    other = jnp.array([w for _, w in kinds for _ in OFFSETS], jnp.int32)
    along_y = (core + other) % 2 == 0
    gx = (x - jnp.where(along_y, second, first) + 4) % 4
    gy = (y - jnp.where(along_y, first, second) + 4) % 4
    owners = (gx * 4 + gy % 2 * 2 + gy // 2) * 2 + other
    at_z = (z - jnp.array((0, 1, -1, 2), jnp.int32) + 4) % 4
    bases = ((((x * 4 + at_z) * 2 + yl) * 2 + yh) * 2 + core) * TILE
    steps = [steps_of(plan) for plan in plans]
    table = jnp.array([n for rows in steps for row in rows for n in row], jnp.int32)
    info = jnp.concatenate([bases, owners, table])

    def run(acc, call, rows, n_c=4, last=False):
        at_step = 4 + len(kinds) * PARTS + sum(4 * len(r) for r in steps[:call])
        at_owner = 4 + firsts[call] * PARTS
        return terms(acc, rows, classes[:n_c], plans[call], info, at_owner, at_step, last)

    own_swapped = swap(own)
    acc = run(None, 0, ((own,), (own_swapped,)), 3)
    acc, up = lax.optimization_barrier((acc, up))
    half = up.shape[0] // 2
    far_a = cross(up[:half], 1, 1)
    down, c_far = lax.optimization_barrier((down, c_far))
    classes = (c, c_up, c_down, c_far)
    far_b = cross(down[half:], 1, -1)
    acc = run(acc, 1, ((own,), (own_swapped,), (up,), (down,)))
    acc, far_a, far_b = lax.optimization_barrier((acc, far_a, far_b))
    acc = run(acc, 2, ((swap(up),), (swap(down),)))
    far, far_swapped = (far_a, far_b), (swap(far_a), swap(far_b))
    mine, others = run(acc, 3, (far_swapped, far), last=True)
    mine = mine + swap(others)
    parts = lax.all_to_all(mine, CHIPS, 0, 0, tiled=True)
    sums = jnp.sum(parts, axis=0)
    return margin_loss(sums[0], sums[1])


def margin_loss(other_sum, target_cos):
    sine = jnp.sqrt(jnp.maximum(1.0 - target_cos * target_cos, 0.0))
    shifted = target_cos * math.cos(MARGIN) - sine * math.sin(MARGIN)
    return jnp.log(other_sum + jnp.exp(LOGIT_SCALE * shifted)) - LOGIT_SCALE * shifted


def solution(mesh):
    finer = Mesh(mesh.devices.reshape(4, 4, 2, 2, 2), AXES)
    rows = ("yh", "c", "x", "z", "yl")
    placed = (P(rows, None), P(AXES, None), P(rows))
    return jax.shard_map(body, mesh=finer, in_specs=placed, out_specs=P(rows), check_vma=False)
```

time: 83.2 us -> 81.3 us (0.977)
  waiting for transfers between devices: 18.4 us -> 10.2 us
  starting transfers between devices: 13.5 us -> 19.6 us
  Pallas kernels: 35.2 us -> 34.2 us
  local copies, waits for them, and re-layouts: 2.88 us -> 3.87 us
    ppermute x6 -> x7, waiting for transfers between devices: 14.1 us -> 7.48 us  [cross(): return lax.ppermute(x, DEVICES, pairs)]
    ppermute x6 -> x7, starting transfers between devices: 8.81 us -> 13.1 us  [cross(): return lax.ppermute(x, DEVICES, pairs)]
    ppermute x3, waiting for transfers between devices: 3.35 us -> 1.79 us  [up_z(): return lax.ppermute(x, 'z', [(i, (i + by) % 4) for i in range(4)])]
    pallas_call x4, Pallas kernels: 33 us -> 31.9 us  [terms(): pl.pallas_call(functools.partial(terms_kernel, [len(t) for t in tiles], n...]
    ppermute x5 -> x6, starting transfers between devices: 0.59 us -> 1.53 us  [swap(): return lax.ppermute(x, 'c', [(0, 1), (1, 0)])]
    unnamed x17 -> x29, local copies, waits for them, and re-layouts: 2.86 us -> 3.78 us
    ppermute x3, starting transfers between devices: 4.09 us -> 4.97 us  [up_z(): return lax.ppermute(x, 'z', [(i, (i + by) % 4) for i in range(4)])]
  transfers between devices with their start and end apart: 14 -> 16, of which waited for: 9 -> 7; matrix products, arithmetic and copies ran while one was open for 1% -> 1% of each run, Pallas kernels for 30% -> 30%
where the time goes in v3:
time: 81.3 us; the launch traced here: 81 us
  Pallas kernels  34.2 us (42%)
  starting transfers between devices  19.6 us (24%)
  blocking collectives  12.2 us (15%)
  waiting for transfers between devices  10.2 us (13%)
  local copies, waits for them, and re-layouts  3.87 us (5%)
    pallas_call x4, Pallas kernels, terms(): pl.pallas_call(functools.partial(terms_kernel, [len(t) for t in tiles], n...  31.9 us
    ppermute x7, starting transfers between devices, cross(): return lax.ppermute(x, DEVICES, pairs)  13.1 us
    all_to_all x1, blocking collectives, body(): parts = lax.all_to_all(mine, CHIPS, 0, 0, tiled=True)  12.2 us
    ppermute x7, waiting for transfers between devices, cross(): return lax.ppermute(x, DEVICES, pairs)  7.48 us
    ppermute x3, starting transfers between devices, up_z(): return lax.ppermute(x, 'z', [(i, (i + by) % 4) for i in range(4)])  4.97 us
    unnamed x29, local copies, waits for them, and re-layouts  3.78 us
    pallas_call x1, Pallas kernels, normalized(): pl.pallas_call(unit_kernel, out_shape=[jax.ShapeDtypeStruct(s, jnp.bfloat...  2.24 us
    ppermute x3, waiting for transfers between devices, up_z(): return lax.ppermute(x, 'z', [(i, (i + by) % 4) for i in range(4)])  1.79 us
  transfers between devices with their start and end apart: 16, of which 7 were waited for; matrix products, arithmetic and copies ran while one was open for 1% of the time, Pallas kernels for 30%

profile of v3, /device:TPU:0, one launch (start us, length us, event | category | flops | bytes accessed | tf_op | source)
XLA Modules:
  0.0 81.0 jit_solution(1281328999225049892)
XLA Ops:
  0.0 2.2 %shard_map.82 = (bf16[272,512]{1,0:T(8,128)(2,1)}, bf16[512,512]{1,0:T(8,128)(2,1)}) custom-call(bf16[256,512]{1,0:T(8,128)(2,1)} %e_ref.1, bf16[512,512]{1,0:T(8,128)(2,1)} %c_ref.1, s32[1,256]{1,0:T(1,128)} %bitcast.5), custom_call_target="tpu_custom_call" | custom-call | tf_op jit(solution)/shard_map/pallas_call | solution.py:45
  2.2 2.0 %collective-permute-start.1 = (bf16[512,512]{1,0:T(8,128)(2,1)}, bf16[512,512]{1,0:T(8,128)(2,1)S(1)}, u32[]{:S(2)}, u32[]{:S(2)}) collective-permute-start(bf16[512,512]{1,0:T(8,128)(2,1)} %get-tuple-element.22.refs_2_.refs_5_.refs_3_), channel_id=1, source_target_pairs={{0,8},{8,16},{16,24},{24,0},{1,9},{9,17},{17,25},{25,1},{2,10},{10... | collective-permute-start | bytes 1572872 | tf_op jit(solution)/shard_map/ppermute | solution.py:218
  4.2 2.1 %collective-permute-start.2 = (bf16[512,512]{1,0:T(8,128)(2,1)}, bf16[512,512]{1,0:T(8,128)(2,1)S(1)}, u32[]{:S(2)}, u32[]{:S(2)}) collective-permute-start(bf16[512,512]{1,0:T(8,128)(2,1)} %get-tuple-element.22.refs_2_.refs_5_.refs_3_), channel_id=1, source_target_pairs={{0,24},{8,0},{16,8},{24,16},{1,25},{9,1},{17,9},{25,17},{2,26},{10... | collective-permute-start | bytes 1572872 | tf_op jit(solution)/shard_map/ppermute | solution.py:218
  6.4 0.0 copy-start.10
  6.4 0.0 copy-start.11
  6.4 0.0 copy-start.12
  6.4 0.0 copy-start.9
  6.4 0.0 copy-start.8
  6.4 3.3 %collective-permute-start = (bf16[272,512]{1,0:T(8,128)(2,1)}, bf16[272,512]{1,0:T(8,128)(2,1)S(1)}, u32[]{:S(2)}, u32[]{:S(2)}) collective-permute-start(bf16[272,512]{1,0:T(8,128)(2,1)} %get-tuple-element.21), channel_id=1, source_target_pairs={{0,2},{1,65},{4,6},{5,69},{2,0},{3,67},{6,4},{7,71},{32,34},{33,97... | collective-permute-start | bytes 835592 | tf_op jit(solution)/shard_map/ppermute | solution.py:206
  9.7 0.7 collective-permute-start.3
  10.3 2.6 %collective-permute-start.4 = (bf16[272,512]{1,0:T(8,128)(2,1)}, bf16[272,512]{1,0:T(8,128)(2,1)S(1)}, u32[]{:S(2)}, u32[]{:S(2)}) collective-permute-start(bf16[272,512]{1,0:T(8,128)(2,1)} %get-tuple-element.21), channel_id=1, source_target_pairs={{0,6},{1,97},{4,0},{5,101},{2,4},{3,99},{6,2},{7,103},{32,38},{33,... | collective-permute-start | bytes 835592 | tf_op jit(solution)/shard_map/ppermute | solution.py:206
  12.9 1.0 %constant_dynamic-update-slice_fusion.3 = bf16[1088,512]{1,0:T(8,128)(2,1)S(1)} fusion(bf16[272,512]{1,0:T(8,128)(2,1)} %get-tuple-element.21), kind=kLoop, calls=%fused_computation.3 | loop fusion | bytes 557056
  13.9 0.8 %collective-permute-done = bf16[272,512]{1,0:T(8,128)(2,1)S(1)} collective-permute-done((bf16[272,512]{1,0:T(8,128)(2,1)}, bf16[272,512]{1,0:T(8,128)(2,1)S(1)}, u32[]{:S(2)}, u32[]{:S(2)}) %collective-permute-start) | collective-permute-done | bytes 278560 | tf_op jit(solution)/shard_map/ppermute | solution.py:206
  14.7 3.0 %collective-permute-done.3 = bf16[272,512]{1,0:T(8,128)(2,1)S(1)} collective-permute-done((bf16[272,512]{1,0:T(8,128)(2,1)}, bf16[272,512]{1,0:T(8,128)(2,1)S(1)}, u32[]{:S(2)}, u32[]{:S(2)}) %collective-permute-start.3) | collective-permute-done | bytes 278560 | tf_op jit(solution)/shard_map/ppermute | solution.py:206
  17.7 0.3 collective-permute-done.4
  18.1 0.4 collective-permute-done.1.refs_3_.refs_6_.refs_4_
  18.5 0.0 collective-permute-done.2.refs_4_.refs_7_.refs_5_
  18.5 0.0 copy-start.6
  18.6 0.0 copy-start
  18.6 0.1 collective-permute-start.5
  18.7 0.6 copy-done.3
  19.3 1.5 %collective-permute-start.6 = (bf16[1088,512]{1,0:T(8,128)(2,1)S(1)}, bf16[1088,512]{1,0:T(8,128)(2,1)S(1)}, u32[]{:S(2)}, u32[]{:S(2)}) collective-permute-start(bf16[1088,512]{1,0:T(8,128)(2,1)S(1)} %constant_dynamic-update-slice_fusion.refs_0_.refs_1_), channel_id=1, source_target_pairs={{0,32},{1,5},{4,36},{5,3},{2,34},{3,7},{6,38},{7,1},{32,64},{33,37... | collective-permute-start | bytes 3342344 | tf_op jit(solution)/shard_map/ppermute | solution.py:206
  20.8 0.0 copy-done.6
  20.8 1.7 %collective-permute-start.7 = (bf16[1088,512]{1,0:T(8,128)(2,1)S(1)}, bf16[1088,512]{1,0:T(8,128)(2,1)S(1)}, u32[]{:S(2)}, u32[]{:S(2)}) collective-permute-start(bf16[1088,512]{1,0:T(8,128)(2,1)S(1)} %constant_dynamic-update-slice_fusion.refs_0_.refs_1_), channel_id=1, source_target_pairs={{0,96},{1,7},{4,100},{5,1},{2,98},{3,5},{6,102},{7,3},{32,0},{33,3... | collective-permute-start | bytes 3342344 | tf_op jit(solution)/shard_map/ppermute | solution.py:206
  22.5 0.0 copy-done.10
  22.5 0.0 copy-done.11
  22.5 0.0 copy-done.12
  22.6 0.9 %collective-permute-start.8 = (bf16[512,512]{1,0:T(8,128)(2,1)}, bf16[512,512]{1,0:T(8,128)(2,1)S(1)}, u32[]{:S(2)}, u32[]{:S(2)}) collective-permute-start(bf16[512,512]{1,0:T(8,128)(2,1)} %copy-done.3), channel_id=1, source_target_pairs={{0,8},{8,16},{16,24},{24,0},{1,9},{9,17},{17,25},{25,1},{2,10},{10... | collective-permute-start | bytes 1572872 | tf_op jit(solution)/shard_map/ppermute | solution.py:218
  23.4 0.0 copy-done.9
  23.4 0.0 copy-done.8
  23.5 0.1 pad_add_fusion.info_ref
  23.5 0.0 collective-permute-done.5.refs_1_.refs_2_
  23.5 0.0 copy-done
  23.5 1.0 %copy-done.2 = bf16[512,512]{1,0:T(8,128)(2,1)S(1)} copy-done((bf16[512,512]{1,0:T(8,128)(2,1)S(1)}, bf16[512,512]{1,0:T(8,128)(2,1)}, u32[]{:S(2)}) %copy-start.2) | copy-done | bytes 524312
  24.6 1.0 %copy-done.4 = bf16[512,512]{1,0:T(8,128)(2,1)S(1)} copy-done((bf16[512,512]{1,0:T(8,128)(2,1)S(1)}, bf16[512,512]{1,0:T(8,128)(2,1)}, u32[]{:S(2)}) %copy-start.4) | copy-done | bytes 524312
  25.6 7.0 %shard_map.83.refs_0_ = f32[32,16,256]{2,1,0:T(8,128)S(1)} custom-call(s32[164]{0:T(256)S(1)} %pad_add_fusion.info_ref, bf16[1088,512]{1,0:T(8,128)(2,1)} %copy-done, bf16[1088,512]{1,0:T(8,128)(2,1)} %collective-permute-done.5.refs_1_.refs_2_, bf16[512,512]{1,0:T(8,128)(2,1)S(1)} %copy-done.2, bf16[512,512]{1,0:T(8,128)(2,1)S(1)} %copy-done.4, ...), custom_call_target="tpu_custom_call" | custom-call | flops 3221225472 | bytes 3670016 | tf_op jit(solution)/shard_map/pallas_call | solution.py:175
  32.6 0.0 copy-start.1
  32.7 0.0 copy-start.5
  32.7 0.0 copy-start.7
  32.7 3.3 %collective-permute-done.6.refs_3_ = bf16[1088,512]{1,0:T(8,128)(2,1)S(1)} collective-permute-done((bf16[1088,512]{1,0:T(8,128)(2,1)S(1)}, bf16[1088,512]{1,0:T(8,128)(2,1)S(1)}, u32[]{:S(2)}, u32[]{:S(2)}) %collective-permute-start.6) | collective-permute-done | bytes 1114144 | tf_op jit(solution)/shard_map/ppermute | solution.py:206
  36.0 1.4 %collective-permute-done.8.refs_8_.refs_6_ = bf16[512,512]{1,0:T(8,128)(2,1)S(1)} collective-permute-done((bf16[512,512]{1,0:T(8,128)(2,1)}, bf16[512,512]{1,0:T(8,128)(2,1)S(1)}, u32[]{:S(2)}, u32[]{:S(2)}) %collective-permute-start.8) | collective-permute-done | bytes 524320 | tf_op jit(solution)/shard_map/ppermute | solution.py:218
  37.4 0.0 collective-permute-done.7.refs_4_
  37.4 0.0 collective-permute-start.11
  37.4 0.5 collective-permute-start.12
  38.0 1.6 %collective-permute-start.9 = (bf16[544,512]{1,0:T(8,128)(2,1)S(1)}, bf16[544,512]{1,0:T(8,128)(2,1)S(1)}, u32[]{:S(2)}, u32[]{:S(2)}) collective-permute-start(bf16[544,512]{1,0:T(8,128)(2,1)S(1)} %slice.12), channel_id=1, source_target_pairs={{0,32},{1,5},{4,36},{5,3},{2,34},{3,7},{6,38},{7,1},{32,64},{33,37... | collective-permute-start | bytes 1671176 | tf_op jit(solution)/shard_map/ppermute | solution.py:206
  39.5 1.7 %collective-permute-start.10 = (bf16[544,512]{1,0:T(8,128)(2,1)S(1)}, bf16[544,512]{1,0:T(8,128)(2,1)S(1)}, u32[]{:S(2)}, u32[]{:S(2)}) collective-permute-start(bf16[544,512]{1,0:T(8,128)(2,1)S(1)} %slice.13), channel_id=1, source_target_pairs={{0,96},{1,7},{4,100},{5,1},{2,98},{3,5},{6,102},{7,3},{32,0},{33,3... | collective-permute-start | bytes 1671176 | tf_op jit(solution)/shard_map/ppermute | solution.py:206
  41.3 0.0 copy-done.1
  41.3 0.0 copy-done.5
  41.3 0.0 copy-done.7
  41.3 9.4 %shard_map.84.refs_0_ = f32[32,16,256]{2,1,0:T(8,128)S(1)} custom-call(s32[164]{0:T(256)S(1)} %pad_add_fusion.info_ref, f32[32,16,256]{2,1,0:T(8,128)S(1)} %shard_map.83.refs_0_, bf16[1088,512]{1,0:T(8,128)(2,1)S(1)} %copy-done.1, bf16[1088,512]{1,0:T(8,128)(2,1)} %collective-permute-done.5.refs_1_.refs_2_, ...), custom_call_target="tpu_custom_call", output_to_operand_aliasing={{}: (1, {})} | custom-call | flops 5368709120 | bytes 6291456 | tf_op jit(solution)/shard_map/pallas_call | solution.py:175
  50.7 0.0 collective-permute-done.9.refs_3_
  50.7 0.0 collective-permute-done.10.refs_4_
  50.7 0.1 collective-permute-start.13
  50.8 0.5 collective-permute-start.14
  51.3 0.0 collective-permute-done.11.refs_1_
  51.3 0.0 collective-permute-done.12.refs_2_
  51.3 7.7 %shard_map.85.refs_0_ = f32[32,16,256]{2,1,0:T(8,128)S(1)} custom-call(s32[164]{0:T(256)S(1)} %pad_add_fusion.info_ref, f32[32,16,256]{2,1,0:T(8,128)S(1)} %shard_map.84.refs_0_, bf16[1088,512]{1,0:T(8,128)(2,1)S(1)} %collective-permute-done.11.refs_1_, bf16[1088,512]{1,0:T(8,128)(2,1)S(1)} %collective-permute-done.12.refs_2_, ...), custom_call_target="tpu_custom_call", output_to_operand_aliasing={{}: (1, {})} | custom-call | flops 4294967296 | bytes 4194304 | tf_op jit(solution)/shard_map/pallas_call | solution.py:175
  59.0 0.0 collective-permute-done.13.refs_1_
  59.0 0.0 collective-permute-done.14.refs_2_
  59.0 7.8 %shard_map.86 = (f32[32,16,256]{2,1,0:T(8,128)S(1)}, f32[16,2,256]{2,1,0:T(2,128)S(1)}, f32[16,2,256]{2,1,0:T(2,128)S(1)}) custom-call(s32[164]{0:T(256)S(1)} %pad_add_fusion.info_ref, f32[32,16,256]{2,1,0:T(8,128)S(1)} %shard_map.85.refs_0_, bf16[544,512]{1,0:T(8,128)(2,1)S(1)} %collective-permute-done.13.refs_1_, ...), custom_call_target="tpu_custom_call", output_to_operand_aliasing={{0}: (1, {})} | custom-call | flops 4294967296 | bytes 4194304 | tf_op jit(solution)/shard_map/pallas_call | solution.py:175
  66.8 0.4 collective-permute-start.15
  67.2 0.9 %collective-permute-done.15 = f32[16,2,256]{2,1,0:T(2,128)S(1)} collective-permute-done((f32[16,2,256]{2,1,0:T(2,128)S(1)}, f32[16,2,256]{2,1,0:T(2,128)S(1)}, u32[]{:S(2)}, u32[]{:S(2)}) %collective-permute-start.15) | collective-permute-done | bytes 32800 | tf_op jit(solution)/shard_map/ppermute | solution.py:214
  68.2 12.2 %all_to_all.5 = f32[16,2,256]{2,1,0:T(2,128)S(1)} all-to-all(f32[16,2,256]{2,1,0:T(2,128)S(1)} %add.104), channel_id=1, replica_groups=mesh['x'=4,'z'=4,'yl'=2,'yh'=2,'c'=2] {'x','yl','yh'}, dimensions={0} | all-to-all | bytes 65536 | tf_op jit(solution)/shard_map/all_to_all | solution.py:277
  80.4 0.6 log_subtract_fusion
  (13 shorter events, 0.3 us)
Async XLA Ops:
  2.2 16.3 %collective-permute-start.1 = (bf16[512,512]{1,0:T(8,128)(2,1)}, bf16[512,512]{1,0:T(8,128)(2,1)S(1)}, u32[]{:S(2)}, u32[]{:S(2)}) collective-permute-start(bf16[512,512]{1,0:T(8,128)(2,1)} %get-tuple-element.22.refs_2_.refs_5_.refs_3_), channel_id=1, source_target_pairs={{0,8},{8,16},{16,24},{24,0},{1,9},{9,17},{17,25},{25,1},{2,10},{10... | collective-permute-start | bytes 1572872 | tf_op jit(solution)/shard_map/ppermute | solution.py:218
  4.2 14.3 %collective-permute-start.2 = (bf16[512,512]{1,0:T(8,128)(2,1)}, bf16[512,512]{1,0:T(8,128)(2,1)S(1)}, u32[]{:S(2)}, u32[]{:S(2)}) collective-permute-start(bf16[512,512]{1,0:T(8,128)(2,1)} %get-tuple-element.22.refs_2_.refs_5_.refs_3_), channel_id=1, source_target_pairs={{0,24},{8,0},{16,8},{24,16},{1,25},{9,1},{17,9},{25,17},{2,26},{10... | collective-permute-start | bytes 1572872 | tf_op jit(solution)/shard_map/ppermute | solution.py:218
  6.4 16.2 %copy-start.10 = (s32[32]{0:T(128)S(1)}, s32[32]{0:T(128)}, u32[]{:S(2)}) copy-start(s32[32]{0:T(128)} %constant.103.clone) | copy-start | bytes 388
  6.4 16.2 %copy-start.11 = (s32[32]{0:T(128)S(1)}, s32[32]{0:T(128)}, u32[]{:S(2)}) copy-start(s32[32]{0:T(128)} %constant.102.clone) | copy-start | bytes 388
  6.4 16.2 %copy-start.12 = (s32[32]{0:T(128)S(1)}, s32[32]{0:T(128)}, u32[]{:S(2)}) copy-start(s32[32]{0:T(128)} %constant.101.clone) | copy-start | bytes 388
  6.4 17.1 %copy-start.9 = (s32[4]{0:T(128)S(1)}, s32[4]{0:T(128)}, u32[]{:S(2)}) copy-start(s32[4]{0:T(128)} %constant.106) | copy-start | bytes 52
  6.4 17.1 %copy-start.8 = (s32[128]{0:T(128)S(1)}, s32[128]{0:T(128)}, u32[]{:S(2)}) copy-start(s32[128]{0:T(128)} %constant.105.clone) | copy-start | bytes 1540
  6.4 8.3 %collective-permute-start = (bf16[272,512]{1,0:T(8,128)(2,1)}, bf16[272,512]{1,0:T(8,128)(2,1)S(1)}, u32[]{:S(2)}, u32[]{:S(2)}) collective-permute-start(bf16[272,512]{1,0:T(8,128)(2,1)} %get-tuple-element.21), channel_id=1, source_target_pairs={{0,2},{1,65},{4,6},{5,69},{2,0},{3,67},{6,4},{7,71},{32,34},{33,97... | collective-permute-start | bytes 835592 | tf_op jit(solution)/shard_map/ppermute | solution.py:206
  9.7 8.1 %collective-permute-start.3 = (bf16[272,512]{1,0:T(8,128)(2,1)}, bf16[272,512]{1,0:T(8,128)(2,1)S(1)}, u32[]{:S(2)}, u32[]{:S(2)}) collective-permute-start(bf16[272,512]{1,0:T(8,128)(2,1)} %get-tuple-element.21), channel_id=1, source_target_pairs={{0,4},{1,33},{4,2},{5,37},{2,6},{3,35},{6,0},{7,39},{32,36},{33,65... | collective-permute-start | bytes 835592 | tf_op jit(solution)/shard_map/ppermute | solution.py:206
  10.3 7.7 %collective-permute-start.4 = (bf16[272,512]{1,0:T(8,128)(2,1)}, bf16[272,512]{1,0:T(8,128)(2,1)S(1)}, u32[]{:S(2)}, u32[]{:S(2)}) collective-permute-start(bf16[272,512]{1,0:T(8,128)(2,1)} %get-tuple-element.21), channel_id=1, source_target_pairs={{0,6},{1,97},{4,0},{5,101},{2,4},{3,99},{6,2},{7,103},{32,38},{33,... | collective-permute-start | bytes 835592 | tf_op jit(solution)/shard_map/ppermute | solution.py:206
  18.5 0.8 copy-start.3
  18.5 2.3 %copy-start.6 = (bf16[512,512]{1,0:T(8,128)(2,1)}, bf16[512,512]{1,0:T(8,128)(2,1)S(1)}, u32[]{:S(2)}) copy-start(bf16[512,512]{1,0:T(8,128)(2,1)S(1)} %collective-permute-done.2.refs_4_.refs_7_.refs_5_) | copy-start | bytes 1572868
  18.6 5.0 %copy-start = (bf16[1088,512]{1,0:T(8,128)(2,1)}, bf16[1088,512]{1,0:T(8,128)(2,1)S(1)}, u32[]{:S(2)}) copy-start(bf16[1088,512]{1,0:T(8,128)(2,1)S(1)} %constant_dynamic-update-slice_fusion.refs_0_.refs_1_) | copy-start | bytes 3342340
  18.6 4.9 %collective-permute-start.5 = (bf16[1088,512]{1,0:T(8,128)(2,1)S(1)}, bf16[1088,512]{1,0:T(8,128)(2,1)}, u32[]{:S(2)}, u32[]{:S(2)}) collective-permute-start(bf16[1088,512]{1,0:T(8,128)(2,1)S(1)} %constant_dynamic-update-slice_fusion.refs_0_.refs_1_), channel_id=1, source_target_pairs={{0,1},{1,0},{2,3},{3,2},{4,5},{5,4},{6,7},{7,6},{8,9},{9,8},{10,11... | collective-permute-start | bytes 3342344 | tf_op jit(solution)/shard_map/ppermute | solution.py:214
  19.3 16.7 %collective-permute-start.6 = (bf16[1088,512]{1,0:T(8,128)(2,1)S(1)}, bf16[1088,512]{1,0:T(8,128)(2,1)S(1)}, u32[]{:S(2)}, u32[]{:S(2)}) collective-permute-start(bf16[1088,512]{1,0:T(8,128)(2,1)S(1)} %constant_dynamic-update-slice_fusion.refs_0_.refs_1_), channel_id=1, source_target_pairs={{0,32},{1,5},{4,36},{5,3},{2,34},{3,7},{6,38},{7,1},{32,64},{33,37... | collective-permute-start | bytes 3342344 | tf_op jit(solution)/shard_map/ppermute | solution.py:206
  20.8 16.6 %collective-permute-start.7 = (bf16[1088,512]{1,0:T(8,128)(2,1)S(1)}, bf16[1088,512]{1,0:T(8,128)(2,1)S(1)}, u32[]{:S(2)}, u32[]{:S(2)}) collective-permute-start(bf16[1088,512]{1,0:T(8,128)(2,1)S(1)} %constant_dynamic-update-slice_fusion.refs_0_.refs_1_), channel_id=1, source_target_pairs={{0,96},{1,7},{4,100},{5,1},{2,98},{3,5},{6,102},{7,3},{32,0},{33,3... | collective-permute-start | bytes 3342344 | tf_op jit(solution)/shard_map/ppermute | solution.py:206
  22.6 14.8 %collective-permute-start.8 = (bf16[512,512]{1,0:T(8,128)(2,1)}, bf16[512,512]{1,0:T(8,128)(2,1)S(1)}, u32[]{:S(2)}, u32[]{:S(2)}) collective-permute-start(bf16[512,512]{1,0:T(8,128)(2,1)} %copy-done.3), channel_id=1, source_target_pairs={{0,8},{8,16},{16,24},{24,0},{1,9},{9,17},{17,25},{25,1},{2,10},{10... | collective-permute-start | bytes 1572872 | tf_op jit(solution)/shard_map/ppermute | solution.py:218
  23.5 1.0 %copy-start.2 = (bf16[512,512]{1,0:T(8,128)(2,1)S(1)}, bf16[512,512]{1,0:T(8,128)(2,1)}, u32[]{:S(2)}) copy-start(bf16[512,512]{1,0:T(8,128)(2,1)} %get-tuple-element.22.refs_2_.refs_5_.refs_3_) | copy-start | bytes 1572868
  24.6 1.0 %copy-start.4 = (bf16[512,512]{1,0:T(8,128)(2,1)S(1)}, bf16[512,512]{1,0:T(8,128)(2,1)}, u32[]{:S(2)}) copy-start(bf16[512,512]{1,0:T(8,128)(2,1)} %copy-done.3) | copy-start | bytes 1572868
  32.6 8.6 %copy-start.1 = (bf16[1088,512]{1,0:T(8,128)(2,1)S(1)}, bf16[1088,512]{1,0:T(8,128)(2,1)}, u32[]{:S(2)}) copy-start(bf16[1088,512]{1,0:T(8,128)(2,1)} %copy-done) | copy-start | bytes 3342340
  32.7 8.6 %copy-start.5 = (bf16[512,512]{1,0:T(8,128)(2,1)S(1)}, bf16[512,512]{1,0:T(8,128)(2,1)}, u32[]{:S(2)}) copy-start(bf16[512,512]{1,0:T(8,128)(2,1)} %copy-done.3) | copy-start | bytes 1572868
  32.7 8.6 %copy-start.7 = (bf16[512,512]{1,0:T(8,128)(2,1)S(1)}, bf16[512,512]{1,0:T(8,128)(2,1)}, u32[]{:S(2)}) copy-start(bf16[512,512]{1,0:T(8,128)(2,1)} %copy-done.6) | copy-start | bytes 1572868
  37.4 14.0 %collective-permute-start.11 = (bf16[1088,512]{1,0:T(8,128)(2,1)S(1)}, bf16[1088,512]{1,0:T(8,128)(2,1)S(1)}, u32[]{:S(2)}, u32[]{:S(2)}) collective-permute-start(bf16[1088,512]{1,0:T(8,128)(2,1)S(1)} %collective-permute-done.6.refs_3_), channel_id=1, source_target_pairs={{0,1},{1,0},{2,3},{3,2},{4,5},{5,4},{6,7},{7,6},{8,9},{9,8},{10,11... | collective-permute-start | bytes 3342344 | tf_op jit(solution)/shard_map/ppermute | solution.py:214
  37.4 14.0 %collective-permute-start.12 = (bf16[1088,512]{1,0:T(8,128)(2,1)S(1)}, bf16[1088,512]{1,0:T(8,128)(2,1)S(1)}, u32[]{:S(2)}, u32[]{:S(2)}) collective-permute-start(bf16[1088,512]{1,0:T(8,128)(2,1)S(1)} %collective-permute-done.7.refs_4_), channel_id=1, source_target_pairs={{0,1},{1,0},{2,3},{3,2},{4,5},{5,4},{6,7},{7,6},{8,9},{9,8},{10,11... | collective-permute-start | bytes 3342344 | tf_op jit(solution)/shard_map/ppermute | solution.py:214
  38.0 12.8 %collective-permute-start.9 = (bf16[544,512]{1,0:T(8,128)(2,1)S(1)}, bf16[544,512]{1,0:T(8,128)(2,1)S(1)}, u32[]{:S(2)}, u32[]{:S(2)}) collective-permute-start(bf16[544,512]{1,0:T(8,128)(2,1)S(1)} %slice.12), channel_id=1, source_target_pairs={{0,32},{1,5},{4,36},{5,3},{2,34},{3,7},{6,38},{7,1},{32,64},{33,37... | collective-permute-start | bytes 1671176 | tf_op jit(solution)/shard_map/ppermute | solution.py:206
  39.5 11.2 %collective-permute-start.10 = (bf16[544,512]{1,0:T(8,128)(2,1)S(1)}, bf16[544,512]{1,0:T(8,128)(2,1)S(1)}, u32[]{:S(2)}, u32[]{:S(2)}) collective-permute-start(bf16[544,512]{1,0:T(8,128)(2,1)S(1)} %slice.13), channel_id=1, source_target_pairs={{0,96},{1,7},{4,100},{5,1},{2,98},{3,5},{6,102},{7,3},{32,0},{33,3... | collective-permute-start | bytes 1671176 | tf_op jit(solution)/shard_map/ppermute | solution.py:206
  50.7 8.3 %collective-permute-start.13 = (bf16[544,512]{1,0:T(8,128)(2,1)S(1)}, bf16[544,512]{1,0:T(8,128)(2,1)S(1)}, u32[]{:S(2)}, u32[]{:S(2)}) collective-permute-start(bf16[544,512]{1,0:T(8,128)(2,1)S(1)} %collective-permute-done.9.refs_3_), channel_id=1, source_target_pairs={{0,1},{1,0},{2,3},{3,2},{4,5},{5,4},{6,7},{7,6},{8,9},{9,8},{10,11... | collective-permute-start | bytes 1671176 | tf_op jit(solution)/shard_map/ppermute | solution.py:214
  50.8 8.2 %collective-permute-start.14 = (bf16[544,512]{1,0:T(8,128)(2,1)S(1)}, bf16[544,512]{1,0:T(8,128)(2,1)S(1)}, u32[]{:S(2)}, u32[]{:S(2)}) collective-permute-start(bf16[544,512]{1,0:T(8,128)(2,1)S(1)} %collective-permute-done.10.refs_4_), channel_id=1, source_target_pairs={{0,1},{1,0},{2,3},{3,2},{4,5},{5,4},{6,7},{7,6},{8,9},{9,8},{10,11... | collective-permute-start | bytes 1671176 | tf_op jit(solution)/shard_map/ppermute | solution.py:214
  66.8 1.3 %collective-permute-start.15 = (f32[16,2,256]{2,1,0:T(2,128)S(1)}, f32[16,2,256]{2,1,0:T(2,128)S(1)}, u32[]{:S(2)}, u32[]{:S(2)}) collective-permute-start(f32[16,2,256]{2,1,0:T(2,128)S(1)} %get-tuple-element.36), channel_id=1, source_target_pairs={{0,1},{1,0},{2,3},{3,2},{4,5},{5,4},{6,7},{7,6},{8,9},{9,8},{10,11... | collective-permute-start | bytes 98312 | tf_op jit(solution)/shard_map/ppermute | solution.py:214

commit v4 on v3

--- a/solution.py
+++ b/solution.py
@@ -10,7 +10,6 @@
 from jax.sharding import PartitionSpec as P
 
 AXES = ("x", "z", "yl", "yh", "c")
-CHIPS = ("x", "yl", "yh")
 DEVICES = ("x", "yl", "yh", "c")
 EPSILON = 1e-06
 LOGIT_SCALE = 30.0
@@ -71,43 +70,34 @@
     return rows
 
 
-def terms_kernel(shares, n_c, n_steps, at_owner, at_step, first, last, info_ref, *refs):
+def terms_kernel(n_e, n_c, n_steps, at_owner, at_step, first, last, info_ref, *refs):
     refs = list(refs)
     if not first:
         refs.pop(0)
-    n_e = len(shares)
-    e_refs = [[refs.pop(0) for _ in range(n)] for n in shares]
+    e_refs = [refs.pop(0) for _ in range(n_e)]
     c_refs = [refs.pop(0) for _ in range(n_c)]
     acc_ref = refs.pop(0)
-    outs = [refs.pop(0) for _ in range(2 * last)]
+    out_ref = refs.pop(0) if last else None
     e_buf, l_buf, c_buf, even, odd, sems = refs
 
-    def part_copies(n, ref, first_row):
-        rows = e_buf.at[pl.ds(pl.multiple_of(n * ROWS, ROWS), ROWS)]
-        labels = ref.at[pl.ds(first_row + ROWS, PITCH - ROWS)]
+    def rows_copies(tile, ref):
+        rows = e_buf.at[pl.ds(pl.multiple_of(tile * WIDE, WIDE), WIDE)]
+        labels = ref.at[pl.ds(WIDE, PITCH - ROWS)]
         return [
-            pltpu.make_async_copy(ref.at[pl.ds(first_row, ROWS)], rows, sems.at[n]),
-            pltpu.make_async_copy(labels, l_buf.at[n], sems.at[PARTS * n_e + n]),
+            pltpu.make_async_copy(ref.at[pl.ds(0, WIDE)], rows, sems.at[tile]),
+            pltpu.make_async_copy(labels, l_buf.at[tile], sems.at[n_e + tile]),
         ]
-
-    def rows_copies(tile):
-        copies = []
-        for i in range(PARTS):
-            each = PARTS // shares[tile]
-            ref = e_refs[tile][i // each]
-            copies += part_copies(tile * PARTS + i, ref, i % each * PITCH)
-        return copies
 
     def class_copy(k, ref):
         here = c_buf.at[pl.ds(pl.multiple_of(k * TILE, TILE), TILE)]
-        return pltpu.make_async_copy(ref, here, sems.at[2 * PARTS * n_e + k])
+        return pltpu.make_async_copy(ref, here, sems.at[2 * n_e + k])
 
     def entry(step, which):
         return info_ref[at_step + 4 * step + which]
 
     starts = [[class_copy(k, ref)] for k, ref in enumerate(c_refs)]
-    starts[1:1] = [rows_copies(0)]
-    starts += [rows_copies(r) for r in range(1, n_e)]
+    starts[1:1] = [rows_copies(0, e_refs[0])]
+    starts += [rows_copies(r, e_refs[r]) for r in range(1, n_e)]
     for copies in starts:
         for copy in copies:
             copy.start()
@@ -118,9 +108,8 @@
     def arrived(step):
         @pl.when(entry(step, 2) == 1)
         def _():
-            for i in range(PARTS):
-                for copy in part_copies(entry(step, 0) * PARTS + i, e_refs[0][0], 0):
-                    copy.wait()
+            for copy in rows_copies(entry(step, 0), e_refs[0]):
+                copy.wait()
 
         @pl.when(entry(step, 3) == 1)
         def _():
@@ -133,7 +122,8 @@
 
     def add(x_ref, step):
         n = entry(step, 0) * PARTS
-        parts = [l_buf[n + i].astype(jnp.float32)[:1].astype(jnp.int32) for i in range(PARTS)]
+        tile = l_buf[entry(step, 0)].astype(jnp.float32)
+        parts = [tile[4 * i : 4 * i + 1].astype(jnp.int32) for i in range(PARTS)]
         lab = jnp.concatenate([h[:, :ROWS] * 256 + h[:, ROWS:] for h in parts], axis=1)
         s, t = add_terms(x_ref, lab - sub - info_ref[entry(step, 1)])
         for i in range(PARTS):
@@ -158,11 +148,12 @@
 
     lax.fori_loop(0, n_steps // 2, two_steps, 0)
 
-    for which, out in enumerate(outs):
-        for g in range(16):
+    if last:
+        core = info_ref[4]
+        for o in range(32):
             for i in range(2):
-                part = acc_ref[2 * g + which, 8 * i : 8 * i + 8, :]
-                out[g, i : i + 1, :] = jnp.sum(part, axis=0, keepdims=True)
+                total = jnp.sum(acc_ref[o, 8 * i : 8 * i + 8, :], axis=0, keepdims=True)
+                out_ref[o + core * (1 - 2 * (o % 2)), i : i + 1, :] = total
 
 
 def terms(acc, tiles, classes, plan, info, at_owner, at_step, last=False):
@@ -171,29 +162,29 @@
     smem = pl.BlockSpec(memory_space=pltpu.SMEM)
     vmem = pl.BlockSpec(memory_space=pltpu.VMEM)
     n_steps = len(steps_of(plan))
-    sums = jax.ShapeDtypeStruct((16, 2, 256), jnp.float32)
+    sums = jax.ShapeDtypeStruct((32, 2, 256), jnp.float32)
     out = pl.pallas_call(
-        functools.partial(terms_kernel, [len(t) for t in tiles], n_c, n_steps, at_owner, at_step, first, last),
-        out_shape=[jax.ShapeDtypeStruct((32, 16, 256), jnp.float32)] + [sums] * (2 * last),
+        functools.partial(terms_kernel, n_e, n_c, n_steps, at_owner, at_step, first, last),
+        out_shape=[jax.ShapeDtypeStruct((32, 16, 256), jnp.float32)] + [sums] * last,
         in_specs=[smem] + [vmem] * (not first) + [pl.BlockSpec(memory_space=pl.ANY)] * (len(rows) + n_c),
-        out_specs=[vmem] * (1 + 2 * last),
+        out_specs=[vmem] * (1 + last),
         scratch_shapes=[
             pltpu.VMEM((n_e * WIDE, 512), jnp.bfloat16),
-            pltpu.VMEM((n_e * PARTS, PITCH - ROWS, 512), jnp.bfloat16),
+            pltpu.VMEM((n_e, PITCH - ROWS, 512), jnp.bfloat16),
             pltpu.VMEM((n_c * TILE, 512), jnp.bfloat16),
             pltpu.VMEM((TILE, WIDE), jnp.float32),
             pltpu.VMEM((TILE, WIDE), jnp.float32),
-            pltpu.SemaphoreType.DMA((2 * PARTS * n_e + n_c,)),
+            pltpu.SemaphoreType.DMA((2 * n_e + n_c,)),
         ],
         input_output_aliases={} if first else {1: 0},
-        compiler_params=pltpu.CompilerParams(vmem_limit_bytes=(52 if first else 24) * MIB),
+        compiler_params=pltpu.CompilerParams(vmem_limit_bytes=24 * MIB),
         cost_estimate=pl.CostEstimate(
             flops=n_steps * 2 * TILE * WIDE * 512,
             bytes_accessed=(2 * n_e + n_c) * TILE * 1024,
             transcendentals=n_steps * TILE * WIDE,
         ),
     )(info, *([] if first else [acc]), *rows, *classes)
-    return out[1:] if last else out[0]
+    return out[-1]
 
 
 def cross(x, way, by):
@@ -229,19 +220,22 @@
     e_far, c_up, c_down, e_up, e_down = lax.optimization_barrier(
         (e_far, c_up, c_down, e_up, e_down)
     )
-    own = jnp.concatenate([e, e_up, e_down, e_far])
+    parts = (e, e_up, e_down, e_far)
+    below = [p[ROWS : ROWS + (PITCH - ROWS) // PARTS] for p in parts]
+    own = jnp.concatenate([p[:ROWS] for p in parts] + below)
     up, down = cross(own, 1, 1), cross(own, 1, -1)
     c_far = up_z(c_up, 1)
     classes = (c, c_up, c_down, c_far)
 
-    kinds = ((0, 0), (0, 1), (1, 0), (-1, 0), (1, 1), (-1, 1), (2, 1), (2, 0))
+    kinds = ((0, 0), (0, 1), (1, 0), (-1, 0), (1, 1), (-1, 1), (2, 0), (2, 1))
     plans = (
         (((0, 1), (0, 1, 2)),),
         (((2, 3), (0, 1, 2, 3)), ((0, 1), (3,))),
         (((0, 1), (0, 1, 2, 3)),),
-        (((0, 1), (0, 1, 2, 3)),),
+        (((0,), (0, 1, 2, 3)),),
+        (((0,), (0, 1, 2, 3)),),
     )
-    firsts = (0, 0, 4, 6)
+    firsts = (0, 0, 4, 6, 7)
     second = jnp.array([d for d, _ in kinds for _ in OFFSETS], jnp.int32)
     first = jnp.array([o for _ in kinds for o in OFFSETS], jnp.int32)
     other = jnp.array([w for _, w in kinds for _ in OFFSETS], jnp.int32)
@@ -253,28 +247,25 @@
     bases = ((((x * 4 + at_z) * 2 + yl) * 2 + yh) * 2 + core) * TILE
     steps = [steps_of(plan) for plan in plans]
     table = jnp.array([n for rows in steps for row in rows for n in row], jnp.int32)
-    info = jnp.concatenate([bases, owners, table])
+    info = jnp.concatenate([bases, core[None], owners, table])
 
     def run(acc, call, rows, n_c=4, last=False):
-        at_step = 4 + len(kinds) * PARTS + sum(4 * len(r) for r in steps[:call])
-        at_owner = 4 + firsts[call] * PARTS
+        at_step = 5 + len(kinds) * PARTS + sum(4 * len(r) for r in steps[:call])
+        at_owner = 5 + firsts[call] * PARTS
         return terms(acc, rows, classes[:n_c], plans[call], info, at_owner, at_step, last)
 
     own_swapped = swap(own)
     acc = run(None, 0, ((own,), (own_swapped,)), 3)
     acc, up = lax.optimization_barrier((acc, up))
-    half = up.shape[0] // 2
-    far_a = cross(up[:half], 1, 1)
+    far = cross(up, 1, 1)
     down, c_far = lax.optimization_barrier((down, c_far))
     classes = (c, c_up, c_down, c_far)
-    far_b = cross(down[half:], 1, -1)
     acc = run(acc, 1, ((own,), (own_swapped,), (up,), (down,)))
-    acc, far_a, far_b = lax.optimization_barrier((acc, far_a, far_b))
     acc = run(acc, 2, ((swap(up),), (swap(down),)))
-    far, far_swapped = (far_a, far_b), (swap(far_a), swap(far_b))
-    mine, others = run(acc, 3, (far_swapped, far), last=True)
-    mine = mine + swap(others)
-    parts = lax.all_to_all(mine, CHIPS, 0, 0, tiled=True)
+    acc, far = lax.optimization_barrier((acc, far))
+    acc = run(acc, 3, ((far,),))
+    sums = run(acc, 4, ((swap(far),),), last=True)
+    parts = lax.all_to_all(sums, DEVICES, 0, 0, tiled=True)
     sums = jnp.sum(parts, axis=0)
     return margin_loss(sums[0], sums[1])
 

time: 81.3 us -> 81 us (level); the launches traced: 81 us -> 79.6 us
  starting transfers between devices: 19.6 us -> 17 us
  local copies, waits for them, and re-layouts: 3.87 us -> 6.24 us
  Pallas kernels: 34.2 us -> 32.9 us
  blocking collectives: 12.2 us -> 13.4 us
  waiting for transfers between devices: 10.2 us -> 9.01 us
    ppermute x7 -> x6, starting transfers between devices: 13.1 us -> 10.9 us  [cross(): return lax.ppermute(x, DEVICES, pairs)]
    slice x2 -> x8, local copies, waits for them, and re-layouts: 0.07 us -> 1.77 us  [the longest x4 1.06 us: body(): own = jnp.concatenate([p[:ROWS] for p in parts] + below)]
    ppermute x7 -> x6, waiting for transfers between devices: 7.48 us -> 6.11 us  [cross(): return lax.ppermute(x, DEVICES, pairs)]
    pallas_call x4 -> x5, Pallas kernels: 31.9 us -> 30.7 us  [terms(): pl.pallas_call(functools.partial(terms_kernel, n_e, n_c, n_steps, at_owne...]
    all_to_all x1, blocking collectives: 12.2 us -> 13.4 us  [body(): parts = lax.all_to_all(sums, DEVICES, 0, 0, tiled=True)]
    ppermute x3, waiting for transfers between devices: 1.79 us -> 2.88 us  [up_z(): return lax.ppermute(x, 'z', [(i, (i + by) % 4) for i in range(4)])]
    ppermute x6 -> x4, waiting for transfers between devices: 0.95 us -> 0.01 us  [swap(): return lax.ppermute(x, 'c', [(0, 1), (1, 0)])]
    unnamed x29 -> x26, local copies, waits for them, and re-layouts: 3.78 us -> 4.05 us
  transfers between devices with their start and end apart: 16 -> 13, of which waited for: 7 -> 6; matrix products, arithmetic and copies ran while one was open for 1% -> 2% of each run, Pallas kernels for 30% -> 33%
where the time goes in v4:
time: 81 us; the launch traced here: 79.6 us
  Pallas kernels  32.9 us (41%)
  starting transfers between devices  17 us (21%)
  blocking collectives  13.4 us (17%)
  waiting for transfers between devices  9.01 us (11%)
  local copies, waits for them, and re-layouts  6.24 us (8%)
    pallas_call x5, Pallas kernels, terms(): pl.pallas_call(functools.partial(terms_kernel, n_e, n_c, n_steps, at_owne...  30.7 us
    all_to_all x1, blocking collectives, body(): parts = lax.all_to_all(sums, DEVICES, 0, 0, tiled=True)  13.4 us
    ppermute x6, starting transfers between devices, cross(): return lax.ppermute(x, DEVICES, pairs)  10.9 us
    ppermute x6, waiting for transfers between devices, cross(): return lax.ppermute(x, DEVICES, pairs)  6.11 us
    ppermute x3, starting transfers between devices, up_z(): return lax.ppermute(x, 'z', [(i, (i + by) % 4) for i in range(4)])  5.27 us
    unnamed x26, local copies, waits for them, and re-layouts  4.05 us
    ppermute x3, waiting for transfers between devices, up_z(): return lax.ppermute(x, 'z', [(i, (i + by) % 4) for i in range(4)])  2.88 us
    pallas_call x1, Pallas kernels, normalized(): pl.pallas_call(unit_kernel, out_shape=[jax.ShapeDtypeStruct(s, jnp.bfloat...  2.2 us
  transfers between devices with their start and end apart: 13, of which 6 were waited for; matrix products, arithmetic and copies ran while one was open for 2% of the time, Pallas kernels for 33%

profile of v4, /device:TPU:0, one launch (start us, length us, event | category | flops | bytes accessed | tf_op | source)
XLA Modules:
  0.0 79.6 jit_solution(16190396413401131529)
XLA Ops:
  0.0 2.2 %shard_map.82 = (bf16[272,512]{1,0:T(8,128)(2,1)}, bf16[512,512]{1,0:T(8,128)(2,1)}) custom-call(bf16[256,512]{1,0:T(8,128)(2,1)} %e_ref.1, bf16[512,512]{1,0:T(8,128)(2,1)} %c_ref.1, s32[1,256]{1,0:T(1,128)} %bitcast.6), custom_call_target="tpu_custom_call" | custom-call | tf_op jit(solution)/shard_map/pallas_call | solution.py:44
  2.2 2.0 %collective-permute-start.1 = (bf16[512,512]{1,0:T(8,128)(2,1)}, bf16[512,512]{1,0:T(8,128)(2,1)S(1)}, u32[]{:S(2)}, u32[]{:S(2)}) collective-permute-start(bf16[512,512]{1,0:T(8,128)(2,1)} %get-tuple-element.20.refs_2_.refs_5_.refs_3_), channel_id=1, source_target_pairs={{0,8},{8,16},{16,24},{24,0},{1,9},{9,17},{17,25},{25,1},{2,10},{10... | collective-permute-start | bytes 1572872 | tf_op jit(solution)/shard_map/ppermute | solution.py:209
  4.2 2.1 %collective-permute-start.2 = (bf16[512,512]{1,0:T(8,128)(2,1)}, bf16[512,512]{1,0:T(8,128)(2,1)S(1)}, u32[]{:S(2)}, u32[]{:S(2)}) collective-permute-start(bf16[512,512]{1,0:T(8,128)(2,1)} %get-tuple-element.20.refs_2_.refs_5_.refs_3_), channel_id=1, source_target_pairs={{0,24},{8,0},{16,8},{24,16},{1,25},{9,1},{17,9},{25,17},{2,26},{10... | collective-permute-start | bytes 1572872 | tf_op jit(solution)/shard_map/ppermute | solution.py:209
  6.3 3.2 %collective-permute-start = (bf16[272,512]{1,0:T(8,128)(2,1)}, bf16[272,512]{1,0:T(8,128)(2,1)S(1)}, u32[]{:S(2)}, u32[]{:S(2)}) collective-permute-start(bf16[272,512]{1,0:T(8,128)(2,1)} %get-tuple-element.19), channel_id=1, source_target_pairs={{0,2},{1,65},{4,6},{5,69},{2,0},{3,67},{6,4},{7,71},{32,34},{33,97... | collective-permute-start | bytes 835592 | tf_op jit(solution)/shard_map/ppermute | solution.py:197
  9.5 0.7 collective-permute-start.3
  10.2 2.6 %collective-permute-start.4 = (bf16[272,512]{1,0:T(8,128)(2,1)}, bf16[272,512]{1,0:T(8,128)(2,1)S(1)}, u32[]{:S(2)}, u32[]{:S(2)}) collective-permute-start(bf16[272,512]{1,0:T(8,128)(2,1)} %get-tuple-element.19), channel_id=1, source_target_pairs={{0,6},{1,97},{4,0},{5,101},{2,4},{3,99},{6,2},{7,103},{32,38},{33,... | collective-permute-start | bytes 835592 | tf_op jit(solution)/shard_map/ppermute | solution.py:197
  12.8 1.0 %slice.30 = bf16[256,512]{1,0:T(8,128)(2,1)S(1)} slice(bf16[272,512]{1,0:T(8,128)(2,1)} %get-tuple-element.19), slice={[0:256], [0:512]} | slice | bytes 524288 | tf_op jit(solution)/shard_map/slice | solution.py:225
  13.8 0.7 slice.34
  14.5 0.1 collective-permute-done
  14.6 3.0 %collective-permute-done.3 = bf16[272,512]{1,0:T(8,128)(2,1)S(1)} collective-permute-done((bf16[272,512]{1,0:T(8,128)(2,1)}, bf16[272,512]{1,0:T(8,128)(2,1)S(1)}, u32[]{:S(2)}, u32[]{:S(2)}) %collective-permute-start.3) | collective-permute-done | bytes 278560 | tf_op jit(solution)/shard_map/ppermute | solution.py:197
  17.6 0.3 collective-permute-done.4
  17.9 0.5 collective-permute-done.1.refs_3_.refs_6_.refs_4_
  18.5 0.0 copy-start.2
  18.5 0.0 collective-permute-done.2.refs_4_.refs_7_.refs_5_
  18.5 0.0 copy-start.5
  18.6 0.7 copy-done.2
  19.2 0.2 copy-done.5
  19.4 0.0 copy-start.9
  19.4 0.0 copy-start.10
  19.4 0.0 copy-start.11
  19.5 0.0 copy-start.8
  19.5 0.0 copy-start.12
  19.5 0.4 concatenate.7.refs_0_.refs_1_
  19.9 0.1 collective-permute-start.5
  20.0 1.6 %collective-permute-start.6 = (bf16[1040,512]{1,0:T(8,128)(2,1)S(1)}, bf16[1040,512]{1,0:T(8,128)(2,1)S(1)}, u32[]{:S(2)}, u32[]{:S(2)}) collective-permute-start(bf16[1040,512]{1,0:T(8,128)(2,1)S(1)} %concatenate.7.refs_0_.refs_1_), channel_id=1, source_target_pairs={{0,32},{1,5},{4,36},{5,3},{2,34},{3,7},{6,38},{7,1},{32,64},{33,37... | collective-permute-start | bytes 3194888 | tf_op jit(solution)/shard_map/ppermute | solution.py:197
  21.5 1.7 %collective-permute-start.7 = (bf16[1040,512]{1,0:T(8,128)(2,1)S(1)}, bf16[1040,512]{1,0:T(8,128)(2,1)}, u32[]{:S(2)}, u32[]{:S(2)}) collective-permute-start(bf16[1040,512]{1,0:T(8,128)(2,1)S(1)} %concatenate.7.refs_0_.refs_1_), channel_id=1, source_target_pairs={{0,96},{1,7},{4,100},{5,1},{2,98},{3,5},{6,102},{7,3},{32,0},{33,3... | collective-permute-start | bytes 3194888 | tf_op jit(solution)/shard_map/ppermute | solution.py:197
  23.3 0.0 copy-done.9
  23.3 0.0 copy-done.10
  23.3 0.0 copy-done.11
  23.3 1.1 %collective-permute-start.8 = (bf16[512,512]{1,0:T(8,128)(2,1)}, bf16[512,512]{1,0:T(8,128)(2,1)S(1)}, u32[]{:S(2)}, u32[]{:S(2)}) collective-permute-start(bf16[512,512]{1,0:T(8,128)(2,1)} %copy-done.2), channel_id=1, source_target_pairs={{0,8},{8,16},{16,24},{24,0},{1,9},{9,17},{17,25},{25,1},{2,10},{10... | collective-permute-start | bytes 1572872 | tf_op jit(solution)/shard_map/ppermute | solution.py:209
  24.5 0.0 copy-done.8
  24.5 0.0 copy-done.12
  24.5 0.1 pad_add_fusion.info_ref
  24.6 0.0 collective-permute-done.5.refs_1_.refs_2_
  24.6 0.0 copy-start
  24.6 1.0 %copy-done = bf16[512,512]{1,0:T(8,128)(2,1)S(1)} copy-done((bf16[512,512]{1,0:T(8,128)(2,1)S(1)}, bf16[512,512]{1,0:T(8,128)(2,1)}, u32[]{:S(2)}) %copy-start) | copy-done | bytes 524312
  25.6 0.0 copy-start.3
  25.6 1.0 %copy-done.3 = bf16[512,512]{1,0:T(8,128)(2,1)S(1)} copy-done((bf16[512,512]{1,0:T(8,128)(2,1)S(1)}, bf16[512,512]{1,0:T(8,128)(2,1)}, u32[]{:S(2)}) %copy-start.3) | copy-done | bytes 524312
  26.7 0.0 copy-start.6
  26.7 1.0 %copy-done.6 = bf16[512,512]{1,0:T(8,128)(2,1)S(1)} copy-done((bf16[512,512]{1,0:T(8,128)(2,1)S(1)}, bf16[512,512]{1,0:T(8,128)(2,1)}, u32[]{:S(2)}) %copy-start.6) | copy-done | bytes 524312
  27.7 0.0 copy-start.4
  27.7 0.0 copy-start.7
  27.7 5.9 %shard_map.83.refs_0_ = f32[32,16,256]{2,1,0:T(8,128)S(1)} custom-call(s32[165]{0:T(256)S(1)} %pad_add_fusion.info_ref, bf16[1040,512]{1,0:T(8,128)(2,1)S(1)} %concatenate.7.refs_0_.refs_1_, bf16[1040,512]{1,0:T(8,128)(2,1)S(1)} %collective-permute-done.5.refs_1_.refs_2_, bf16[512,512]{1,0:T(8,128)(2,1)S(1)} %copy-done, bf16[512,512]{1,0:T(8,128)(2,1)S(1)} %copy-done.3, ...), custom_call_target="tpu_custom_call" | custom-call | flops 3221225472 | bytes 3670016 | tf_op jit(solution)/shard_map/pallas_call | solution.py:166
  33.6 2.7 %collective-permute-done.6.refs_3_ = bf16[1040,512]{1,0:T(8,128)(2,1)S(1)} collective-permute-done((bf16[1040,512]{1,0:T(8,128)(2,1)S(1)}, bf16[1040,512]{1,0:T(8,128)(2,1)S(1)}, u32[]{:S(2)}, u32[]{:S(2)}) %collective-permute-start.6) | collective-permute-done | bytes 1064992 | tf_op jit(solution)/shard_map/ppermute | solution.py:197
  36.2 2.3 %collective-permute-done.8.refs_8_.refs_6_.refs_5_ = bf16[512,512]{1,0:T(8,128)(2,1)S(1)} collective-permute-done((bf16[512,512]{1,0:T(8,128)(2,1)}, bf16[512,512]{1,0:T(8,128)(2,1)S(1)}, u32[]{:S(2)}, u32[]{:S(2)}) %collective-permute-start.8) | collective-permute-done | bytes 524320 | tf_op jit(solution)/shard_map/ppermute | solution.py:209
  38.6 0.0 collective-permute-done.7.refs_4_
  38.6 0.0 collective-permute-start.9
  38.6 0.5 collective-permute-start.10
  39.1 1.2 %collective-permute-start.11 = (bf16[1040,512]{1,0:T(8,128)(2,1)S(1)}, bf16[1040,512]{1,0:T(8,128)(2,1)S(1)}, u32[]{:S(2)}, u32[]{:S(2)}) collective-permute-start(bf16[1040,512]{1,0:T(8,128)(2,1)S(1)} %collective-permute-done.6.refs_3_), channel_id=1, source_target_pairs={{0,32},{1,5},{4,36},{5,3},{2,34},{3,7},{6,38},{7,1},{32,64},{33,37... | collective-permute-start | bytes 3194888 | tf_op jit(solution)/shard_map/ppermute | solution.py:197
  40.3 0.0 copy-done.4
  40.3 0.0 copy-done.7
  40.3 8.8 %shard_map.84.refs_0_ = f32[32,16,256]{2,1,0:T(8,128)S(1)} custom-call(s32[165]{0:T(256)S(1)} %pad_add_fusion.info_ref, f32[32,16,256]{2,1,0:T(8,128)S(1)} %shard_map.83.refs_0_, bf16[1040,512]{1,0:T(8,128)(2,1)S(1)} %concatenate.7.refs_0_.refs_1_, bf16[1040,512]{1,0:T(8,128)(2,1)S(1)} %collective-permute-done.5.refs_1_.refs_2_, ...), custom_call_target="tpu_custom_call", output_to_operand_aliasing={{}: (1, {})} | custom-call | flops 5368709120 | bytes 6291456 | tf_op jit(solution)/shard_map/pallas_call | solution.py:166
  49.0 0.0 copy-start.1
  49.0 0.0 collective-permute-done.9.refs_1_
  49.0 0.0 collective-permute-done.10.refs_2_
  49.1 7.3 %shard_map.85.refs_0_ = f32[32,16,256]{2,1,0:T(8,128)S(1)} custom-call(s32[165]{0:T(256)S(1)} %pad_add_fusion.info_ref, f32[32,16,256]{2,1,0:T(8,128)S(1)} %shard_map.84.refs_0_, bf16[1040,512]{1,0:T(8,128)(2,1)S(1)} %collective-permute-done.9.refs_1_, bf16[1040,512]{1,0:T(8,128)(2,1)S(1)} %collective-permute-done.10.refs_2_, ...), custom_call_target="tpu_custom_call", output_to_operand_aliasing={{}: (1, {})} | custom-call | flops 4294967296 | bytes 4194304 | tf_op jit(solution)/shard_map/pallas_call | solution.py:166
  56.3 0.0 collective-permute-done.11.refs_1_
  56.3 0.3 collective-permute-start.12
  56.6 0.0 copy-done.1
  56.6 4.4 %shard_map.86.refs_0_ = f32[32,16,256]{2,1,0:T(8,128)S(1)} custom-call(s32[165]{0:T(256)S(1)} %pad_add_fusion.info_ref, f32[32,16,256]{2,1,0:T(8,128)S(1)} %shard_map.85.refs_0_, bf16[1040,512]{1,0:T(8,128)(2,1)S(1)} %collective-permute-done.11.refs_1_, bf16[512,512]{1,0:T(8,128)(2,1)S(1)} %copy-done.1, ...), custom_call_target="tpu_custom_call", output_to_operand_aliasing={{}: (1, {})} | custom-call | flops 2147483648 | bytes 3145728 | tf_op jit(solution)/shard_map/pallas_call | solution.py:166
  61.0 0.0 collective-permute-done.12.refs_1_
  61.0 4.5 %shard_map.87 = (f32[32,16,256]{2,1,0:T(8,128)S(1)}, f32[32,2,256]{2,1,0:T(2,128)S(1)}) custom-call(s32[165]{0:T(256)S(1)} %pad_add_fusion.info_ref, f32[32,16,256]{2,1,0:T(8,128)S(1)} %shard_map.86.refs_0_, bf16[1040,512]{1,0:T(8,128)(2,1)S(1)} %collective-permute-done.12.refs_1_, bf16[512,512]{1,0:T(8,128)(2,1)S(1)} %copy-done.1, ...), custom_call_target="tpu_custom_call", output_to_operand_aliasing={{0}: (1, {})} | custom-call | flops 2147483648 | bytes 3145728 | tf_op jit(solution)/shard_map/pallas_call | solution.py:166
  65.5 13.4 %all_to_all.5 = f32[32,2,256]{2,1,0:T(2,128)S(1)} all-to-all(f32[32,2,256]{2,1,0:T(2,128)S(1)} %get-tuple-element.32), channel_id=1, replica_groups=mesh['x'=4,'z'=4,'yl'=2,'yh'=2,'c'=2] {'x','yl','yh','c'}, dimensions={0} | all-to-all | bytes 131072 | tf_op jit(solution)/shard_map/all_to_all | solution.py:268
  79.0 0.6 log_subtract_fusion
  (10 shorter events, 0.2 us)
Async XLA Ops:
  2.2 16.3 %collective-permute-start.1 = (bf16[512,512]{1,0:T(8,128)(2,1)}, bf16[512,512]{1,0:T(8,128)(2,1)S(1)}, u32[]{:S(2)}, u32[]{:S(2)}) collective-permute-start(bf16[512,512]{1,0:T(8,128)(2,1)} %get-tuple-element.20.refs_2_.refs_5_.refs_3_), channel_id=1, source_target_pairs={{0,8},{8,16},{16,24},{24,0},{1,9},{9,17},{17,25},{25,1},{2,10},{10... | collective-permute-start | bytes 1572872 | tf_op jit(solution)/shard_map/ppermute | solution.py:209
  4.2 14.3 %collective-permute-start.2 = (bf16[512,512]{1,0:T(8,128)(2,1)}, bf16[512,512]{1,0:T(8,128)(2,1)S(1)}, u32[]{:S(2)}, u32[]{:S(2)}) collective-permute-start(bf16[512,512]{1,0:T(8,128)(2,1)} %get-tuple-element.20.refs_2_.refs_5_.refs_3_), channel_id=1, source_target_pairs={{0,24},{8,0},{16,8},{24,16},{1,25},{9,1},{17,9},{25,17},{2,26},{10... | collective-permute-start | bytes 1572872 | tf_op jit(solution)/shard_map/ppermute | solution.py:209
  6.3 8.3 %collective-permute-start = (bf16[272,512]{1,0:T(8,128)(2,1)}, bf16[272,512]{1,0:T(8,128)(2,1)S(1)}, u32[]{:S(2)}, u32[]{:S(2)}) collective-permute-start(bf16[272,512]{1,0:T(8,128)(2,1)} %get-tuple-element.19), channel_id=1, source_target_pairs={{0,2},{1,65},{4,6},{5,69},{2,0},{3,67},{6,4},{7,71},{32,34},{33,97... | collective-permute-start | bytes 835592 | tf_op jit(solution)/shard_map/ppermute | solution.py:197
  9.5 8.1 %collective-permute-start.3 = (bf16[272,512]{1,0:T(8,128)(2,1)}, bf16[272,512]{1,0:T(8,128)(2,1)S(1)}, u32[]{:S(2)}, u32[]{:S(2)}) collective-permute-start(bf16[272,512]{1,0:T(8,128)(2,1)} %get-tuple-element.19), channel_id=1, source_target_pairs={{0,4},{1,33},{4,2},{5,37},{2,6},{3,35},{6,0},{7,39},{32,36},{33,65... | collective-permute-start | bytes 835592 | tf_op jit(solution)/shard_map/ppermute | solution.py:197
  10.2 7.7 %collective-permute-start.4 = (bf16[272,512]{1,0:T(8,128)(2,1)}, bf16[272,512]{1,0:T(8,128)(2,1)S(1)}, u32[]{:S(2)}, u32[]{:S(2)}) collective-permute-start(bf16[272,512]{1,0:T(8,128)(2,1)} %get-tuple-element.19), channel_id=1, source_target_pairs={{0,6},{1,97},{4,0},{5,101},{2,4},{3,99},{6,2},{7,103},{32,38},{33,... | collective-permute-start | bytes 835592 | tf_op jit(solution)/shard_map/ppermute | solution.py:197
  18.5 0.8 copy-start.2
  18.5 1.0 %copy-start.5 = (bf16[512,512]{1,0:T(8,128)(2,1)}, bf16[512,512]{1,0:T(8,128)(2,1)S(1)}, u32[]{:S(2)}) copy-start(bf16[512,512]{1,0:T(8,128)(2,1)S(1)} %collective-permute-done.2.refs_4_.refs_7_.refs_5_) | copy-start | bytes 1572868
  19.4 3.9 %copy-start.9 = (s32[32]{0:T(128)S(1)}, s32[32]{0:T(128)}, u32[]{:S(2)}) copy-start(s32[32]{0:T(128)} %constant.103.clone) | copy-start | bytes 388
  19.4 3.9 %copy-start.10 = (s32[32]{0:T(128)S(1)}, s32[32]{0:T(128)}, u32[]{:S(2)}) copy-start(s32[32]{0:T(128)} %constant.102.clone) | copy-start | bytes 388
  19.4 3.9 %copy-start.11 = (s32[32]{0:T(128)S(1)}, s32[32]{0:T(128)}, u32[]{:S(2)}) copy-start(s32[32]{0:T(128)} %constant.101.clone) | copy-start | bytes 388
  19.5 5.0 %copy-start.8 = (s32[4]{0:T(128)S(1)}, s32[4]{0:T(128)}, u32[]{:S(2)}) copy-start(s32[4]{0:T(128)} %constant.106) | copy-start | bytes 52
  19.5 5.0 %copy-start.12 = (s32[128]{0:T(128)S(1)}, s32[128]{0:T(128)}, u32[]{:S(2)}) copy-start(s32[128]{0:T(128)} %constant.105.clone) | copy-start | bytes 1540
  19.9 4.7 %collective-permute-start.5 = (bf16[1040,512]{1,0:T(8,128)(2,1)S(1)}, bf16[1040,512]{1,0:T(8,128)(2,1)S(1)}, u32[]{:S(2)}, u32[]{:S(2)}) collective-permute-start(bf16[1040,512]{1,0:T(8,128)(2,1)S(1)} %concatenate.7.refs_0_.refs_1_), channel_id=1, source_target_pairs={{0,1},{1,0},{2,3},{3,2},{4,5},{5,4},{6,7},{7,6},{8,9},{9,8},{10,11... | collective-permute-start | bytes 3194888 | tf_op jit(solution)/shard_map/ppermute | solution.py:205
  20.0 16.3 %collective-permute-start.6 = (bf16[1040,512]{1,0:T(8,128)(2,1)S(1)}, bf16[1040,512]{1,0:T(8,128)(2,1)S(1)}, u32[]{:S(2)}, u32[]{:S(2)}) collective-permute-start(bf16[1040,512]{1,0:T(8,128)(2,1)S(1)} %concatenate.7.refs_0_.refs_1_), channel_id=1, source_target_pairs={{0,32},{1,5},{4,36},{5,3},{2,34},{3,7},{6,38},{7,1},{32,64},{33,37... | collective-permute-start | bytes 3194888 | tf_op jit(solution)/shard_map/ppermute | solution.py:197
  21.5 17.0 %collective-permute-start.7 = (bf16[1040,512]{1,0:T(8,128)(2,1)S(1)}, bf16[1040,512]{1,0:T(8,128)(2,1)}, u32[]{:S(2)}, u32[]{:S(2)}) collective-permute-start(bf16[1040,512]{1,0:T(8,128)(2,1)S(1)} %concatenate.7.refs_0_.refs_1_), channel_id=1, source_target_pairs={{0,96},{1,7},{4,100},{5,1},{2,98},{3,5},{6,102},{7,3},{32,0},{33,3... | collective-permute-start | bytes 3194888 | tf_op jit(solution)/shard_map/ppermute | solution.py:197
  23.3 15.2 %collective-permute-start.8 = (bf16[512,512]{1,0:T(8,128)(2,1)}, bf16[512,512]{1,0:T(8,128)(2,1)S(1)}, u32[]{:S(2)}, u32[]{:S(2)}) collective-permute-start(bf16[512,512]{1,0:T(8,128)(2,1)} %copy-done.2), channel_id=1, source_target_pairs={{0,8},{8,16},{16,24},{24,0},{1,9},{9,17},{17,25},{25,1},{2,10},{10... | collective-permute-start | bytes 1572872 | tf_op jit(solution)/shard_map/ppermute | solution.py:209
  24.6 1.0 %copy-start = (bf16[512,512]{1,0:T(8,128)(2,1)S(1)}, bf16[512,512]{1,0:T(8,128)(2,1)}, u32[]{:S(2)}) copy-start(bf16[512,512]{1,0:T(8,128)(2,1)} %get-tuple-element.20.refs_2_.refs_5_.refs_3_) | copy-start | bytes 1572868
  25.6 1.0 %copy-start.3 = (bf16[512,512]{1,0:T(8,128)(2,1)S(1)}, bf16[512,512]{1,0:T(8,128)(2,1)}, u32[]{:S(2)}) copy-start(bf16[512,512]{1,0:T(8,128)(2,1)} %copy-done.2) | copy-start | bytes 1572868
  26.7 1.0 %copy-start.6 = (bf16[512,512]{1,0:T(8,128)(2,1)S(1)}, bf16[512,512]{1,0:T(8,128)(2,1)}, u32[]{:S(2)}) copy-start(bf16[512,512]{1,0:T(8,128)(2,1)} %copy-done.5) | copy-start | bytes 1572868
  27.7 12.5 %copy-start.4 = (bf16[512,512]{1,0:T(8,128)(2,1)S(1)}, bf16[512,512]{1,0:T(8,128)(2,1)}, u32[]{:S(2)}) copy-start(bf16[512,512]{1,0:T(8,128)(2,1)} %copy-done.2) | copy-start | bytes 1572868
  27.7 12.5 %copy-start.7 = (bf16[512,512]{1,0:T(8,128)(2,1)S(1)}, bf16[512,512]{1,0:T(8,128)(2,1)}, u32[]{:S(2)}) copy-start(bf16[512,512]{1,0:T(8,128)(2,1)} %copy-done.5) | copy-start | bytes 1572868
  38.6 10.5 %collective-permute-start.9 = (bf16[1040,512]{1,0:T(8,128)(2,1)S(1)}, bf16[1040,512]{1,0:T(8,128)(2,1)S(1)}, u32[]{:S(2)}, u32[]{:S(2)}) collective-permute-start(bf16[1040,512]{1,0:T(8,128)(2,1)S(1)} %collective-permute-done.6.refs_3_), channel_id=1, source_target_pairs={{0,1},{1,0},{2,3},{3,2},{4,5},{5,4},{6,7},{7,6},{8,9},{9,8},{10,11... | collective-permute-start | bytes 3194888 | tf_op jit(solution)/shard_map/ppermute | solution.py:205
  38.6 10.5 %collective-permute-start.10 = (bf16[1040,512]{1,0:T(8,128)(2,1)}, bf16[1040,512]{1,0:T(8,128)(2,1)S(1)}, u32[]{:S(2)}, u32[]{:S(2)}) collective-permute-start(bf16[1040,512]{1,0:T(8,128)(2,1)} %collective-permute-done.7.refs_4_), channel_id=1, source_target_pairs={{0,1},{1,0},{2,3},{3,2},{4,5},{5,4},{6,7},{7,6},{8,9},{9,8},{10,11... | collective-permute-start | bytes 3194888 | tf_op jit(solution)/shard_map/ppermute | solution.py:205
  39.1 17.2 %collective-permute-start.11 = (bf16[1040,512]{1,0:T(8,128)(2,1)S(1)}, bf16[1040,512]{1,0:T(8,128)(2,1)S(1)}, u32[]{:S(2)}, u32[]{:S(2)}) collective-permute-start(bf16[1040,512]{1,0:T(8,128)(2,1)S(1)} %collective-permute-done.6.refs_3_), channel_id=1, source_target_pairs={{0,32},{1,5},{4,36},{5,3},{2,34},{3,7},{6,38},{7,1},{32,64},{33,37... | collective-permute-start | bytes 3194888 | tf_op jit(solution)/shard_map/ppermute | solution.py:197
  49.0 7.6 %copy-start.1 = (bf16[512,512]{1,0:T(8,128)(2,1)S(1)}, bf16[512,512]{1,0:T(8,128)(2,1)}, u32[]{:S(2)}) copy-start(bf16[512,512]{1,0:T(8,128)(2,1)} %get-tuple-element.20.refs_2_.refs_5_.refs_3_) | copy-start | bytes 1572868
  56.3 4.7 %collective-permute-start.12 = (bf16[1040,512]{1,0:T(8,128)(2,1)S(1)}, bf16[1040,512]{1,0:T(8,128)(2,1)S(1)}, u32[]{:S(2)}, u32[]{:S(2)}) collective-permute-start(bf16[1040,512]{1,0:T(8,128)(2,1)S(1)} %collective-permute-done.11.refs_1_), channel_id=1, source_target_pairs={{0,1},{1,0},{2,3},{3,2},{4,5},{5,4},{6,7},{7,6},{8,9},{9,8},{10,11... | collective-permute-start | bytes 3194888 | tf_op jit(solution)/shard_map/ppermute | solution.py:205

commit v5 on v4

--- a/solution.py
+++ b/solution.py
@@ -256,9 +256,8 @@
 
     own_swapped = swap(own)
     acc = run(None, 0, ((own,), (own_swapped,)), 3)
-    acc, up = lax.optimization_barrier((acc, up))
+    c_far, acc, up = lax.optimization_barrier((c_far, acc, up))
     far = cross(up, 1, 1)
-    down, c_far = lax.optimization_barrier((down, c_far))
     classes = (c, c_up, c_down, c_far)
     acc = run(acc, 1, ((own,), (own_swapped,), (up,), (down,)))
     acc = run(acc, 2, ((swap(up),), (swap(down),)))

time: 81 us -> 81 us (level)
    ppermute x3, waiting for transfers between devices: 2.88 us -> 5.54 us  [up_z(): return lax.ppermute(x, 'z', [(i, (i + by) % 4) for i in range(4)])]
    ppermute x6, waiting for transfers between devices: 6.11 us -> 3.46 us  [cross(): return lax.ppermute(x, DEVICES, pairs)]
  transfers between devices with their start and end apart: 13 -> 13, of which waited for: 6 -> 5; matrix products, arithmetic and copies ran while one was open for 2% -> 2% of each run, Pallas kernels for 33% -> 33%
where the time goes in v5:
time: 81 us; the launch traced here: 79.6 us
  Pallas kernels  32.9 us (41%)
  starting transfers between devices  17 us (21%)
  blocking collectives  13.4 us (17%)
  waiting for transfers between devices  9.01 us (11%)
  local copies, waits for them, and re-layouts  6.24 us (8%)
    pallas_call x5, Pallas kernels, terms(): pl.pallas_call(functools.partial(terms_kernel, n_e, n_c, n_steps, at_owne...  30.7 us
    all_to_all x1, blocking collectives, body(): parts = lax.all_to_all(sums, DEVICES, 0, 0, tiled=True)  13.4 us
    ppermute x6, starting transfers between devices, cross(): return lax.ppermute(x, DEVICES, pairs)  10.9 us
    ppermute x3, waiting for transfers between devices, up_z(): return lax.ppermute(x, 'z', [(i, (i + by) % 4) for i in range(4)])  5.54 us
    ppermute x3, starting transfers between devices, up_z(): return lax.ppermute(x, 'z', [(i, (i + by) % 4) for i in range(4)])  5.27 us
    unnamed x26, local copies, waits for them, and re-layouts  4.05 us
    ppermute x6, waiting for transfers between devices, cross(): return lax.ppermute(x, DEVICES, pairs)  3.46 us
    pallas_call x1, Pallas kernels, normalized(): pl.pallas_call(unit_kernel, out_shape=[jax.ShapeDtypeStruct(s, jnp.bfloat...  2.2 us
  transfers between devices with their start and end apart: 13, of which 5 were waited for; matrix products, arithmetic and copies ran while one was open for 2% of the time, Pallas kernels for 33%

profile of v5, /device:TPU:0, one launch (start us, length us, event | category | flops | bytes accessed | tf_op | source)
XLA Modules:
  0.0 79.6 jit_solution(8846868434896956532)
XLA Ops:
  0.0 2.2 %shard_map.82 = (bf16[272,512]{1,0:T(8,128)(2,1)}, bf16[512,512]{1,0:T(8,128)(2,1)}) custom-call(bf16[256,512]{1,0:T(8,128)(2,1)} %e_ref.1, bf16[512,512]{1,0:T(8,128)(2,1)} %c_ref.1, s32[1,256]{1,0:T(1,128)} %bitcast.6), custom_call_target="tpu_custom_call" | custom-call | tf_op jit(solution)/shard_map/pallas_call | solution.py:44
  2.2 2.0 %collective-permute-start.1 = (bf16[512,512]{1,0:T(8,128)(2,1)}, bf16[512,512]{1,0:T(8,128)(2,1)S(1)}, u32[]{:S(2)}, u32[]{:S(2)}) collective-permute-start(bf16[512,512]{1,0:T(8,128)(2,1)} %get-tuple-element.19.refs_2_.refs_5_.refs_3_), channel_id=1, source_target_pairs={{0,8},{8,16},{16,24},{24,0},{1,9},{9,17},{17,25},{25,1},{2,10},{10... | collective-permute-start | bytes 1572872 | tf_op jit(solution)/shard_map/ppermute | solution.py:209
  4.2 2.1 %collective-permute-start.2 = (bf16[512,512]{1,0:T(8,128)(2,1)}, bf16[512,512]{1,0:T(8,128)(2,1)S(1)}, u32[]{:S(2)}, u32[]{:S(2)}) collective-permute-start(bf16[512,512]{1,0:T(8,128)(2,1)} %get-tuple-element.19.refs_2_.refs_5_.refs_3_), channel_id=1, source_target_pairs={{0,24},{8,0},{16,8},{24,16},{1,25},{9,1},{17,9},{25,17},{2,26},{10... | collective-permute-start | bytes 1572872 | tf_op jit(solution)/shard_map/ppermute | solution.py:209
  6.3 3.2 %collective-permute-start = (bf16[272,512]{1,0:T(8,128)(2,1)}, bf16[272,512]{1,0:T(8,128)(2,1)S(1)}, u32[]{:S(2)}, u32[]{:S(2)}) collective-permute-start(bf16[272,512]{1,0:T(8,128)(2,1)} %get-tuple-element.18), channel_id=1, source_target_pairs={{0,2},{1,65},{4,6},{5,69},{2,0},{3,67},{6,4},{7,71},{32,34},{33,97... | collective-permute-start | bytes 835592 | tf_op jit(solution)/shard_map/ppermute | solution.py:197
  9.5 0.7 collective-permute-start.3
  10.2 2.6 %collective-permute-start.4 = (bf16[272,512]{1,0:T(8,128)(2,1)}, bf16[272,512]{1,0:T(8,128)(2,1)S(1)}, u32[]{:S(2)}, u32[]{:S(2)}) collective-permute-start(bf16[272,512]{1,0:T(8,128)(2,1)} %get-tuple-element.18), channel_id=1, source_target_pairs={{0,6},{1,97},{4,0},{5,101},{2,4},{3,99},{6,2},{7,103},{32,38},{33,... | collective-permute-start | bytes 835592 | tf_op jit(solution)/shard_map/ppermute | solution.py:197
  12.8 1.0 %slice.30 = bf16[256,512]{1,0:T(8,128)(2,1)S(1)} slice(bf16[272,512]{1,0:T(8,128)(2,1)} %get-tuple-element.18), slice={[0:256], [0:512]} | slice | bytes 524288 | tf_op jit(solution)/shard_map/slice | solution.py:225
  13.8 0.7 slice.34
  14.5 0.1 collective-permute-done
  14.6 3.0 %collective-permute-done.3 = bf16[272,512]{1,0:T(8,128)(2,1)S(1)} collective-permute-done((bf16[272,512]{1,0:T(8,128)(2,1)}, bf16[272,512]{1,0:T(8,128)(2,1)S(1)}, u32[]{:S(2)}, u32[]{:S(2)}) %collective-permute-start.3) | collective-permute-done | bytes 278560 | tf_op jit(solution)/shard_map/ppermute | solution.py:197
  17.6 0.3 collective-permute-done.4
  17.9 0.5 collective-permute-done.1.refs_3_.refs_6_.refs_4_
  18.5 0.0 copy-start.2
  18.5 0.0 collective-permute-done.2.refs_4_.refs_7_.refs_5_
  18.5 0.0 copy-start.5
  18.6 0.7 copy-done.2
  19.2 0.2 copy-done.5
  19.4 0.0 copy-start.9
  19.4 0.0 copy-start.10
  19.4 0.0 copy-start.11
  19.5 0.0 copy-start.8
  19.5 0.0 copy-start.12
  19.5 0.4 concatenate.7.refs_0_.refs_1_
  19.9 0.1 collective-permute-start.6
  20.0 1.6 %collective-permute-start.7 = (bf16[1040,512]{1,0:T(8,128)(2,1)S(1)}, bf16[1040,512]{1,0:T(8,128)(2,1)S(1)}, u32[]{:S(2)}, u32[]{:S(2)}) collective-permute-start(bf16[1040,512]{1,0:T(8,128)(2,1)S(1)} %concatenate.7.refs_0_.refs_1_), channel_id=1, source_target_pairs={{0,32},{1,5},{4,36},{5,3},{2,34},{3,7},{6,38},{7,1},{32,64},{33,37... | collective-permute-start | bytes 3194888 | tf_op jit(solution)/shard_map/ppermute | solution.py:197
  21.5 1.7 %collective-permute-start.8 = (bf16[1040,512]{1,0:T(8,128)(2,1)S(1)}, bf16[1040,512]{1,0:T(8,128)(2,1)}, u32[]{:S(2)}, u32[]{:S(2)}) collective-permute-start(bf16[1040,512]{1,0:T(8,128)(2,1)S(1)} %concatenate.7.refs_0_.refs_1_), channel_id=1, source_target_pairs={{0,96},{1,7},{4,100},{5,1},{2,98},{3,5},{6,102},{7,3},{32,0},{33,3... | collective-permute-start | bytes 3194888 | tf_op jit(solution)/shard_map/ppermute | solution.py:197
  23.3 0.0 copy-done.9
  23.3 0.0 copy-done.10
  23.3 0.0 copy-done.11
  23.3 1.1 %collective-permute-start.5 = (bf16[512,512]{1,0:T(8,128)(2,1)}, bf16[512,512]{1,0:T(8,128)(2,1)S(1)}, u32[]{:S(2)}, u32[]{:S(2)}) collective-permute-start(bf16[512,512]{1,0:T(8,128)(2,1)} %copy-done.2), channel_id=1, source_target_pairs={{0,8},{8,16},{16,24},{24,0},{1,9},{9,17},{17,25},{25,1},{2,10},{10... | collective-permute-start | bytes 1572872 | tf_op jit(solution)/shard_map/ppermute | solution.py:209
  24.5 0.0 copy-done.8
  24.5 0.0 copy-done.12
  24.5 0.1 pad_add_fusion.info_ref
  24.6 0.0 collective-permute-done.6.refs_1_.refs_2_
  24.6 0.0 copy-start
  24.6 1.0 %copy-done = bf16[512,512]{1,0:T(8,128)(2,1)S(1)} copy-done((bf16[512,512]{1,0:T(8,128)(2,1)S(1)}, bf16[512,512]{1,0:T(8,128)(2,1)}, u32[]{:S(2)}) %copy-start) | copy-done | bytes 524312
  25.6 0.0 copy-start.3
  25.6 1.0 %copy-done.3 = bf16[512,512]{1,0:T(8,128)(2,1)S(1)} copy-done((bf16[512,512]{1,0:T(8,128)(2,1)S(1)}, bf16[512,512]{1,0:T(8,128)(2,1)}, u32[]{:S(2)}) %copy-start.3) | copy-done | bytes 524312
  26.7 0.0 copy-start.6
  26.7 1.0 %copy-done.6 = bf16[512,512]{1,0:T(8,128)(2,1)S(1)} copy-done((bf16[512,512]{1,0:T(8,128)(2,1)S(1)}, bf16[512,512]{1,0:T(8,128)(2,1)}, u32[]{:S(2)}) %copy-start.6) | copy-done | bytes 524312
  27.7 0.0 copy-start.4
  27.7 0.0 copy-start.7
  27.7 5.9 %shard_map.83.refs_0_ = f32[32,16,256]{2,1,0:T(8,128)S(1)} custom-call(s32[165]{0:T(256)S(1)} %pad_add_fusion.info_ref, bf16[1040,512]{1,0:T(8,128)(2,1)S(1)} %concatenate.7.refs_0_.refs_1_, bf16[1040,512]{1,0:T(8,128)(2,1)S(1)} %collective-permute-done.6.refs_1_.refs_2_, bf16[512,512]{1,0:T(8,128)(2,1)S(1)} %copy-done, bf16[512,512]{1,0:T(8,128)(2,1)S(1)} %copy-done.3, ...), custom_call_target="tpu_custom_call" | custom-call | flops 3221225472 | bytes 3670016 | tf_op jit(solution)/shard_map/pallas_call | solution.py:166
  33.6 5.0 %collective-permute-done.5.refs_8_.refs_6_.refs_5_ = bf16[512,512]{1,0:T(8,128)(2,1)S(1)} collective-permute-done((bf16[512,512]{1,0:T(8,128)(2,1)}, bf16[512,512]{1,0:T(8,128)(2,1)S(1)}, u32[]{:S(2)}, u32[]{:S(2)}) %collective-permute-start.5) | collective-permute-done | bytes 524320 | tf_op jit(solution)/shard_map/ppermute | solution.py:209
  38.6 0.0 collective-permute-done.7.refs_3_
  38.6 0.0 collective-permute-start.9
  38.6 0.0 collective-permute-done.8.refs_4_
  38.6 0.5 collective-permute-start.10
  39.1 1.2 %collective-permute-start.11 = (bf16[1040,512]{1,0:T(8,128)(2,1)S(1)}, bf16[1040,512]{1,0:T(8,128)(2,1)S(1)}, u32[]{:S(2)}, u32[]{:S(2)}) collective-permute-start(bf16[1040,512]{1,0:T(8,128)(2,1)S(1)} %collective-permute-done.7.refs_3_), channel_id=1, source_target_pairs={{0,32},{1,5},{4,36},{5,3},{2,34},{3,7},{6,38},{7,1},{32,64},{33,37... | collective-permute-start | bytes 3194888 | tf_op jit(solution)/shard_map/ppermute | solution.py:197
  40.3 0.0 copy-done.4
  40.3 0.0 copy-done.7
  40.3 8.8 %shard_map.84.refs_0_ = f32[32,16,256]{2,1,0:T(8,128)S(1)} custom-call(s32[165]{0:T(256)S(1)} %pad_add_fusion.info_ref, f32[32,16,256]{2,1,0:T(8,128)S(1)} %shard_map.83.refs_0_, bf16[1040,512]{1,0:T(8,128)(2,1)S(1)} %concatenate.7.refs_0_.refs_1_, bf16[1040,512]{1,0:T(8,128)(2,1)S(1)} %collective-permute-done.6.refs_1_.refs_2_, ...), custom_call_target="tpu_custom_call", output_to_operand_aliasing={{}: (1, {})} | custom-call | flops 5368709120 | bytes 6291456 | tf_op jit(solution)/shard_map/pallas_call | solution.py:166
  49.0 0.0 copy-start.1
  49.0 0.0 collective-permute-done.9.refs_1_
  49.1 0.0 collective-permute-done.10.refs_2_
  49.1 7.3 %shard_map.85.refs_0_ = f32[32,16,256]{2,1,0:T(8,128)S(1)} custom-call(s32[165]{0:T(256)S(1)} %pad_add_fusion.info_ref, f32[32,16,256]{2,1,0:T(8,128)S(1)} %shard_map.84.refs_0_, bf16[1040,512]{1,0:T(8,128)(2,1)S(1)} %collective-permute-done.9.refs_1_, bf16[1040,512]{1,0:T(8,128)(2,1)S(1)} %collective-permute-done.10.refs_2_, ...), custom_call_target="tpu_custom_call", output_to_operand_aliasing={{}: (1, {})} | custom-call | flops 4294967296 | bytes 4194304 | tf_op jit(solution)/shard_map/pallas_call | solution.py:166
  56.3 0.0 collective-permute-done.11.refs_1_
  56.3 0.3 collective-permute-start.12
  56.6 0.0 copy-done.1
  56.6 4.4 %shard_map.86.refs_0_ = f32[32,16,256]{2,1,0:T(8,128)S(1)} custom-call(s32[165]{0:T(256)S(1)} %pad_add_fusion.info_ref, f32[32,16,256]{2,1,0:T(8,128)S(1)} %shard_map.85.refs_0_, bf16[1040,512]{1,0:T(8,128)(2,1)S(1)} %collective-permute-done.11.refs_1_, bf16[512,512]{1,0:T(8,128)(2,1)S(1)} %copy-done.1, ...), custom_call_target="tpu_custom_call", output_to_operand_aliasing={{}: (1, {})} | custom-call | flops 2147483648 | bytes 3145728 | tf_op jit(solution)/shard_map/pallas_call | solution.py:166
  61.0 0.0 collective-permute-done.12.refs_1_
  61.0 4.5 %shard_map.87 = (f32[32,16,256]{2,1,0:T(8,128)S(1)}, f32[32,2,256]{2,1,0:T(2,128)S(1)}) custom-call(s32[165]{0:T(256)S(1)} %pad_add_fusion.info_ref, f32[32,16,256]{2,1,0:T(8,128)S(1)} %shard_map.86.refs_0_, bf16[1040,512]{1,0:T(8,128)(2,1)S(1)} %collective-permute-done.12.refs_1_, bf16[512,512]{1,0:T(8,128)(2,1)S(1)} %copy-done.1, ...), custom_call_target="tpu_custom_call", output_to_operand_aliasing={{0}: (1, {})} | custom-call | flops 2147483648 | bytes 3145728 | tf_op jit(solution)/shard_map/pallas_call | solution.py:166
  65.5 13.4 %all_to_all.5 = f32[32,2,256]{2,1,0:T(2,128)S(1)} all-to-all(f32[32,2,256]{2,1,0:T(2,128)S(1)} %get-tuple-element.30), channel_id=1, replica_groups=mesh['x'=4,'z'=4,'yl'=2,'yh'=2,'c'=2] {'x','yl','yh','c'}, dimensions={0} | all-to-all | bytes 131072 | tf_op jit(solution)/shard_map/all_to_all | solution.py:267
  79.0 0.6 log_subtract_fusion
  (10 shorter events, 0.2 us)
Async XLA Ops:
  2.2 16.3 %collective-permute-start.1 = (bf16[512,512]{1,0:T(8,128)(2,1)}, bf16[512,512]{1,0:T(8,128)(2,1)S(1)}, u32[]{:S(2)}, u32[]{:S(2)}) collective-permute-start(bf16[512,512]{1,0:T(8,128)(2,1)} %get-tuple-element.19.refs_2_.refs_5_.refs_3_), channel_id=1, source_target_pairs={{0,8},{8,16},{16,24},{24,0},{1,9},{9,17},{17,25},{25,1},{2,10},{10... | collective-permute-start | bytes 1572872 | tf_op jit(solution)/shard_map/ppermute | solution.py:209
  4.2 14.3 %collective-permute-start.2 = (bf16[512,512]{1,0:T(8,128)(2,1)}, bf16[512,512]{1,0:T(8,128)(2,1)S(1)}, u32[]{:S(2)}, u32[]{:S(2)}) collective-permute-start(bf16[512,512]{1,0:T(8,128)(2,1)} %get-tuple-element.19.refs_2_.refs_5_.refs_3_), channel_id=1, source_target_pairs={{0,24},{8,0},{16,8},{24,16},{1,25},{9,1},{17,9},{25,17},{2,26},{10... | collective-permute-start | bytes 1572872 | tf_op jit(solution)/shard_map/ppermute | solution.py:209
  6.3 8.3 %collective-permute-start = (bf16[272,512]{1,0:T(8,128)(2,1)}, bf16[272,512]{1,0:T(8,128)(2,1)S(1)}, u32[]{:S(2)}, u32[]{:S(2)}) collective-permute-start(bf16[272,512]{1,0:T(8,128)(2,1)} %get-tuple-element.18), channel_id=1, source_target_pairs={{0,2},{1,65},{4,6},{5,69},{2,0},{3,67},{6,4},{7,71},{32,34},{33,97... | collective-permute-start | bytes 835592 | tf_op jit(solution)/shard_map/ppermute | solution.py:197
  9.5 8.1 %collective-permute-start.3 = (bf16[272,512]{1,0:T(8,128)(2,1)}, bf16[272,512]{1,0:T(8,128)(2,1)S(1)}, u32[]{:S(2)}, u32[]{:S(2)}) collective-permute-start(bf16[272,512]{1,0:T(8,128)(2,1)} %get-tuple-element.18), channel_id=1, source_target_pairs={{0,4},{1,33},{4,2},{5,37},{2,6},{3,35},{6,0},{7,39},{32,36},{33,65... | collective-permute-start | bytes 835592 | tf_op jit(solution)/shard_map/ppermute | solution.py:197
  10.2 7.7 %collective-permute-start.4 = (bf16[272,512]{1,0:T(8,128)(2,1)}, bf16[272,512]{1,0:T(8,128)(2,1)S(1)}, u32[]{:S(2)}, u32[]{:S(2)}) collective-permute-start(bf16[272,512]{1,0:T(8,128)(2,1)} %get-tuple-element.18), channel_id=1, source_target_pairs={{0,6},{1,97},{4,0},{5,101},{2,4},{3,99},{6,2},{7,103},{32,38},{33,... | collective-permute-start | bytes 835592 | tf_op jit(solution)/shard_map/ppermute | solution.py:197
  18.5 0.8 copy-start.2
  18.5 1.0 %copy-start.5 = (bf16[512,512]{1,0:T(8,128)(2,1)}, bf16[512,512]{1,0:T(8,128)(2,1)S(1)}, u32[]{:S(2)}) copy-start(bf16[512,512]{1,0:T(8,128)(2,1)S(1)} %collective-permute-done.2.refs_4_.refs_7_.refs_5_) | copy-start | bytes 1572868
  19.4 3.9 %copy-start.9 = (s32[32]{0:T(128)S(1)}, s32[32]{0:T(128)}, u32[]{:S(2)}) copy-start(s32[32]{0:T(128)} %constant.101.clone) | copy-start | bytes 388
  19.4 3.9 %copy-start.10 = (s32[32]{0:T(128)S(1)}, s32[32]{0:T(128)}, u32[]{:S(2)}) copy-start(s32[32]{0:T(128)} %constant.102.clone) | copy-start | bytes 388
  19.4 3.9 %copy-start.11 = (s32[32]{0:T(128)S(1)}, s32[32]{0:T(128)}, u32[]{:S(2)}) copy-start(s32[32]{0:T(128)} %constant.103.clone) | copy-start | bytes 388
  19.5 5.0 %copy-start.8 = (s32[4]{0:T(128)S(1)}, s32[4]{0:T(128)}, u32[]{:S(2)}) copy-start(s32[4]{0:T(128)} %constant.106) | copy-start | bytes 52
  19.5 5.0 %copy-start.12 = (s32[128]{0:T(128)S(1)}, s32[128]{0:T(128)}, u32[]{:S(2)}) copy-start(s32[128]{0:T(128)} %constant.105.clone) | copy-start | bytes 1540
  19.9 4.7 %collective-permute-start.6 = (bf16[1040,512]{1,0:T(8,128)(2,1)S(1)}, bf16[1040,512]{1,0:T(8,128)(2,1)S(1)}, u32[]{:S(2)}, u32[]{:S(2)}) collective-permute-start(bf16[1040,512]{1,0:T(8,128)(2,1)S(1)} %concatenate.7.refs_0_.refs_1_), channel_id=1, source_target_pairs={{0,1},{1,0},{2,3},{3,2},{4,5},{5,4},{6,7},{7,6},{8,9},{9,8},{10,11... | collective-permute-start | bytes 3194888 | tf_op jit(solution)/shard_map/ppermute | solution.py:205
  20.0 18.6 %collective-permute-start.7 = (bf16[1040,512]{1,0:T(8,128)(2,1)S(1)}, bf16[1040,512]{1,0:T(8,128)(2,1)S(1)}, u32[]{:S(2)}, u32[]{:S(2)}) collective-permute-start(bf16[1040,512]{1,0:T(8,128)(2,1)S(1)} %concatenate.7.refs_0_.refs_1_), channel_id=1, source_target_pairs={{0,32},{1,5},{4,36},{5,3},{2,34},{3,7},{6,38},{7,1},{32,64},{33,37... | collective-permute-start | bytes 3194888 | tf_op jit(solution)/shard_map/ppermute | solution.py:197
  21.5 17.0 %collective-permute-start.8 = (bf16[1040,512]{1,0:T(8,128)(2,1)S(1)}, bf16[1040,512]{1,0:T(8,128)(2,1)}, u32[]{:S(2)}, u32[]{:S(2)}) collective-permute-start(bf16[1040,512]{1,0:T(8,128)(2,1)S(1)} %concatenate.7.refs_0_.refs_1_), channel_id=1, source_target_pairs={{0,96},{1,7},{4,100},{5,1},{2,98},{3,5},{6,102},{7,3},{32,0},{33,3... | collective-permute-start | bytes 3194888 | tf_op jit(solution)/shard_map/ppermute | solution.py:197
  23.3 15.2 %collective-permute-start.5 = (bf16[512,512]{1,0:T(8,128)(2,1)}, bf16[512,512]{1,0:T(8,128)(2,1)S(1)}, u32[]{:S(2)}, u32[]{:S(2)}) collective-permute-start(bf16[512,512]{1,0:T(8,128)(2,1)} %copy-done.2), channel_id=1, source_target_pairs={{0,8},{8,16},{16,24},{24,0},{1,9},{9,17},{17,25},{25,1},{2,10},{10... | collective-permute-start | bytes 1572872 | tf_op jit(solution)/shard_map/ppermute | solution.py:209
  24.6 1.0 %copy-start = (bf16[512,512]{1,0:T(8,128)(2,1)S(1)}, bf16[512,512]{1,0:T(8,128)(2,1)}, u32[]{:S(2)}) copy-start(bf16[512,512]{1,0:T(8,128)(2,1)} %get-tuple-element.19.refs_2_.refs_5_.refs_3_) | copy-start | bytes 1572868
  25.6 1.0 %copy-start.3 = (bf16[512,512]{1,0:T(8,128)(2,1)S(1)}, bf16[512,512]{1,0:T(8,128)(2,1)}, u32[]{:S(2)}) copy-start(bf16[512,512]{1,0:T(8,128)(2,1)} %copy-done.2) | copy-start | bytes 1572868
  26.7 1.0 %copy-start.6 = (bf16[512,512]{1,0:T(8,128)(2,1)S(1)}, bf16[512,512]{1,0:T(8,128)(2,1)}, u32[]{:S(2)}) copy-start(bf16[512,512]{1,0:T(8,128)(2,1)} %copy-done.5) | copy-start | bytes 1572868
  27.7 12.5 %copy-start.4 = (bf16[512,512]{1,0:T(8,128)(2,1)S(1)}, bf16[512,512]{1,0:T(8,128)(2,1)}, u32[]{:S(2)}) copy-start(bf16[512,512]{1,0:T(8,128)(2,1)} %copy-done.2) | copy-start | bytes 1572868
  27.7 12.5 %copy-start.7 = (bf16[512,512]{1,0:T(8,128)(2,1)S(1)}, bf16[512,512]{1,0:T(8,128)(2,1)}, u32[]{:S(2)}) copy-start(bf16[512,512]{1,0:T(8,128)(2,1)} %copy-done.5) | copy-start | bytes 1572868
  38.6 10.5 %collective-permute-start.9 = (bf16[1040,512]{1,0:T(8,128)(2,1)S(1)}, bf16[1040,512]{1,0:T(8,128)(2,1)S(1)}, u32[]{:S(2)}, u32[]{:S(2)}) collective-permute-start(bf16[1040,512]{1,0:T(8,128)(2,1)S(1)} %collective-permute-done.7.refs_3_), channel_id=1, source_target_pairs={{0,1},{1,0},{2,3},{3,2},{4,5},{5,4},{6,7},{7,6},{8,9},{9,8},{10,11... | collective-permute-start | bytes 3194888 | tf_op jit(solution)/shard_map/ppermute | solution.py:205
  38.6 10.5 %collective-permute-start.10 = (bf16[1040,512]{1,0:T(8,128)(2,1)}, bf16[1040,512]{1,0:T(8,128)(2,1)S(1)}, u32[]{:S(2)}, u32[]{:S(2)}) collective-permute-start(bf16[1040,512]{1,0:T(8,128)(2,1)} %collective-permute-done.8.refs_4_), channel_id=1, source_target_pairs={{0,1},{1,0},{2,3},{3,2},{4,5},{5,4},{6,7},{7,6},{8,9},{9,8},{10,11... | collective-permute-start | bytes 3194888 | tf_op jit(solution)/shard_map/ppermute | solution.py:205
  39.1 17.2 %collective-permute-start.11 = (bf16[1040,512]{1,0:T(8,128)(2,1)S(1)}, bf16[1040,512]{1,0:T(8,128)(2,1)S(1)}, u32[]{:S(2)}, u32[]{:S(2)}) collective-permute-start(bf16[1040,512]{1,0:T(8,128)(2,1)S(1)} %collective-permute-done.7.refs_3_), channel_id=1, source_target_pairs={{0,32},{1,5},{4,36},{5,3},{2,34},{3,7},{6,38},{7,1},{32,64},{33,37... | collective-permute-start | bytes 3194888 | tf_op jit(solution)/shard_map/ppermute | solution.py:197
  49.0 7.6 %copy-start.1 = (bf16[512,512]{1,0:T(8,128)(2,1)S(1)}, bf16[512,512]{1,0:T(8,128)(2,1)}, u32[]{:S(2)}) copy-start(bf16[512,512]{1,0:T(8,128)(2,1)} %get-tuple-element.19.refs_2_.refs_5_.refs_3_) | copy-start | bytes 1572868
  56.3 4.7 %collective-permute-start.12 = (bf16[1040,512]{1,0:T(8,128)(2,1)S(1)}, bf16[1040,512]{1,0:T(8,128)(2,1)S(1)}, u32[]{:S(2)}, u32[]{:S(2)}) collective-permute-start(bf16[1040,512]{1,0:T(8,128)(2,1)S(1)} %collective-permute-done.11.refs_1_), channel_id=1, source_target_pairs={{0,1},{1,0},{2,3},{3,2},{4,5},{5,4},{6,7},{7,6},{8,9},{9,8},{10,11... | collective-permute-start | bytes 3194888 | tf_op jit(solution)/shard_map/ppermute | solution.py:205

commit v6 on v4

--- a/solution.py
+++ b/solution.py
@@ -33,7 +33,9 @@
 
 def unit_kernel(e_ref, c_ref, l_ref, a_ref, u_ref):
     u_ref[...] = unit_block(c_ref)
-    a_ref[:ROWS, :] = unit_block(e_ref)
+    rows = ROWS // 2
+    here = pl.ds(pl.multiple_of(pl.program_id(0) * rows, rows), rows)
+    a_ref[here, :] = unit_block(e_ref)
     label = jnp.concatenate([l_ref[...] // 256, l_ref[...] % 256], axis=1)
     label = jnp.broadcast_to(label.astype(jnp.float32), (PITCH - ROWS, 2 * ROWS))
     a_ref[ROWS:, :] = label.astype(jnp.bfloat16)
@@ -43,6 +45,16 @@
     shapes = [(PITCH, embeddings.shape[1]), centers.shape]
     return pl.pallas_call(
         unit_kernel,
+        grid=(2,),
+        in_specs=[
+            pl.BlockSpec((ROWS // 2, 512), lambda i: (i, 0)),
+            pl.BlockSpec((TILE // 2, 512), lambda i: (i, 0)),
+            pl.BlockSpec((1, ROWS), lambda i: (0, 0)),
+        ],
+        out_specs=[
+            pl.BlockSpec((PITCH, 512), lambda i: (0, 0)),
+            pl.BlockSpec((TILE // 2, 512), lambda i: (i, 0)),
+        ],
         out_shape=[jax.ShapeDtypeStruct(s, jnp.bfloat16) for s in shapes],
     )(embeddings, centers, labels.reshape(1, ROWS))
 

time: 81 us -> 80.9 us (level)
  no operation moved by 1% of the time
where the time goes in v6:
time: 80.9 us; the launch traced here: 79.5 us
  Pallas kernels  32.8 us (41%)
  starting transfers between devices  17 us (21%)
  blocking collectives  13.4 us (17%)
  waiting for transfers between devices  8.99 us (11%)
  local copies, waits for them, and re-layouts  6.24 us (8%)
    pallas_call x5, Pallas kernels, terms(): pl.pallas_call(functools.partial(terms_kernel, n_e, n_c, n_steps, at_owne...  30.7 us
    all_to_all x1, blocking collectives, body(): parts = lax.all_to_all(sums, DEVICES, 0, 0, tiled=True)  13.4 us
    ppermute x6, starting transfers between devices, cross(): return lax.ppermute(x, DEVICES, pairs)  10.9 us
    ppermute x6, waiting for transfers between devices, cross(): return lax.ppermute(x, DEVICES, pairs)  6.11 us
    ppermute x3, starting transfers between devices, up_z(): return lax.ppermute(x, 'z', [(i, (i + by) % 4) for i in range(4)])  5.29 us
    unnamed x26, local copies, waits for them, and re-layouts  4.05 us
    ppermute x3, waiting for transfers between devices, up_z(): return lax.ppermute(x, 'z', [(i, (i + by) % 4) for i in range(4)])  2.86 us
    pallas_call x1, Pallas kernels, normalized(): pl.pallas_call(unit_kernel, grid=(2,), in_specs=[pl.BlockSpec((ROWS // 2,...  2.12 us
  transfers between devices with their start and end apart: 13, of which 6 were waited for; matrix products, arithmetic and copies ran while one was open for 2% of the time, Pallas kernels for 33%

profile of v6, /device:TPU:0, one launch (start us, length us, event | category | flops | bytes accessed | tf_op | source)
XLA Modules:
  0.0 79.5 jit_solution(7547882613017455512)
XLA Ops:
  0.0 2.1 %shard_map.82 = (bf16[272,512]{1,0:T(8,128)(2,1)}, bf16[512,512]{1,0:T(8,128)(2,1)}) custom-call(bf16[256,512]{1,0:T(8,128)(2,1)} %e_ref.1, bf16[512,512]{1,0:T(8,128)(2,1)} %c_ref.1, s32[1,256]{1,0:T(1,128)} %bitcast.6), custom_call_target="tpu_custom_call" | custom-call | tf_op jit(solution)/shard_map/pallas_call | solution.py:46
  2.1 2.0 %collective-permute-start.1 = (bf16[512,512]{1,0:T(8,128)(2,1)}, bf16[512,512]{1,0:T(8,128)(2,1)S(1)}, u32[]{:S(2)}, u32[]{:S(2)}) collective-permute-start(bf16[512,512]{1,0:T(8,128)(2,1)} %get-tuple-element.20.refs_2_.refs_5_.refs_3_), channel_id=1, source_target_pairs={{0,8},{8,16},{16,24},{24,0},{1,9},{9,17},{17,25},{25,1},{2,10},{10... | collective-permute-start | bytes 1572872 | tf_op jit(solution)/shard_map/ppermute | solution.py:221
  4.1 2.1 %collective-permute-start.2 = (bf16[512,512]{1,0:T(8,128)(2,1)}, bf16[512,512]{1,0:T(8,128)(2,1)S(1)}, u32[]{:S(2)}, u32[]{:S(2)}) collective-permute-start(bf16[512,512]{1,0:T(8,128)(2,1)} %get-tuple-element.20.refs_2_.refs_5_.refs_3_), channel_id=1, source_target_pairs={{0,24},{8,0},{16,8},{24,16},{1,25},{9,1},{17,9},{25,17},{2,26},{10... | collective-permute-start | bytes 1572872 | tf_op jit(solution)/shard_map/ppermute | solution.py:221
  6.3 3.2 %collective-permute-start = (bf16[272,512]{1,0:T(8,128)(2,1)}, bf16[272,512]{1,0:T(8,128)(2,1)S(1)}, u32[]{:S(2)}, u32[]{:S(2)}) collective-permute-start(bf16[272,512]{1,0:T(8,128)(2,1)} %get-tuple-element.19), channel_id=1, source_target_pairs={{0,2},{1,65},{4,6},{5,69},{2,0},{3,67},{6,4},{7,71},{32,34},{33,97... | collective-permute-start | bytes 835592 | tf_op jit(solution)/shard_map/ppermute | solution.py:209
  9.5 0.7 collective-permute-start.3
  10.1 2.6 %collective-permute-start.4 = (bf16[272,512]{1,0:T(8,128)(2,1)}, bf16[272,512]{1,0:T(8,128)(2,1)S(1)}, u32[]{:S(2)}, u32[]{:S(2)}) collective-permute-start(bf16[272,512]{1,0:T(8,128)(2,1)} %get-tuple-element.19), channel_id=1, source_target_pairs={{0,6},{1,97},{4,0},{5,101},{2,4},{3,99},{6,2},{7,103},{32,38},{33,... | collective-permute-start | bytes 835592 | tf_op jit(solution)/shard_map/ppermute | solution.py:209
  12.7 1.0 %slice.30 = bf16[256,512]{1,0:T(8,128)(2,1)S(1)} slice(bf16[272,512]{1,0:T(8,128)(2,1)} %get-tuple-element.19), slice={[0:256], [0:512]} | slice | bytes 524288 | tf_op jit(solution)/shard_map/slice | solution.py:237
  13.7 0.7 slice.34
  14.4 0.1 collective-permute-done
  14.5 3.0 %collective-permute-done.3 = bf16[272,512]{1,0:T(8,128)(2,1)S(1)} collective-permute-done((bf16[272,512]{1,0:T(8,128)(2,1)}, bf16[272,512]{1,0:T(8,128)(2,1)S(1)}, u32[]{:S(2)}, u32[]{:S(2)}) %collective-permute-start.3) | collective-permute-done | bytes 278560 | tf_op jit(solution)/shard_map/ppermute | solution.py:209
  17.5 0.3 collective-permute-done.4
  17.9 0.5 collective-permute-done.1.refs_3_.refs_6_.refs_4_
  18.4 0.0 copy-start.2
  18.4 0.0 collective-permute-done.2.refs_4_.refs_7_.refs_5_
  18.4 0.0 copy-start.5
  18.5 0.7 copy-done.2
  19.2 0.2 copy-done.5
  19.4 0.0 copy-start.9
  19.4 0.0 copy-start.10
  19.4 0.0 copy-start.11
  19.4 0.0 copy-start.8
  19.4 0.0 copy-start.12
  19.4 0.4 concatenate.7.refs_0_.refs_1_
  19.8 0.1 collective-permute-start.5
  19.9 1.6 %collective-permute-start.6 = (bf16[1040,512]{1,0:T(8,128)(2,1)S(1)}, bf16[1040,512]{1,0:T(8,128)(2,1)S(1)}, u32[]{:S(2)}, u32[]{:S(2)}) collective-permute-start(bf16[1040,512]{1,0:T(8,128)(2,1)S(1)} %concatenate.7.refs_0_.refs_1_), channel_id=1, source_target_pairs={{0,32},{1,5},{4,36},{5,3},{2,34},{3,7},{6,38},{7,1},{32,64},{33,37... | collective-permute-start | bytes 3194888 | tf_op jit(solution)/shard_map/ppermute | solution.py:209
  21.5 1.7 %collective-permute-start.7 = (bf16[1040,512]{1,0:T(8,128)(2,1)S(1)}, bf16[1040,512]{1,0:T(8,128)(2,1)}, u32[]{:S(2)}, u32[]{:S(2)}) collective-permute-start(bf16[1040,512]{1,0:T(8,128)(2,1)S(1)} %concatenate.7.refs_0_.refs_1_), channel_id=1, source_target_pairs={{0,96},{1,7},{4,100},{5,1},{2,98},{3,5},{6,102},{7,3},{32,0},{33,3... | collective-permute-start | bytes 3194888 | tf_op jit(solution)/shard_map/ppermute | solution.py:209
  23.2 0.0 copy-done.9
  23.2 0.0 copy-done.10
  23.2 0.0 copy-done.11
  23.3 1.1 %collective-permute-start.8 = (bf16[512,512]{1,0:T(8,128)(2,1)}, bf16[512,512]{1,0:T(8,128)(2,1)S(1)}, u32[]{:S(2)}, u32[]{:S(2)}) collective-permute-start(bf16[512,512]{1,0:T(8,128)(2,1)} %copy-done.2), channel_id=1, source_target_pairs={{0,8},{8,16},{16,24},{24,0},{1,9},{9,17},{17,25},{25,1},{2,10},{10... | collective-permute-start | bytes 1572872 | tf_op jit(solution)/shard_map/ppermute | solution.py:221
  24.4 0.0 copy-done.8
  24.4 0.0 copy-done.12
  24.4 0.1 pad_add_fusion.info_ref
  24.5 0.0 collective-permute-done.5.refs_1_.refs_2_
  24.5 0.0 copy-start
  24.5 1.0 %copy-done = bf16[512,512]{1,0:T(8,128)(2,1)S(1)} copy-done((bf16[512,512]{1,0:T(8,128)(2,1)S(1)}, bf16[512,512]{1,0:T(8,128)(2,1)}, u32[]{:S(2)}) %copy-start) | copy-done | bytes 524312
  25.6 0.0 copy-start.3
  25.6 1.0 %copy-done.3 = bf16[512,512]{1,0:T(8,128)(2,1)S(1)} copy-done((bf16[512,512]{1,0:T(8,128)(2,1)S(1)}, bf16[512,512]{1,0:T(8,128)(2,1)}, u32[]{:S(2)}) %copy-start.3) | copy-done | bytes 524312
  26.6 0.0 copy-start.6
  26.6 1.0 %copy-done.6 = bf16[512,512]{1,0:T(8,128)(2,1)S(1)} copy-done((bf16[512,512]{1,0:T(8,128)(2,1)S(1)}, bf16[512,512]{1,0:T(8,128)(2,1)}, u32[]{:S(2)}) %copy-start.6) | copy-done | bytes 524312
  27.6 0.0 copy-start.4
  27.6 0.0 copy-start.7
  27.6 5.9 %shard_map.83.refs_0_ = f32[32,16,256]{2,1,0:T(8,128)S(1)} custom-call(s32[165]{0:T(256)S(1)} %pad_add_fusion.info_ref, bf16[1040,512]{1,0:T(8,128)(2,1)S(1)} %concatenate.7.refs_0_.refs_1_, bf16[1040,512]{1,0:T(8,128)(2,1)S(1)} %collective-permute-done.5.refs_1_.refs_2_, bf16[512,512]{1,0:T(8,128)(2,1)S(1)} %copy-done, bf16[512,512]{1,0:T(8,128)(2,1)S(1)} %copy-done.3, ...), custom_call_target="tpu_custom_call" | custom-call | flops 3221225472 | bytes 3670016 | tf_op jit(solution)/shard_map/pallas_call | solution.py:178
  33.5 2.7 %collective-permute-done.6.refs_3_ = bf16[1040,512]{1,0:T(8,128)(2,1)S(1)} collective-permute-done((bf16[1040,512]{1,0:T(8,128)(2,1)S(1)}, bf16[1040,512]{1,0:T(8,128)(2,1)S(1)}, u32[]{:S(2)}, u32[]{:S(2)}) %collective-permute-start.6) | collective-permute-done | bytes 1064992 | tf_op jit(solution)/shard_map/ppermute | solution.py:209
  36.2 2.3 %collective-permute-done.8.refs_8_.refs_6_.refs_5_ = bf16[512,512]{1,0:T(8,128)(2,1)S(1)} collective-permute-done((bf16[512,512]{1,0:T(8,128)(2,1)}, bf16[512,512]{1,0:T(8,128)(2,1)S(1)}, u32[]{:S(2)}, u32[]{:S(2)}) %collective-permute-start.8) | collective-permute-done | bytes 524320 | tf_op jit(solution)/shard_map/ppermute | solution.py:221
  38.5 0.0 collective-permute-done.7.refs_4_
  38.5 0.0 collective-permute-start.9
  38.5 0.5 collective-permute-start.10
  39.0 1.2 %collective-permute-start.11 = (bf16[1040,512]{1,0:T(8,128)(2,1)S(1)}, bf16[1040,512]{1,0:T(8,128)(2,1)S(1)}, u32[]{:S(2)}, u32[]{:S(2)}) collective-permute-start(bf16[1040,512]{1,0:T(8,128)(2,1)S(1)} %collective-permute-done.6.refs_3_), channel_id=1, source_target_pairs={{0,32},{1,5},{4,36},{5,3},{2,34},{3,7},{6,38},{7,1},{32,64},{33,37... | collective-permute-start | bytes 3194888 | tf_op jit(solution)/shard_map/ppermute | solution.py:209
  40.2 0.0 copy-done.4
  40.2 0.0 copy-done.7
  40.2 8.8 %shard_map.84.refs_0_ = f32[32,16,256]{2,1,0:T(8,128)S(1)} custom-call(s32[165]{0:T(256)S(1)} %pad_add_fusion.info_ref, f32[32,16,256]{2,1,0:T(8,128)S(1)} %shard_map.83.refs_0_, bf16[1040,512]{1,0:T(8,128)(2,1)S(1)} %concatenate.7.refs_0_.refs_1_, bf16[1040,512]{1,0:T(8,128)(2,1)S(1)} %collective-permute-done.5.refs_1_.refs_2_, ...), custom_call_target="tpu_custom_call", output_to_operand_aliasing={{}: (1, {})} | custom-call | flops 5368709120 | bytes 6291456 | tf_op jit(solution)/shard_map/pallas_call | solution.py:178
  49.0 0.0 copy-start.1
  49.0 0.0 collective-permute-done.9.refs_1_
  49.0 0.0 collective-permute-done.10.refs_2_
  49.0 7.3 %shard_map.85.refs_0_ = f32[32,16,256]{2,1,0:T(8,128)S(1)} custom-call(s32[165]{0:T(256)S(1)} %pad_add_fusion.info_ref, f32[32,16,256]{2,1,0:T(8,128)S(1)} %shard_map.84.refs_0_, bf16[1040,512]{1,0:T(8,128)(2,1)S(1)} %collective-permute-done.9.refs_1_, bf16[1040,512]{1,0:T(8,128)(2,1)S(1)} %collective-permute-done.10.refs_2_, ...), custom_call_target="tpu_custom_call", output_to_operand_aliasing={{}: (1, {})} | custom-call | flops 4294967296 | bytes 4194304 | tf_op jit(solution)/shard_map/pallas_call | solution.py:178
  56.2 0.0 collective-permute-done.11.refs_1_
  56.3 0.3 collective-permute-start.12
  56.5 0.0 copy-done.1
  56.5 4.4 %shard_map.86.refs_0_ = f32[32,16,256]{2,1,0:T(8,128)S(1)} custom-call(s32[165]{0:T(256)S(1)} %pad_add_fusion.info_ref, f32[32,16,256]{2,1,0:T(8,128)S(1)} %shard_map.85.refs_0_, bf16[1040,512]{1,0:T(8,128)(2,1)S(1)} %collective-permute-done.11.refs_1_, bf16[512,512]{1,0:T(8,128)(2,1)S(1)} %copy-done.1, ...), custom_call_target="tpu_custom_call", output_to_operand_aliasing={{}: (1, {})} | custom-call | flops 2147483648 | bytes 3145728 | tf_op jit(solution)/shard_map/pallas_call | solution.py:178
  60.9 0.0 collective-permute-done.12.refs_1_
  60.9 4.5 %shard_map.87 = (f32[32,16,256]{2,1,0:T(8,128)S(1)}, f32[32,2,256]{2,1,0:T(2,128)S(1)}) custom-call(s32[165]{0:T(256)S(1)} %pad_add_fusion.info_ref, f32[32,16,256]{2,1,0:T(8,128)S(1)} %shard_map.86.refs_0_, bf16[1040,512]{1,0:T(8,128)(2,1)S(1)} %collective-permute-done.12.refs_1_, bf16[512,512]{1,0:T(8,128)(2,1)S(1)} %copy-done.1, ...), custom_call_target="tpu_custom_call", output_to_operand_aliasing={{0}: (1, {})} | custom-call | flops 2147483648 | bytes 3145728 | tf_op jit(solution)/shard_map/pallas_call | solution.py:178
  65.4 13.4 %all_to_all.5 = f32[32,2,256]{2,1,0:T(2,128)S(1)} all-to-all(f32[32,2,256]{2,1,0:T(2,128)S(1)} %get-tuple-element.32), channel_id=1, replica_groups=mesh['x'=4,'z'=4,'yl'=2,'yh'=2,'c'=2] {'x','yl','yh','c'}, dimensions={0} | all-to-all | bytes 131072 | tf_op jit(solution)/shard_map/all_to_all | solution.py:280
  78.9 0.6 log_subtract_fusion
  (10 shorter events, 0.2 us)
Async XLA Ops:
  2.1 16.3 %collective-permute-start.1 = (bf16[512,512]{1,0:T(8,128)(2,1)}, bf16[512,512]{1,0:T(8,128)(2,1)S(1)}, u32[]{:S(2)}, u32[]{:S(2)}) collective-permute-start(bf16[512,512]{1,0:T(8,128)(2,1)} %get-tuple-element.20.refs_2_.refs_5_.refs_3_), channel_id=1, source_target_pairs={{0,8},{8,16},{16,24},{24,0},{1,9},{9,17},{17,25},{25,1},{2,10},{10... | collective-permute-start | bytes 1572872 | tf_op jit(solution)/shard_map/ppermute | solution.py:221
  4.1 14.3 %collective-permute-start.2 = (bf16[512,512]{1,0:T(8,128)(2,1)}, bf16[512,512]{1,0:T(8,128)(2,1)S(1)}, u32[]{:S(2)}, u32[]{:S(2)}) collective-permute-start(bf16[512,512]{1,0:T(8,128)(2,1)} %get-tuple-element.20.refs_2_.refs_5_.refs_3_), channel_id=1, source_target_pairs={{0,24},{8,0},{16,8},{24,16},{1,25},{9,1},{17,9},{25,17},{2,26},{10... | collective-permute-start | bytes 1572872 | tf_op jit(solution)/shard_map/ppermute | solution.py:221
  6.3 8.3 %collective-permute-start = (bf16[272,512]{1,0:T(8,128)(2,1)}, bf16[272,512]{1,0:T(8,128)(2,1)S(1)}, u32[]{:S(2)}, u32[]{:S(2)}) collective-permute-start(bf16[272,512]{1,0:T(8,128)(2,1)} %get-tuple-element.19), channel_id=1, source_target_pairs={{0,2},{1,65},{4,6},{5,69},{2,0},{3,67},{6,4},{7,71},{32,34},{33,97... | collective-permute-start | bytes 835592 | tf_op jit(solution)/shard_map/ppermute | solution.py:209
  9.5 8.1 %collective-permute-start.3 = (bf16[272,512]{1,0:T(8,128)(2,1)}, bf16[272,512]{1,0:T(8,128)(2,1)S(1)}, u32[]{:S(2)}, u32[]{:S(2)}) collective-permute-start(bf16[272,512]{1,0:T(8,128)(2,1)} %get-tuple-element.19), channel_id=1, source_target_pairs={{0,4},{1,33},{4,2},{5,37},{2,6},{3,35},{6,0},{7,39},{32,36},{33,65... | collective-permute-start | bytes 835592 | tf_op jit(solution)/shard_map/ppermute | solution.py:209
  10.1 7.7 %collective-permute-start.4 = (bf16[272,512]{1,0:T(8,128)(2,1)}, bf16[272,512]{1,0:T(8,128)(2,1)S(1)}, u32[]{:S(2)}, u32[]{:S(2)}) collective-permute-start(bf16[272,512]{1,0:T(8,128)(2,1)} %get-tuple-element.19), channel_id=1, source_target_pairs={{0,6},{1,97},{4,0},{5,101},{2,4},{3,99},{6,2},{7,103},{32,38},{33,... | collective-permute-start | bytes 835592 | tf_op jit(solution)/shard_map/ppermute | solution.py:209
  18.4 0.8 copy-start.2
  18.4 1.0 %copy-start.5 = (bf16[512,512]{1,0:T(8,128)(2,1)}, bf16[512,512]{1,0:T(8,128)(2,1)S(1)}, u32[]{:S(2)}) copy-start(bf16[512,512]{1,0:T(8,128)(2,1)S(1)} %collective-permute-done.2.refs_4_.refs_7_.refs_5_) | copy-start | bytes 1572868
  19.4 3.9 %copy-start.9 = (s32[32]{0:T(128)S(1)}, s32[32]{0:T(128)}, u32[]{:S(2)}) copy-start(s32[32]{0:T(128)} %constant.103.clone) | copy-start | bytes 388
  19.4 3.9 %copy-start.10 = (s32[32]{0:T(128)S(1)}, s32[32]{0:T(128)}, u32[]{:S(2)}) copy-start(s32[32]{0:T(128)} %constant.102.clone) | copy-start | bytes 388
  19.4 3.9 %copy-start.11 = (s32[32]{0:T(128)S(1)}, s32[32]{0:T(128)}, u32[]{:S(2)}) copy-start(s32[32]{0:T(128)} %constant.101.clone) | copy-start | bytes 388
  19.4 5.0 %copy-start.8 = (s32[4]{0:T(128)S(1)}, s32[4]{0:T(128)}, u32[]{:S(2)}) copy-start(s32[4]{0:T(128)} %constant.106) | copy-start | bytes 52
  19.4 5.0 %copy-start.12 = (s32[128]{0:T(128)S(1)}, s32[128]{0:T(128)}, u32[]{:S(2)}) copy-start(s32[128]{0:T(128)} %constant.105.clone) | copy-start | bytes 1540
  19.8 4.7 %collective-permute-start.5 = (bf16[1040,512]{1,0:T(8,128)(2,1)S(1)}, bf16[1040,512]{1,0:T(8,128)(2,1)S(1)}, u32[]{:S(2)}, u32[]{:S(2)}) collective-permute-start(bf16[1040,512]{1,0:T(8,128)(2,1)S(1)} %concatenate.7.refs_0_.refs_1_), channel_id=1, source_target_pairs={{0,1},{1,0},{2,3},{3,2},{4,5},{5,4},{6,7},{7,6},{8,9},{9,8},{10,11... | collective-permute-start | bytes 3194888 | tf_op jit(solution)/shard_map/ppermute | solution.py:217
  19.9 16.3 %collective-permute-start.6 = (bf16[1040,512]{1,0:T(8,128)(2,1)S(1)}, bf16[1040,512]{1,0:T(8,128)(2,1)S(1)}, u32[]{:S(2)}, u32[]{:S(2)}) collective-permute-start(bf16[1040,512]{1,0:T(8,128)(2,1)S(1)} %concatenate.7.refs_0_.refs_1_), channel_id=1, source_target_pairs={{0,32},{1,5},{4,36},{5,3},{2,34},{3,7},{6,38},{7,1},{32,64},{33,37... | collective-permute-start | bytes 3194888 | tf_op jit(solution)/shard_map/ppermute | solution.py:209
  21.5 17.0 %collective-permute-start.7 = (bf16[1040,512]{1,0:T(8,128)(2,1)S(1)}, bf16[1040,512]{1,0:T(8,128)(2,1)}, u32[]{:S(2)}, u32[]{:S(2)}) collective-permute-start(bf16[1040,512]{1,0:T(8,128)(2,1)S(1)} %concatenate.7.refs_0_.refs_1_), channel_id=1, source_target_pairs={{0,96},{1,7},{4,100},{5,1},{2,98},{3,5},{6,102},{7,3},{32,0},{33,3... | collective-permute-start | bytes 3194888 | tf_op jit(solution)/shard_map/ppermute | solution.py:209
  23.3 15.2 %collective-permute-start.8 = (bf16[512,512]{1,0:T(8,128)(2,1)}, bf16[512,512]{1,0:T(8,128)(2,1)S(1)}, u32[]{:S(2)}, u32[]{:S(2)}) collective-permute-start(bf16[512,512]{1,0:T(8,128)(2,1)} %copy-done.2), channel_id=1, source_target_pairs={{0,8},{8,16},{16,24},{24,0},{1,9},{9,17},{17,25},{25,1},{2,10},{10... | collective-permute-start | bytes 1572872 | tf_op jit(solution)/shard_map/ppermute | solution.py:221
  24.5 1.0 %copy-start = (bf16[512,512]{1,0:T(8,128)(2,1)S(1)}, bf16[512,512]{1,0:T(8,128)(2,1)}, u32[]{:S(2)}) copy-start(bf16[512,512]{1,0:T(8,128)(2,1)} %get-tuple-element.20.refs_2_.refs_5_.refs_3_) | copy-start | bytes 1572868
  25.6 1.0 %copy-start.3 = (bf16[512,512]{1,0:T(8,128)(2,1)S(1)}, bf16[512,512]{1,0:T(8,128)(2,1)}, u32[]{:S(2)}) copy-start(bf16[512,512]{1,0:T(8,128)(2,1)} %copy-done.2) | copy-start | bytes 1572868
  26.6 1.0 %copy-start.6 = (bf16[512,512]{1,0:T(8,128)(2,1)S(1)}, bf16[512,512]{1,0:T(8,128)(2,1)}, u32[]{:S(2)}) copy-start(bf16[512,512]{1,0:T(8,128)(2,1)} %copy-done.5) | copy-start | bytes 1572868
  27.6 12.5 %copy-start.4 = (bf16[512,512]{1,0:T(8,128)(2,1)S(1)}, bf16[512,512]{1,0:T(8,128)(2,1)}, u32[]{:S(2)}) copy-start(bf16[512,512]{1,0:T(8,128)(2,1)} %copy-done.2) | copy-start | bytes 1572868
  27.6 12.5 %copy-start.7 = (bf16[512,512]{1,0:T(8,128)(2,1)S(1)}, bf16[512,512]{1,0:T(8,128)(2,1)}, u32[]{:S(2)}) copy-start(bf16[512,512]{1,0:T(8,128)(2,1)} %copy-done.5) | copy-start | bytes 1572868
  38.5 10.5 %collective-permute-start.9 = (bf16[1040,512]{1,0:T(8,128)(2,1)S(1)}, bf16[1040,512]{1,0:T(8,128)(2,1)S(1)}, u32[]{:S(2)}, u32[]{:S(2)}) collective-permute-start(bf16[1040,512]{1,0:T(8,128)(2,1)S(1)} %collective-permute-done.6.refs_3_), channel_id=1, source_target_pairs={{0,1},{1,0},{2,3},{3,2},{4,5},{5,4},{6,7},{7,6},{8,9},{9,8},{10,11... | collective-permute-start | bytes 3194888 | tf_op jit(solution)/shard_map/ppermute | solution.py:217
  38.5 10.5 %collective-permute-start.10 = (bf16[1040,512]{1,0:T(8,128)(2,1)}, bf16[1040,512]{1,0:T(8,128)(2,1)S(1)}, u32[]{:S(2)}, u32[]{:S(2)}) collective-permute-start(bf16[1040,512]{1,0:T(8,128)(2,1)} %collective-permute-done.7.refs_4_), channel_id=1, source_target_pairs={{0,1},{1,0},{2,3},{3,2},{4,5},{5,4},{6,7},{7,6},{8,9},{9,8},{10,11... | collective-permute-start | bytes 3194888 | tf_op jit(solution)/shard_map/ppermute | solution.py:217
  39.0 17.2 %collective-permute-start.11 = (bf16[1040,512]{1,0:T(8,128)(2,1)S(1)}, bf16[1040,512]{1,0:T(8,128)(2,1)S(1)}, u32[]{:S(2)}, u32[]{:S(2)}) collective-permute-start(bf16[1040,512]{1,0:T(8,128)(2,1)S(1)} %collective-permute-done.6.refs_3_), channel_id=1, source_target_pairs={{0,32},{1,5},{4,36},{5,3},{2,34},{3,7},{6,38},{7,1},{32,64},{33,37... | collective-permute-start | bytes 3194888 | tf_op jit(solution)/shard_map/ppermute | solution.py:209
  49.0 7.6 %copy-start.1 = (bf16[512,512]{1,0:T(8,128)(2,1)S(1)}, bf16[512,512]{1,0:T(8,128)(2,1)}, u32[]{:S(2)}) copy-start(bf16[512,512]{1,0:T(8,128)(2,1)} %get-tuple-element.20.refs_2_.refs_5_.refs_3_) | copy-start | bytes 1572868
  56.3 4.7 %collective-permute-start.12 = (bf16[1040,512]{1,0:T(8,128)(2,1)S(1)}, bf16[1040,512]{1,0:T(8,128)(2,1)S(1)}, u32[]{:S(2)}, u32[]{:S(2)}) collective-permute-start(bf16[1040,512]{1,0:T(8,128)(2,1)S(1)} %collective-permute-done.11.refs_1_), channel_id=1, source_target_pairs={{0,1},{1,0},{2,3},{3,2},{4,5},{5,4},{6,7},{7,6},{8,9},{9,8},{10,11... | collective-permute-start | bytes 3194888 | tf_op jit(solution)/shard_map/ppermute | solution.py:217
